TPU v7x, 512 devices: a whole 4x4x16 slice. The times are simulated.
512 devices in a mesh: tm: 16 (over y, x), space: 32 (over z, core).
Axes of the slice: x: 4, y: 4, z: 16, core: 2. Of those that a mesh axis runs over, the one named last changes fastest.
Arguments:
- video: float32 [32, 64, 32, 256], P('tm', 'space'), may hold values from -6 to 6
- clip_ids: int32 [32], replicated, may hold values from 0 to 9, never falling along the last dimension, each value on 1 to 4 neighbouring positions
- norm1_gain: float32 [256], replicated, may hold values from 0.1 to 1.9
- conv1_weight: float32 [3, 3, 3, 256, 256], P(None, None, None, 'tm'), may hold values from -0.078125 to 0.078125
- norm2_gain: float32 [256], replicated, may hold values from 0.1 to 1.9
- conv2_weight: float32 [3, 3, 3, 256, 256], P(None, None, None, 'tm'), may hold values from -0.078125 to 0.078125
- norm3_gain: float32 [256], replicated, may hold values from 0.1 to 1.9
- qk_weight: float32 [2, 256, 256], replicated, may hold values from -40 to 40
- value_weight: float32 [256, 256], replicated, may hold values from -0.375 to 0.375
- proj_weight: float32 [256, 256], replicated, may hold values from -0.375 to 0.375
Outputs:
- encoded: float32 [32, 64, 32, 256], P('tm', 'space')
Inputs may be any that keep to these rules, and one draw needn't show every extreme that they name: clip_ids never falls; each clip has 1 to 4 consecutive frames, and one has exactly 4.
All inputs are finite; a program needn't handle non-finite values.
Results may differ from a plain program's by a relative error of at most 0.0003.
Values sent between devices are 32-bit elements; how exact they have to be, the bound alone decides.
No kernel may reach another device: no remote copies, remote signals or barrier semaphores. Data moves between devices by JAX's collectives and lax.ppermute only.
A program may use at most 64 MiB of HBM per device.

v0:
```python
import math

import jax
import jax.numpy as jnp
from jax import lax
from jax.sharding import PartitionSpec as P

highest = lax.Precision.HIGHEST
epsilon = 1e-06


def extended_2(block, sides, width):
    for axis, dim in sides:
        count = lax.axis_size(axis)
        forward = [(i, i + 1) for i in range(count - 1)]
        backward = [(target, source) for source, target in forward]
        low = lax.ppermute(
            lax.slice_in_dim(block, block.shape[dim] - width, None, axis=dim), axis, forward
        )
        high = lax.ppermute(lax.slice_in_dim(block, 0, width, axis=dim), axis, backward)
        block = jnp.concatenate([low, block, high], axis=dim)
    return block


def from_behind(block, axis, distance):
    devices = range(lax.axis_size(axis))
    route = [(i - distance, i) for i in devices if i - distance in devices]
    return lax.ppermute(block, axis, route)


def rms_scale(volume, gain_vec):
    return (
        volume * lax.rsqrt(jnp.mean(volume * volume, axis=-1, keepdims=True) + epsilon) * gain_vec
    )


def row_margin(volume):
    extended = extended_2(volume, (("space", 1),), 1)
    return jnp.pad(extended, ((0, 0), (0, 0), (1, 1), (0, 0)))


def patch_stack(extended, ext_ids, out_frames, band_rows, across):
    own_ids = ext_ids[2:]
    pieces = []
    for tap_t in range(3):
        same_clip = (ext_ids[tap_t : tap_t + out_frames] == own_ids).astype(jnp.float32)[
            :, None, None, None
        ]
        for tap_y in range(3):
            for tap_x in range(3):
                pieces.append(
                    extended[
                        tap_t : tap_t + out_frames,
                        tap_y : tap_y + band_rows,
                        tap_x : tap_x + across,
                    ]
                    * same_clip
                )
    return jnp.stack(pieces, axis=3)


def conv_apply(patches, weight):
    portion = lax.all_gather(weight, "tm", axis=3, tiled=True)
    taps_view = portion.reshape(27, portion.shape[3], portion.shape[4])
    return jnp.einsum(
        "fyxpc,pkc->fyxk", patches, taps_view, precision=highest, preferred_element_type=jnp.float32
    )


def conv_block(volume, ext_ids, weight):
    out_frames = volume.shape[0] - 2
    extended = row_margin(volume)
    patches = patch_stack(extended, ext_ids, out_frames, volume.shape[1], volume.shape[2])
    return conv_apply(patches, weight)


def with_cache(volume):
    earlier = from_behind(volume, "tm", 1)
    return jnp.concatenate([earlier, volume], axis=0)


def body(
    video,
    clip_ids,
    norm1_gain,
    conv1_weight,
    norm2_gain,
    conv2_weight,
    norm3_gain,
    qk_weight,
    value_weight,
    proj_weight,
):
    frames, band_rows, across, channels = video.shape
    padded_ids = jnp.concatenate([jnp.full((4,), -1, jnp.int32), clip_ids])
    id_window = lax.dynamic_slice_in_dim(padded_ids, lax.axis_index("tm") * frames, frames + 4)
    first = jax.nn.silu(rms_scale(video, norm1_gain))
    second = conv_block(with_cache(first), id_window[2:], conv1_weight)
    third = jax.nn.silu(rms_scale(second, norm2_gain))
    inner = conv_block(with_cache(third), id_window[2:], conv2_weight)
    blocked = video + inner
    tokens = band_rows * across
    normed = rms_scale(blocked, norm3_gain).reshape(frames, tokens, channels)
    queries = jnp.dot(normed, qk_weight[0], precision=highest)
    factor = 1.0 / math.sqrt(channels)
    keys_local = jnp.dot(normed, qk_weight[1], precision=highest)
    values_local = jnp.dot(normed, value_weight, precision=highest)
    running_max = jnp.full((frames, tokens), -jnp.inf, jnp.float32)
    denominator = jnp.zeros((frames, tokens), jnp.float32)
    weighted = jnp.zeros((frames, tokens, channels), jnp.float32)
    scores = (
        jnp.einsum(
            "fld,fnd->fln",
            queries,
            lax.all_gather(keys_local, "space", axis=1, tiled=True),
            precision=highest,
        )
        * factor
    )
    newest = jnp.max(scores, axis=-1)
    shrink = jnp.exp(running_max - newest)
    weights = jnp.exp(scores - newest[..., None])
    denominator = denominator * shrink + jnp.sum(weights, axis=-1)
    weighted = weighted * shrink[..., None] + jnp.einsum(
        "fln,fnd->fld",
        weights,
        lax.all_gather(values_local, "space", axis=1, tiled=True),
        precision=highest,
    )
    attended = weighted / denominator[..., None]
    projected = jnp.dot(attended, proj_weight, precision=highest)
    return blocked + projected.reshape(frames, band_rows, across, channels)


def solution(mesh):
    in_specs = (
        P("tm", "space", None, None),
        P(),
        P(),
        P(None, None, None, "tm", None),
        P(),
        P(None, None, None, "tm", None),
        P(),
        P(),
        P(),
        P(),
    )
    out_specs = P("tm", "space", None, None)
    return jax.shard_map(body, mesh=mesh, in_specs=in_specs, out_specs=out_specs, check_vma=False)
```

profile of v0, /device:TPU:1, one launch (start us, length us, event | category | flops | bytes accessed | tf_op | source)
XLA Modules:
  0.0 351.1 jit_solution(16185998796386279910)
XLA Ops:
  7.3 1.0 multiply_reduce_fusion.2
  8.3 1.0 divide_multiply_fusion.1
  9.4 4.0 %collective-permute-start = (f32[2,2,32,256]{3,2,1,0:T(8,128)S(1)}, f32[2,2,32,256]{3,2,1,0:T(8,128)S(1)}, u32[]{:S(2)}, u32[]{:S(2)}) collective-permute-start(f32[2,2,32,256]{3,2,1,0:T(8,128)S(1)} %divide_multiply_fusion.1), channel_id=1, source_target_pairs={{0,32},{32,64},{64,96},{96,128},{128,160},{160,192},{192,224},{224... | collective-permute-start | bytes 393224 | tf_op jit(solution)/shard_map/ppermute | solution.py:28
  13.4 0.7 pad_dynamic-slice_fusion
  14.1 1.1 collective-permute-done
  15.3 5.2 %collective-permute-start.1 = (f32[4,1,32,256]{3,2,1,0:T(8,128)S(1)}, f32[4,1,32,256]{3,2,1,0:T(8,128)S(1)}, u32[]{:S(2)}, u32[]{:S(2)}) collective-permute-start(f32[4,1,32,256]{3,2,1,0:T(8,128)S(1)} %get-tuple-element.11), channel_id=1, source_target_pairs={{0,1},{1,2},{2,3},{3,4},{4,5},{5,6},{6,7},{7,8},{8,9},{9,10},{10,1... | collective-permute-start | bytes 393224 | tf_op jit(solution)/shard_map/ppermute | solution.py:17
  20.5 2.8 collective-permute-start.2
  23.3 3.4 collective-permute-done.2
  26.8 0.7 fusion.105
  27.7 0.7 fusion.103
  29.1 0.7 fusion.99
  29.9 0.7 bitcast_dynamic-update-slice_fusion.1
  31.3 0.7 fusion.95
  33.5 0.8 fusion.89
  34.3 0.8 fusion.87
  35.1 0.7 fusion.85
  35.8 0.7 fusion.83
  36.6 0.7 fusion.81
  37.3 0.7 fusion.78
  38.0 0.7 fusion.76
  38.8 0.7 fusion.74
  39.5 0.8 fusion.72
  43.0 0.8 bitcast_dynamic-update-slice_fusion
  46.5 49.4 %all-gather.5.cloned.1.call-done = f32[3,3,3,256,256]{4,3,2,1,0:T(8,128)} async-done(((f32[3,3,3,16,256]{4,3,2,1,0:T(8,128)}), f32[3,3,3,256,256]{4,3,2,1,0:T(8,128)}) %all-gather.5.cloned.1.call-update) | async-done | bytes 7077904 | tf_op jit(solution)/shard_map/all_gather | solution.py:63
  95.9 11.3 %multiply_reduce_fusion.1 = (f32[2,2,32]{2,1,0:T(2,128)S(1)}, f32[2,2,32,256]{3,2,1,0:T(8,128)S(1)}) fusion(f32[2,2,32,27,256]{4,2,3,1,0:T(8,128)} %fusion.63, f32[27,256,256,1,1]{2,1,0,4,3:T(8,128)} %bitcast.308), kind=kOutput, calls=%fused_computation.188 | convolution fusion | flops 2717974528 | bytes 10748416 | tf_op jit(solution)/shard_map/fyxpc,pkc->fyxk/dot_general | solution.py:65
  107.4 3.1 collective-permute-start.3
  110.4 1.9 collective-permute-done.3
  112.4 4.8 %collective-permute-start.4 = (f32[4,1,32,256]{3,2,1,0:T(8,128)S(1)}, f32[4,1,32,256]{3,2,1,0:T(8,128)S(1)}, u32[]{:S(2)}, u32[]{:S(2)}) collective-permute-start(f32[4,1,32,256]{3,2,1,0:T(8,128)S(1)} %get-tuple-element.7), channel_id=1, source_target_pairs={{0,1},{1,2},{2,3},{3,4},{4,5},{5,6},{6,7},{7,8},{8,9},{9,10},{10,1... | collective-permute-start | bytes 393224 | tf_op jit(solution)/shard_map/ppermute | solution.py:17
  117.2 2.1 collective-permute-start.5
  119.3 4.6 %collective-permute-done.5 = f32[4,1,32,256]{3,2,1,0:T(8,128)S(1)} collective-permute-done((f32[4,1,32,256]{3,2,1,0:T(8,128)S(1)}, f32[4,1,32,256]{3,2,1,0:T(8,128)S(1)}, u32[]{:S(2)}, u32[]{:S(2)}) %collective-permute-start.5) | collective-permute-done | bytes 131104 | tf_op jit(solution)/shard_map/ppermute | solution.py:20
  124.1 0.7 fusion.62
  127.0 0.7 bitcast_dynamic-update-slice_fusion.3
  127.7 0.7 fusion.54
  128.5 0.7 fusion.52
  129.2 0.7 fusion.50
  130.0 0.7 fusion.48
  130.7 0.7 fusion.46
  135.1 0.7 fusion.33
  135.8 0.7 fusion.31
  139.9 0.8 bitcast_dynamic-update-slice_fusion.2
  143.4 35.6 %all-gather.7.cloned.1.call-done = f32[3,3,3,256,256]{4,3,2,1,0:T(8,128)} async-done(((f32[3,3,3,16,256]{4,3,2,1,0:T(8,128)}), f32[3,3,3,256,256]{4,3,2,1,0:T(8,128)}) %all-gather.7.cloned.1.call-update) | async-done | bytes 7077904 | tf_op jit(solution)/shard_map/all_gather | solution.py:63
  179.0 11.3 %fusion = f32[2,2,32,256,1]{3,2,0,1,4:T(8,128)S(1)} fusion(f32[27,256,256,1,1]{2,1,3,4,0:T(8,128)} %bitcast.307, f32[2,2,32,27,256]{4,2,1,0,3:T(8,128)} %fusion.20), kind=kOutput, calls=%fused_computation | convolution fusion | flops 2717908992 | bytes 10747904 | tf_op jit(solution)/shard_map/fyxpc,pkc->fyxk/dot_general | solution.py:65
  190.5 0.9 fusion.10
  191.7 0.9 fusion.8
  193.0 72.6 %all-gather.9.cloned.1.call-done = f32[2,2048,256]{2,1,0:T(8,128)} async-done(((f32[2,64,256]{2,1,0:T(8,128)}), f32[2,2048,256]{2,1,0:T(8,128)}) %all-gather.9.cloned.1.call-update) | async-done | bytes 4194320 | tf_op jit(solution)/shard_map/all_gather | solution.py:115
  265.6 6.3 %fusion.108 = (f32[2,64]{1,0:T(2,128)S(1)}, f32[2,64,2048]{2,1,0:T(8,128)S(1)}) fusion(f32[2,64,256]{2,1,0:T(8,128)S(1)} %fusion.12, f32[2,2048,256]{2,1,0:T(8,128)} %all-gather.9.cloned.1.call-done), kind=kOutput, calls=%fused_computation.200 | convolution fusion | flops 805830528 | bytes 5374464 | tf_op jit(solution)/shard_map/fld,fnd->fln/dot_general | solution.py:112
  272.3 66.3 %all-gather.11.cloned.1.call-done = f32[2,2048,256]{2,1,0:T(8,128)} async-done(((f32[2,64,256]{2,1,0:T(8,128)}), f32[2,2048,256]{2,1,0:T(8,128)}) %all-gather.11.cloned.1.call-update) | async-done | bytes 4194320 | tf_op jit(solution)/shard_map/all_gather | solution.py:127
  338.6 5.0 %fusion.2 = f32[2,64,256]{2,1,0:T(8,128)S(1)} fusion(f32[2,2048,256]{2,1,0:T(8,128)} %all-gather.11.cloned.1.call-done, f32[2,64,2048]{2,1,0:T(8,128)S(1)} %get-tuple-element.20, f32[2,64]{1,0:T(2,128)S(1)} %get-tuple-element.19, f32[2,64]{1,0:T(2,128)S(1)} %get-tuple-element.14, f32[2,64]{1,0:T(2,128)S(1)} %get-tuple-element.13), kind=kOutput, calls=%fused_computation.5 | convolution fusion | flops 805634048 | bytes 5375488 | tf_op jit(solution)/shard_map/fln,fnd->fld/dot_general | solution.py:124
  (71 shorter events, 23.6 us)
Async XLA Ops:
  6.5 185.2 %copy-start = (f32[256,256]{1,0:T(8,128)S(1)}, f32[256,256]{1,0:T(8,128)}, u32[]{:S(2)}) copy-start(f32[256,256]{1,0:T(8,128)} %param.18) | copy-start | bytes 786436
  6.5 89.4 %all-gather.5.cloned.1.call-start = ((), (), s32[]{:S(2)}) async-start(), calls=%async_computation | async-start | bytes 7520256 | tf_op jit(solution)/shard_map/all_gather | solution.py:63
  7.3 171.7 %all-gather.7.cloned.1.call-start = ((), (), s32[]{:S(2)}) async-start(), calls=%async_computation.1 | async-start | bytes 7520256 | tf_op jit(solution)/shard_map/all_gather | solution.py:63
  9.4 5.9 %collective-permute-start = (f32[2,2,32,256]{3,2,1,0:T(8,128)S(1)}, f32[2,2,32,256]{3,2,1,0:T(8,128)S(1)}, u32[]{:S(2)}, u32[]{:S(2)}) collective-permute-start(f32[2,2,32,256]{3,2,1,0:T(8,128)S(1)} %divide_multiply_fusion.1), channel_id=1, source_target_pairs={{0,32},{32,64},{64,96},{96,128},{128,160},{160,192},{192,224},{224... | collective-permute-start | bytes 393224 | tf_op jit(solution)/shard_map/ppermute | solution.py:28
  13.3 252.3 %all-gather.9.cloned.1.call-start = ((), (), s32[]{:S(2)}) async-start(), calls=%async_computation.2 | async-start | bytes 4325376 | tf_op jit(solution)/shard_map/all_gather | solution.py:115
  15.3 8.1 %collective-permute-start.1 = (f32[4,1,32,256]{3,2,1,0:T(8,128)S(1)}, f32[4,1,32,256]{3,2,1,0:T(8,128)S(1)}, u32[]{:S(2)}, u32[]{:S(2)}) collective-permute-start(f32[4,1,32,256]{3,2,1,0:T(8,128)S(1)} %get-tuple-element.11), channel_id=1, source_target_pairs={{0,1},{1,2},{2,3},{3,4},{4,5},{5,6},{6,7},{7,8},{8,9},{9,10},{10,1... | collective-permute-start | bytes 393224 | tf_op jit(solution)/shard_map/ppermute | solution.py:17
  20.5 6.3 %collective-permute-start.2 = (f32[4,1,32,256]{3,2,1,0:T(8,128)S(1)}, f32[4,1,32,256]{3,2,1,0:T(8,128)S(1)}, u32[]{:S(2)}, u32[]{:S(2)}) collective-permute-start(f32[4,1,32,256]{3,2,1,0:T(8,128)S(1)} %get-tuple-element.12), channel_id=1, source_target_pairs={{1,0},{2,1},{3,2},{4,3},{5,4},{6,5},{7,6},{8,7},{9,8},{10,9},{11,1... | collective-permute-start | bytes 393224 | tf_op jit(solution)/shard_map/ppermute | solution.py:20
  27.6 15.4 %copy-start.1 = (f32[2,2,32,256]{3,2,1,0:T(8,128)S(1)}, f32[2,2,32,256]{3,2,1,0:T(8,128)}, u32[]{:S(2)}) copy-start(f32[2,2,32,256]{3,2,1,0:T(8,128)} %param.10) | copy-start | bytes 393220
  27.6 15.4 %copy-start.4 = (f32[256]{0:T(256)S(1)}, f32[256]{0:T(256)}, u32[]{:S(2)}) copy-start(f32[256]{0:T(256)} %param.12) | copy-start | bytes 3076
  95.9 11.3 %copy-start.5 = (f32[256]{0:T(256)S(1)}, f32[256]{0:T(256)}, u32[]{:S(2)}) copy-start(f32[256]{0:T(256)} %param.14) | copy-start | bytes 3076
  107.4 5.0 %collective-permute-start.3 = (f32[2,2,32,256]{3,2,1,0:T(8,128)S(1)}, f32[2,2,32,256]{3,2,1,0:T(8,128)S(1)}, u32[]{:S(2)}, u32[]{:S(2)}) collective-permute-start(f32[2,2,32,256]{3,2,1,0:T(8,128)S(1)} %divide_multiply_fusion), channel_id=1, source_target_pairs={{0,32},{32,64},{64,96},{96,128},{128,160},{160,192},{192,224},{224... | collective-permute-start | bytes 393224 | tf_op jit(solution)/shard_map/ppermute | solution.py:28
  112.4 6.9 %collective-permute-start.4 = (f32[4,1,32,256]{3,2,1,0:T(8,128)S(1)}, f32[4,1,32,256]{3,2,1,0:T(8,128)S(1)}, u32[]{:S(2)}, u32[]{:S(2)}) collective-permute-start(f32[4,1,32,256]{3,2,1,0:T(8,128)S(1)} %get-tuple-element.7), channel_id=1, source_target_pairs={{0,1},{1,2},{2,3},{3,4},{4,5},{5,6},{6,7},{7,8},{8,9},{9,10},{10,1... | collective-permute-start | bytes 393224 | tf_op jit(solution)/shard_map/ppermute | solution.py:17
  117.2 6.7 %collective-permute-start.5 = (f32[4,1,32,256]{3,2,1,0:T(8,128)S(1)}, f32[4,1,32,256]{3,2,1,0:T(8,128)S(1)}, u32[]{:S(2)}, u32[]{:S(2)}) collective-permute-start(f32[4,1,32,256]{3,2,1,0:T(8,128)S(1)} %get-tuple-element.8), channel_id=1, source_target_pairs={{1,0},{2,1},{3,2},{4,3},{5,4},{6,5},{7,6},{8,7},{9,8},{10,9},{11,1... | collective-permute-start | bytes 393224 | tf_op jit(solution)/shard_map/ppermute | solution.py:20
  179.0 11.4 %copy-start.6 = (f32[256]{0:T(256)S(1)}, f32[256]{0:T(256)}, u32[]{:S(2)}) copy-start(f32[256]{0:T(256)} %param.16) | copy-start | bytes 3076
  179.0 11.5 %copy-start.2 = (f32[2,256,256]{2,1,0:T(8,128)S(1)}, f32[2,256,256]{2,1,0:T(8,128)}, u32[]{:S(2)}) copy-start(f32[2,256,256]{2,1,0:T(8,128)} %param.17) | copy-start | bytes 1572868
  191.5 147.1 %all-gather.11.cloned.1.call-start = ((), (), s32[]{:S(2)}) async-start(), calls=%async_computation.3 | async-start | bytes 4325376 | tf_op jit(solution)/shard_map/all_gather | solution.py:127
  271.9 71.6 %copy-start.3 = (f32[256,256]{1,0:T(8,128)S(1)}, f32[256,256]{1,0:T(8,128)}, u32[]{:S(2)}) copy-start(f32[256,256]{1,0:T(8,128)} %param.19) | copy-start | bytes 786436
Sparse Core Ops, SparseCore 0:
  10.4 85.4 all-gather.4
  98.9 80.0 all-gather.6
  191.6 74.0 all-gather.8
  267.6 70.9 all-gather.10
where the time goes:
time: 351 us
  waiting for transfers between devices  236 us (67%)
  matrix products  36.3 us (10%)
  other arithmetic  31.9 us (9%)
  starting transfers between devices  22.3 us (6%)
  between operations  13.4 us (4%)
  local copies, waits for them, and re-layouts  11.5 us (3%)
    all_gather x2, waiting for transfers between devices, conv_apply(): portion = lax.all_gather(weight, 'tm', axis=3, tiled=True)  85.1 us
    all_gather x1, waiting for transfers between devices, body(): lax.all_gather(keys_local, 'space', axis=1, tiled=True)  72.6 us
    all_gather x1, waiting for transfers between devices, body(): lax.all_gather(values_local, 'space', axis=1, tiled=True)  66.3 us
    unnamed x38, other arithmetic  28.1 us
    dot_general x2, matrix products, conv_apply(): jnp.einsum('fyxpc,pkc->fyxk', patches, taps_view, precision=highest, pref...  22.6 us
    ppermute x2, starting transfers between devices, extended_2(): lax.ppermute(lax.slice_in_dim(block, block.shape[dim] - width, None, axis...  10 us
    unnamed x28, local copies, waits for them, and re-layouts  9.38 us
    ppermute x2, waiting for transfers between devices, extended_2(): lax.ppermute(lax.slice_in_dim(block, 0, width, axis=dim), axis, backward)  7.96 us
  transfers between devices with their start and end apart: 10, of which 8 were waited for; matrix products, arithmetic and copies ran while one was open for 17% of the time, Pallas kernels for 0%

commit v1 on v0

v1 whole, which is shorter than its diff:
```python
import math

import jax
import jax.numpy as jnp
from jax import lax
from jax.experimental import pallas as pl
from jax.experimental.pallas import tpu as pltpu
from jax.sharding import Mesh
from jax.sharding import PartitionSpec as P

highest = lax.Precision.HIGHEST
epsilon = 1e-06
f32 = jnp.float32
bf16 = jnp.bfloat16

Y, X, K, L, CORES = 4, 4, 8, 2, 2
SPACE = K * L * CORES
OFFSETS = ((0, 8), (2, -2), (4, -4), (6, -6))

VMEM_LIMIT = 48 * 1024 * 1024


def call(kernel, out_shape, scratch, *operands, smem=0):
    return pl.pallas_call(
        kernel,
        out_shape=out_shape,
        in_specs=[pl.BlockSpec(memory_space=pltpu.SMEM)] * smem
        + [pl.BlockSpec(memory_space=pltpu.VMEM)] * (len(operands) - smem),
        out_specs=jax.tree.map(lambda _: pl.BlockSpec(memory_space=pltpu.VMEM), out_shape),
        scratch_shapes=scratch,
        compiler_params=pltpu.CompilerParams(vmem_limit_bytes=VMEM_LIMIT),
    )(*operands)


def shape(*dims):
    return jax.ShapeDtypeStruct(dims, f32)


def column(gain_row):
    return jnp.broadcast_to(gain_row, (128, gain_row.shape[1])).T


def split(value):
    high = value.astype(bf16)
    return high, (value - high.astype(f32)).astype(bf16)


def dot3(a_high, a_low, b_high, b_low, dims=((1,), (0,))):
    def one(a, b):
        return lax.dot_general(a, b, (dims, ((), ())), preferred_element_type=f32)

    return one(a_high, b_low) + one(a_low, b_high) + one(a_high, b_high)


def norm_silu(value, gain):
    scale = lax.rsqrt(jnp.mean(value * value, axis=0, keepdims=True) + epsilon)
    value = value * scale * gain
    return value / (1.0 + jnp.exp(-value))


def lanes():
    lane = lax.broadcasted_iota(jnp.int32, (16, 128), 1)
    return lane, lane % 32, (lane // 32) % 2


def taps(product):
    _, across, row = lanes()
    left, right, first_row = across >= 1, across <= 30, row == 0
    result = []
    for a in range(3):
        rows = []
        for b in range(3):
            base = (a * 9 + b * 3) * 16
            rows.append(
                product[base + 16 : base + 32]
                + jnp.where(left, pltpu.roll(product[base : base + 16], 1, 1), 0.0)
                + jnp.where(right, pltpu.roll(product[base + 32 : base + 48], 127, 1), 0.0)
            )
        stay = jnp.where(first_row, rows[0], rows[2])
        own = rows[1] + jnp.where(first_row, pltpu.roll(stay, 96, 1), pltpu.roll(stay, 32, 1))
        leave = jnp.where(first_row, rows[2], rows[0])
        result.append(jnp.concatenate([own, leave], axis=0))
    return result


def in_time(now, before, mask_1, mask_2):
    lane = lax.broadcasted_iota(jnp.int32, (32, 128), 1)
    pair = jnp.where(lane < 64, now[1], before[1])
    return now[2] + mask_1 * pltpu.roll(pair, 64, 1) + mask_2 * before[0]


def spread_kernel(video_ref, out_ref):
    flipped = video_ref[...].T
    for i in range(Y * X):
        out_ref[i] = flipped


def conv1_kernel(
    place_ref, video_ref, weight_ref, gain_ref, mask_ref, own_ref, up_ref, down_ref, kept_ref
):
    _, _, row = lanes()
    first_row = row == 0
    gain = column(gain_ref[...])
    w_high, w_low = split(weight_ref[...])
    kept_ref[...] = video_ref[pl.ds(4 * place_ref[0], 4), :, place_ref[1]]

    def step(p, before):
        pieces = []
        for half in range(2):
            tile = video_ref[2 * p + half].reshape(256, 128)
            pieces.append(split(norm_silu(tile, gain)))
        high = jnp.concatenate([pieces[0][0], pieces[1][0]], axis=1)
        low = jnp.concatenate([pieces[0][1], pieces[1][1]], axis=1)
        product = dot3(w_high, w_low, high, low)
        outside = []
        for half in range(2):
            j = 2 * p + half
            now = taps(product[:, 128 * half : 128 * half + 128])
            done = in_time(now, before, mask_ref[0, pl.ds(j, 1)], mask_ref[1, pl.ds(j, 1)])
            own_ref[j] = done[:16]
            outside.append(done[16:])
            before = now
        up_ref[p] = jnp.where(first_row, outside[0], pltpu.roll(outside[1], 32, 1))
        down_ref[p] = jnp.where(first_row, pltpu.roll(outside[0], 96, 1), outside[1])
        return before

    zero = jnp.zeros((32, 128), f32)
    lax.fori_loop(0, 8, step, [zero, zero, zero])


def join1_kernel(own_ref, from_above_ref, from_below_ref, out_ref):
    _, _, row = lanes()
    first_row = row == 0
    out_ref[0:4, 0] = jnp.zeros((4, 16, 128), f32)
    for p in range(8):
        above, below = from_above_ref[p], from_below_ref[p]
        added = (
            jnp.where(first_row, above, pltpu.roll(below, 32, 1)),
            jnp.where(first_row, pltpu.roll(above, 96, 1), below),
        )
        for half in range(2):
            j = 2 * p + half
            tile = own_ref[j] + added[half]
            y, q = j // 4, j % 4
            for x in range(X):
                out_ref[4 * y + x, q + 1] = tile
                if q == 3 and y < 3:
                    out_ref[4 * (y + 1) + x, 0] = tile


def conv2_kernel(
    place_ref, second_ref, weight_ref, gain_ref, mask_ref, kept_ref, out_ref, high_ref, low_ref
):
    lane, _, _ = lanes()
    low_half = lane < 64
    gain = column(gain_ref[...])
    for q in range(5):
        tile = second_ref[:, q].reshape(256, 128)
        high, low = split(norm_silu(tile, gain))
        high_ref[:, 128 * q : 128 * q + 128] = high
        low_ref[:, 128 * q : 128 * q + 128] = low
    first = 4 * place_ref[0]

    def step(g, _):
        w_high, w_low = split(weight_ref[g])
        product = dot3(w_high, w_low, high_ref[...], low_ref[...])
        before = taps(product[:, :128])
        for q in range(4):
            now = taps(product[:, 128 * (q + 1) : 128 * (q + 2)])
            done = in_time(
                now, before, mask_ref[0, pl.ds(first + q, 1)], mask_ref[1, pl.ds(first + q, 1)]
            )
            own = done[:16] + kept_ref[q, g]
            leave = done[16:]
            out_ref[q, g] = jnp.where(low_half, own, pltpu.roll(leave, 64, 1))
            out_ref[q + 4, g] = jnp.where(low_half, pltpu.roll(own, 64, 1), leave)
            before = now
        return 0

    lax.fori_loop(0, 4, step, 0)


def join2_kernel(parts_ref, out_ref):
    lane, _, _ = lanes()
    first_row, low_half = lane < 32, lane < 64
    zero = jnp.zeros((16, 128), f32)

    def band(s):
        above = parts_ref[s - 1] if s > 0 else zero
        below = parts_ref[s + 1] if s < SPACE - 1 else zero
        return parts_ref[s] + jnp.where(
            first_row, pltpu.roll(above, 32, 1), pltpu.roll(below, 96, 1)
        )

    for p in range(16):
        tile = jnp.where(low_half, band(2 * p), pltpu.roll(band(2 * p + 1), 64, 1))
        for i in range(X * L):
            out_ref[i, p] = tile


def attend_kernel(
    place_ref, mine_ref, other_ref, gain_ref, qk_ref, value_ref, proj_ref, out_ref,
    blocked_ref, normed_ref, high_ref, low_ref,
):
    gain = column(gain_ref[...])
    even = place_ref[2] == 0
    for p in range(16):
        mine, other = mine_ref[:, p], other_ref[:, p]
        on_0 = jnp.where(even, mine, other)
        on_1 = jnp.where(even, other, mine)
        blocks = []
        for l in range(L):
            for part in (on_0, on_1):
                blocks += [part[2 * x + l] for x in range(X)]
        tile = jnp.concatenate(blocks, axis=0)
        blocked_ref[p] = tile
        normed = tile * lax.rsqrt(jnp.mean(tile * tile, axis=0, keepdims=True) + epsilon) * gain
        normed_ref[:, 128 * p : 128 * p + 128] = normed
        high, low = split(normed)
        high_ref[:, 128 * p : 128 * p + 128] = high
        low_ref[:, 128 * p : 128 * p + 128] = low
    at = place_ref[3]
    rows = blocked_ref[at].T
    normed_rows = rows * lax.rsqrt(jnp.mean(rows * rows, axis=1, keepdims=True) + epsilon) * gain_ref[...]
    queries = jnp.dot(normed_rows, qk_ref[0], precision=highest, preferred_element_type=f32)
    queries = lax.dot_general(
        queries, qk_ref[1], (((1,), (1,)), ((), ())), precision=highest, preferred_element_type=f32
    ) * (1.0 / math.sqrt(256))
    scores = jnp.dot(queries, normed_ref[...], precision=highest, preferred_element_type=f32)
    weights = jnp.exp(scores - jnp.max(scores, axis=1, keepdims=True))
    total = jnp.sum(weights, axis=1, keepdims=True)
    e_high, e_low = split(weights)
    attended = dot3(e_high, e_low, high_ref[...], low_ref[...], ((1,), (1,))) / total
    attended = jnp.dot(attended, value_ref[...], precision=highest, preferred_element_type=f32)
    attended = jnp.dot(attended, proj_ref[...], precision=highest, preferred_element_type=f32)
    result = rows + attended
    swapped = place_ref[4]
    out_ref[swapped] = result[:64]
    out_ref[1 - swapped] = result[64:]


def delivery():
    routes = ([], [])
    for x in range(X):
        for k in range(K):
            for l in range(L):
                for c in range(CORES):
                    source = ((x * K + k) * L + l) * CORES + c
                    chip = (2 * k + l + OFFSETS[x][c]) % (K * L)
                    f = k // 4
                    for route, core in zip(routes, (f, 1 - f)):
                        route.append((source, ((k % 4) * K * L + chip) * CORES + core))
    return routes


def body(
    video,
    clip_ids,
    norm1_gain,
    conv1_weight,
    norm2_gain,
    conv2_weight,
    norm3_gain,
    qk_weight,
    value_weight,
    proj_weight,
):
    space = ("k", "l", "c")
    y, x, k, l, c = (lax.axis_index(n) for n in ("y", "x", "k", "l", "c"))
    offset = jnp.where(c == 0, jnp.where(x == 0, 0, 2 * x), jnp.where(x == 0, 8, -2 * x))
    place = jnp.stack([y, x, c, (2 * k + l + offset) % (K * L), k // 4]).astype(jnp.int32)

    earlier = jnp.concatenate([jnp.full((2,), -1, jnp.int32), clip_ids])
    same = jnp.stack([earlier[1:-1] == clip_ids, earlier[:-2] == clip_ids]).astype(f32)
    masks = jnp.repeat(same, 64, axis=1).reshape(2, 16, 128)

    weight_2 = lax.all_gather(conv2_weight.reshape(432, 256), "y", axis=0)

    spread = call(spread_kernel, shape(Y * X, 256, 128), [], video.reshape(128, 256))
    everywhere = lax.all_to_all(spread, ("y", "x"), 0, 0)
    own, up, down, kept = call(
        conv1_kernel,
        [shape(16, 16, 128), shape(8, 16, 128), shape(8, 16, 128), shape(4, Y, 16, 128)],
        [],
        place,
        everywhere.reshape(16, Y, X, 16, 128),
        conv1_weight.reshape(432, 256),
        norm1_gain.reshape(1, 256),
        masks,
        smem=1,
    )
    onward = [(i, i + 1) for i in range(SPACE - 1)]
    from_above = lax.ppermute(down, space, onward)
    from_below = lax.ppermute(up, space, [(j, i) for i, j in onward])
    second = call(join1_kernel, shape(Y * X, 5, 16, 128), [], own, from_above, from_below)
    second = lax.all_to_all(second, ("y", "x"), 0, 0)
    parts = call(
        conv2_kernel,
        shape(K, 4, 16, 128),
        [pltpu.VMEM((256, 640), bf16)] * 2,
        place,
        second,
        weight_2,
        norm2_gain.reshape(1, 256),
        masks,
        kept,
        smem=1,
    )
    parts = lax.all_to_all(parts.reshape(SPACE, 16, 128), space, 0, 0)
    frame = call(join2_kernel, shape(X * L, 16, 16, 128), [], parts)
    mine = lax.all_to_all(frame, ("x", "l"), 0, 0)
    other = lax.ppermute(mine, "c", [(0, 1), (1, 0)])
    encoded = call(
        attend_kernel,
        shape(2, 64, 256),
        [
            pltpu.VMEM((16, 256, 128), f32),
            pltpu.VMEM((256, 2048), f32),
            pltpu.VMEM((256, 2048), bf16),
            pltpu.VMEM((256, 2048), bf16),
        ],
        place,
        mine,
        other,
        norm3_gain.reshape(1, 256),
        qk_weight,
        value_weight,
        proj_weight,
        smem=1,
    )
    route_0, route_1 = delivery()
    same_core = lax.ppermute(encoded[0], ("x", "k", "l", "c"), route_0)
    other_core = lax.ppermute(encoded[1], ("x", "k", "l", "c"), route_1)
    first_frame = jnp.where(c == 0, same_core, other_core)
    second_frame = jnp.where(c == 0, other_core, same_core)
    return jnp.stack([first_frame, second_frame]).reshape(video.shape)


def solution(mesh):
    grid = Mesh(mesh.devices.reshape(Y, X, K, L, CORES), ("y", "x", "k", "l", "c"))
    tm, space = ("y", "x"), ("k", "l", "c")
    in_specs = (
        P(tm, space, None, None),
        P(),
        P(),
        P(None, None, None, tm, None),
        P(),
        P(None, None, None, tm, None),
        P(),
        P(),
        P(),
        P(),
    )
    return jax.shard_map(
        body, mesh=grid, in_specs=in_specs, out_specs=P(tm, space, None, None), check_vma=False
    )
```

time: 351 us -> 181 us (0.52)
  the two profiles are of different devices: /device:TPU:1 before, /device:TPU:34 now
where the time goes in v1:
time: 181 us
  blocking collectives  76 us (42%)
  waiting for transfers between devices  46.5 us (26%)
  starting transfers between devices  22.6 us (12%)
  Pallas kernels  17.1 us (9%)
  between operations  13.6 us (8%)
  local copies, waits for them, and re-layouts  3.99 us (2%)
    all_to_all x1, blocking collectives, body(): parts = lax.all_to_all(parts.reshape(SPACE, 16, 128), space, 0, 0)  37.1 us
    all_to_all x1, waiting for transfers between devices, body(): everywhere = lax.all_to_all(spread, ('y', 'x'), 0, 0)  26.9 us
    all_to_all x1, blocking collectives, body(): second = lax.all_to_all(second, ('y', 'x'), 0, 0)  20 us
    all_to_all x1, blocking collectives, body(): mine = lax.all_to_all(frame, ('x', 'l'), 0, 0)  18.9 us
    pallas_call x6, Pallas kernels, call(): pl.pallas_call(kernel, out_shape=out_shape, in_specs=[pl.BlockSpec(memory...  17.1 us
    ppermute x1, waiting for transfers between devices, body(): other_core = lax.ppermute(encoded[1], ('x', 'k', 'l', 'c'), route_1)  14.4 us
    all_to_all x1, starting transfers between devices, body(): everywhere = lax.all_to_all(spread, ('y', 'x'), 0, 0)  7.61 us
    ppermute x1, starting transfers between devices, body(): other_core = lax.ppermute(encoded[1], ('x', 'k', 'l', 'c'), route_1)  4.18 us
  transfers between devices with their start and end apart: 7, of which 4 were waited for; matrix products, arithmetic and copies ran while one was open for 0% of the time, Pallas kernels for 4%

profile of v1, /device:TPU:34, one launch (start us, length us, event | category | flops | bytes accessed | tf_op | source)
XLA Modules:
  0.0 180.6 jit_solution(8090155634337914211)
XLA Ops:
  6.5 0.0 all-gather.2.cloned.1.call-start
  6.5 0.7 all-gather.2.cloned.1.call-update
  7.3 0.0 copy-start.6
  7.3 0.9 copy-done.6
  8.2 0.3 shard_map.100
  8.5 0.0 copy-start
  8.5 1.3 copy-done
  9.8 0.0 copy-start.10
  9.8 0.0 copy-start.3
  9.8 0.0 copy-start.8
  9.8 7.6 %all-to-all-start = ((f32[16,256,128]{2,1,0:T(8,128)}), f32[16,256,128]{2,1,0:T(8,128)S(1)}, u32[]{:S(2)}, u32[]{:S(2)}) async-start(f32[16,256,128]{2,1,0:T(8,128)} %copy-done), calls=%async_computation | async-start | bytes 4194304 | tf_op jit(solution)/shard_map/all_to_all | solution.py:280
  17.4 0.0 copy-done.10
  17.4 0.1 compare_bitcast_fusion.1
  17.5 0.1 broadcast_in_dim.3
  17.6 0.1 reshape_reshape.3.mask_ref
  17.7 0.1 stack.41.place_ref
  17.8 26.9 %all-to-all-done = f32[16,256,128]{2,1,0:T(8,128)S(1)} async-done(((f32[16,256,128]{2,1,0:T(8,128)}), f32[16,256,128]{2,1,0:T(8,128)S(1)}, u32[]{:S(2)}, u32[]{:S(2)}) %all-to-all-start) | async-done | bytes 2097184 | tf_op jit(solution)/shard_map/all_to_all | solution.py:280
  44.6 0.0 copy-done.3
  44.6 0.0 copy-done.8
  44.6 6.0 %shard_map.101 = (f32[16,16,128]{2,1,0:T(8,128)S(1)}, f32[8,16,128]{2,1,0:T(8,128)S(1)}, f32[8,16,128]{2,1,0:T(8,128)S(1)}, f32[4,4,16,128]{3,2,1,0:T(8,128)S(1)}) custom-call(s32[5]{0:T(128)S(1)} %stack.41.place_ref, f32[16,4,4,16,128]{4,3,2,1,0:T(8,128)S(1)} %bitcast.23, f32[432,256]{1,0:T(8,128)S(1)} %bitcast.25, f32[1,256]{1,0:T(1,128)S(1)} %bitcast.28, ...), custom_call_target="tpu_custom_call" | custom-call | tf_op jit(solution)/shard_map/pallas_call | solution.py:24
  50.6 1.9 %collective-permute-start = (f32[8,16,128]{2,1,0:T(8,128)S(1)}, f32[8,16,128]{2,1,0:T(8,128)S(1)}, u32[]{:S(2)}, u32[]{:S(2)}) collective-permute-start(f32[8,16,128]{2,1,0:T(8,128)S(1)} %get-tuple-element.10), channel_id=1, source_target_pairs={{0,1},{1,2},{2,3},{3,4},{4,5},{5,6},{6,7},{7,8},{8,9},{9,10},{10,1... | collective-permute-start | bytes 196616 | tf_op jit(solution)/shard_map/ppermute | solution.py:293
  52.5 3.6 %collective-permute-start.1 = (f32[8,16,128]{2,1,0:T(8,128)S(1)}, f32[8,16,128]{2,1,0:T(8,128)S(1)}, u32[]{:S(2)}, u32[]{:S(2)}) collective-permute-start(f32[8,16,128]{2,1,0:T(8,128)S(1)} %get-tuple-element.11), channel_id=1, source_target_pairs={{1,0},{2,1},{3,2},{4,3},{5,4},{6,5},{7,6},{8,7},{9,8},{10,9},{11,1... | collective-permute-start | bytes 196616 | tf_op jit(solution)/shard_map/ppermute | solution.py:294
  56.2 0.0 collective-permute-done.from_above_ref
  56.2 1.9 %collective-permute-done.1.from_below_ref = f32[8,16,128]{2,1,0:T(8,128)S(1)} collective-permute-done((f32[8,16,128]{2,1,0:T(8,128)S(1)}, f32[8,16,128]{2,1,0:T(8,128)S(1)}, u32[]{:S(2)}, u32[]{:S(2)}) %collective-permute-start.1) | collective-permute-done | bytes 65568 | tf_op jit(solution)/shard_map/ppermute | solution.py:294
  58.1 0.1 shard_map.102
  58.2 20.0 %all_to_all.20.second_ref = f32[16,5,16,128]{3,2,1,0:T(8,128)S(1)} all-to-all(f32[16,5,16,128]{3,2,1,0:T(8,128)S(1)} %shard_map.102), channel_id=1, replica_groups=mesh['y'=4,'x'=4,'k'=8,'l'=2,'c'=2] {'y','x'}, dimensions={0} | all-to-all | bytes 1310720 | tf_op jit(solution)/shard_map/all_to_all | solution.py:296
  78.2 0.0 copy-done.9
  78.2 1.5 copy-done.1
  79.7 4.7 %shard_map.103 = f32[8,4,16,128]{3,2,1,0:T(8,128)S(1)} custom-call(s32[5]{0:T(128)S(1)} %stack.41.place_ref, f32[16,5,16,128]{3,2,1,0:T(8,128)S(1)} %all_to_all.20.second_ref, f32[4,432,256]{2,1,0:T(8,128)S(1)} %copy-done.1, f32[1,256]{1,0:T(1,128)S(1)} %bitcast.29, f32[2,16,128]{2,1,0:T(8,128)S(1)} %reshape_reshape.3.mask_ref, ...), custom_call_target="tpu_custom_call" | custom-call | tf_op jit(solution)/shard_map/pallas_call | solution.py:24
  84.4 0.0 copy-start.2
  84.4 0.0 copy-start.4
  84.4 0.0 copy-start.5
  84.4 0.0 copy-start.7
  84.4 37.1 %all_to_all.21.parts_ref = f32[32,16,128]{2,1,0:T(8,128)S(1)} all-to-all(f32[32,16,128]{2,1,0:T(8,128)S(1)} %bitcast.24), channel_id=1, replica_groups=mesh['y'=4,'x'=4,'k'=8,'l'=2,'c'=2] {'k','l','c'}, dimensions={0} | all-to-all | bytes 524288 | tf_op jit(solution)/shard_map/all_to_all | solution.py:309
  121.5 0.5 shard_map.104
  122.0 18.9 %all_to_all.22.mine_ref = f32[8,16,16,128]{3,2,1,0:T(8,128)S(1)} all-to-all(f32[8,16,16,128]{3,2,1,0:T(8,128)S(1)} %shard_map.104), channel_id=1, replica_groups=mesh['y'=4,'x'=4,'k'=8,'l'=2,'c'=2] {'x','l'}, dimensions={0} | all-to-all | bytes 2097152 | tf_op jit(solution)/shard_map/all_to_all | solution.py:311
  140.9 1.9 %collective-permute-start.2 = (f32[8,16,16,128]{3,2,1,0:T(8,128)S(1)}, f32[8,16,16,128]{3,2,1,0:T(8,128)S(1)}, u32[]{:S(2)}, u32[]{:S(2)}) collective-permute-start(f32[8,16,16,128]{3,2,1,0:T(8,128)S(1)} %all_to_all.22.mine_ref), channel_id=1, source_target_pairs={{0,1},{1,0},{2,3},{3,2},{4,5},{5,4},{6,7},{7,6},{8,9},{9,8},{10,11... | collective-permute-start | bytes 3145736 | tf_op jit(solution)/shard_map/ppermute | solution.py:312
  142.8 2.6 %collective-permute-done.2.other_ref = f32[8,16,16,128]{3,2,1,0:T(8,128)S(1)} collective-permute-done((f32[8,16,16,128]{3,2,1,0:T(8,128)S(1)}, f32[8,16,16,128]{3,2,1,0:T(8,128)S(1)}, u32[]{:S(2)}, u32[]{:S(2)}) %collective-permute-start.2) | collective-permute-done | bytes 1048608 | tf_op jit(solution)/shard_map/ppermute | solution.py:312
  145.5 0.0 copy-done.2
  145.5 0.0 copy-done.4
  145.5 0.0 copy-done.5
  145.5 0.0 copy-done.7
  145.5 5.6 %shard_map.105 = f32[2,64,256]{2,1,0:T(8,128)S(1)} custom-call(s32[5]{0:T(128)S(1)} %stack.41.place_ref, f32[8,16,16,128]{3,2,1,0:T(8,128)S(1)} %all_to_all.22.mine_ref, f32[8,16,16,128]{3,2,1,0:T(8,128)S(1)} %collective-permute-done.2.other_ref, f32[1,256]{1,0:T(1,128)S(1)} %bitcast.27, f32[2,256,256]{2,1,0:T(8,128)S(1)} %copy-done.2, ...), custom_call_target="tpu_custom_call" | custom-call | tf_op jit(solution)/shard_map/pallas_call | solution.py:24
  151.1 3.4 %collective-permute-start.3 = (f32[64,256]{1,0:T(8,128)S(1)}, f32[64,256]{1,0:T(8,128)S(1)}, u32[]{:S(2)}, u32[]{:S(2)}) collective-permute-start(f32[64,256]{1,0:T(8,128)S(1)} %get-tuple-element.15), channel_id=1, source_target_pairs={{0,0},{1,16},{2,2},{3,18},{4,36},{5,52},{6,38},{7,54},{8,72},{9,88... | collective-permute-start | bytes 196616 | tf_op jit(solution)/shard_map/ppermute | solution.py:332
  154.5 4.2 %collective-permute-start.4 = (f32[64,256]{1,0:T(8,128)S(1)}, f32[64,256]{1,0:T(8,128)S(1)}, u32[]{:S(2)}, u32[]{:S(2)}) collective-permute-start(f32[64,256]{1,0:T(8,128)S(1)} %get-tuple-element.16), channel_id=1, source_target_pairs={{0,1},{1,17},{2,3},{3,19},{4,37},{5,53},{6,39},{7,55},{8,73},{9,89... | collective-permute-start | bytes 196616 | tf_op jit(solution)/shard_map/ppermute | solution.py:333
  158.7 0.0 collective-permute-done.3
  158.7 14.4 %collective-permute-done.4 = f32[64,256]{1,0:T(8,128)S(1)} collective-permute-done((f32[64,256]{1,0:T(8,128)S(1)}, f32[64,256]{1,0:T(8,128)S(1)}, u32[]{:S(2)}, u32[]{:S(2)}) %collective-permute-start.4) | collective-permute-done | bytes 65568 | tf_op jit(solution)/shard_map/ppermute | solution.py:333
  173.1 0.7 pad_maximum_fusion
  (6 shorter events, 0.0 us)
Async XLA Ops:
  6.5 71.6 %all-gather.2.cloned.1.call-start = ((), (), s32[]{:S(2)}) async-start(), calls=%async_computation.4 | async-start | bytes 2211840 | tf_op jit(solution)/shard_map/all_gather | solution.py:277
  7.3 0.9 copy-start.6
  8.5 1.3 copy-start
  9.8 7.6 %copy-start.10 = (s32[32]{0:T(128)S(1)}, s32[32]{0:T(128)}, u32[]{:S(2)}) copy-start(s32[32]{0:T(128)} %param.11) | copy-start | bytes 388
  9.8 34.8 %copy-start.3 = (f32[3,3,3,16,256]{4,3,2,1,0:T(8,128)S(1)}, f32[3,3,3,16,256]{4,3,2,1,0:T(8,128)}, u32[]{:S(2)}) copy-start(f32[3,3,3,16,256]{4,3,2,1,0:T(8,128)} %param.13) | copy-start | bytes 1327108
  9.8 34.8 %copy-start.8 = (f32[256]{0:T(256)S(1)}, f32[256]{0:T(256)}, u32[]{:S(2)}) copy-start(f32[256]{0:T(256)} %param.12) | copy-start | bytes 3076
  9.8 34.8 %all-to-all-start = ((f32[16,256,128]{2,1,0:T(8,128)}), f32[16,256,128]{2,1,0:T(8,128)S(1)}, u32[]{:S(2)}, u32[]{:S(2)}) async-start(f32[16,256,128]{2,1,0:T(8,128)} %copy-done), calls=%async_computation | async-start | bytes 4194304 | tf_op jit(solution)/shard_map/all_to_all | solution.py:280
  44.6 33.6 %copy-start.9 = (f32[256]{0:T(256)S(1)}, f32[256]{0:T(256)}, u32[]{:S(2)}) copy-start(f32[256]{0:T(256)} %param.14) | copy-start | bytes 3076
  50.6 5.6 %collective-permute-start = (f32[8,16,128]{2,1,0:T(8,128)S(1)}, f32[8,16,128]{2,1,0:T(8,128)S(1)}, u32[]{:S(2)}, u32[]{:S(2)}) collective-permute-start(f32[8,16,128]{2,1,0:T(8,128)S(1)} %get-tuple-element.10), channel_id=1, source_target_pairs={{0,1},{1,2},{2,3},{3,4},{4,5},{5,6},{6,7},{7,8},{8,9},{9,10},{10,1... | collective-permute-start | bytes 196616 | tf_op jit(solution)/shard_map/ppermute | solution.py:293
  52.5 5.5 %collective-permute-start.1 = (f32[8,16,128]{2,1,0:T(8,128)S(1)}, f32[8,16,128]{2,1,0:T(8,128)S(1)}, u32[]{:S(2)}, u32[]{:S(2)}) collective-permute-start(f32[8,16,128]{2,1,0:T(8,128)S(1)} %get-tuple-element.11), channel_id=1, source_target_pairs={{1,0},{2,1},{3,2},{4,3},{5,4},{6,5},{7,6},{8,7},{9,8},{10,9},{11,1... | collective-permute-start | bytes 196616 | tf_op jit(solution)/shard_map/ppermute | solution.py:294
  78.2 1.5 copy-start.1
  84.4 61.1 %copy-start.2 = (f32[2,256,256]{2,1,0:T(8,128)S(1)}, f32[2,256,256]{2,1,0:T(8,128)}, u32[]{:S(2)}) copy-start(f32[2,256,256]{2,1,0:T(8,128)} %qk_ref.1) | copy-start | bytes 1572868
  84.4 61.1 %copy-start.4 = (f32[256,256]{1,0:T(8,128)S(1)}, f32[256,256]{1,0:T(8,128)}, u32[]{:S(2)}) copy-start(f32[256,256]{1,0:T(8,128)} %value_ref.1) | copy-start | bytes 786436
  84.4 61.1 %copy-start.5 = (f32[256,256]{1,0:T(8,128)S(1)}, f32[256,256]{1,0:T(8,128)}, u32[]{:S(2)}) copy-start(f32[256,256]{1,0:T(8,128)} %proj_ref.1) | copy-start | bytes 786436
  84.4 61.1 %copy-start.7 = (f32[256]{0:T(256)S(1)}, f32[256]{0:T(256)}, u32[]{:S(2)}) copy-start(f32[256]{0:T(256)} %param.16) | copy-start | bytes 3076
  140.9 4.5 %collective-permute-start.2 = (f32[8,16,16,128]{3,2,1,0:T(8,128)S(1)}, f32[8,16,16,128]{3,2,1,0:T(8,128)S(1)}, u32[]{:S(2)}, u32[]{:S(2)}) collective-permute-start(f32[8,16,16,128]{3,2,1,0:T(8,128)S(1)} %all_to_all.22.mine_ref), channel_id=1, source_target_pairs={{0,1},{1,0},{2,3},{3,2},{4,5},{5,4},{6,7},{7,6},{8,9},{9,8},{10,11... | collective-permute-start | bytes 3145736 | tf_op jit(solution)/shard_map/ppermute | solution.py:312
  151.1 7.6 %collective-permute-start.3 = (f32[64,256]{1,0:T(8,128)S(1)}, f32[64,256]{1,0:T(8,128)S(1)}, u32[]{:S(2)}, u32[]{:S(2)}) collective-permute-start(f32[64,256]{1,0:T(8,128)S(1)} %get-tuple-element.15), channel_id=1, source_target_pairs={{0,0},{1,16},{2,2},{3,18},{4,36},{5,52},{6,38},{7,54},{8,72},{9,88... | collective-permute-start | bytes 196616 | tf_op jit(solution)/shard_map/ppermute | solution.py:332
  154.5 18.6 %collective-permute-start.4 = (f32[64,256]{1,0:T(8,128)S(1)}, f32[64,256]{1,0:T(8,128)S(1)}, u32[]{:S(2)}, u32[]{:S(2)}) collective-permute-start(f32[64,256]{1,0:T(8,128)S(1)} %get-tuple-element.16), channel_id=1, source_target_pairs={{0,1},{1,17},{2,3},{3,19},{4,37},{5,53},{6,39},{7,55},{8,73},{9,89... | collective-permute-start | bytes 196616 | tf_op jit(solution)/shard_map/ppermute | solution.py:333
Sparse Core Ops, SparseCore 0:
  9.5 48.3 all-gather.1

commit v2 on v1

--- a/solution.py
+++ b/solution.py
@@ -13,7 +13,7 @@
 f32 = jnp.float32
 bf16 = jnp.bfloat16
 
-Y, X, K, L, CORES = 4, 4, 8, 2, 2
+H, W, X, K, L, CORES = 2, 2, 4, 8, 2, 2
 SPACE = K * L * CORES
 OFFSETS = ((0, 8), (2, -2), (4, -4), (6, -6))
 
@@ -91,79 +91,118 @@
 
 def spread_kernel(video_ref, out_ref):
     flipped = video_ref[...].T
-    for i in range(Y * X):
+    for i in range(W * X):
         out_ref[i] = flipped
 
 
 def conv1_kernel(
-    place_ref, video_ref, weight_ref, gain_ref, mask_ref, own_ref, up_ref, down_ref, kept_ref
+    place_ref, video_ref, weight_ref, partner_ref, gain_ref, mask_ref,
+    own_ref, beside_ref, beyond_ref, kept_ref, high_ref, low_ref, product_ref,
 ):
     _, _, row = lanes()
     first_row = row == 0
     gain = column(gain_ref[...])
-    w_high, w_low = split(weight_ref[...])
-    kept_ref[...] = video_ref[pl.ds(4 * place_ref[0], 4), :, place_ref[1]]
+    for g, ref in enumerate((weight_ref, partner_ref)):
+        high_ref[g], low_ref[g] = split(ref[...])
+    half, across, core = place_ref[0], place_ref[2], place_ref[3]
+    kept_ref[...] = video_ref[pl.ds(4 * place_ref[1], 4), :, across]
+
+    def finish(j, now, before):
+        masks = mask_ref[0, pl.ds(8 * half + j, 1)], mask_ref[1, pl.ds(8 * half + j, 1)]
+        outside = []
+        for g in range(2):
+            done = in_time(now[g], before[g], *masks)
+            own_ref[j, half if g == 0 else 1 - half] = done[:16]
+            outside.append(done[16:])
+        up = jnp.where(first_row, outside[0], pltpu.roll(outside[1], 32, 1))
+        down = jnp.where(first_row, pltpu.roll(outside[0], 96, 1), outside[1])
+        on_even = core == 0
+        beside_ref[j] = jnp.where(on_even, down, up)
+        beyond_ref[j] = jnp.where(on_even, up, down)
 
     def step(p, before):
         pieces = []
-        for half in range(2):
-            tile = video_ref[2 * p + half].reshape(256, 128)
+        for side in range(2):
+            tile = video_ref[2 * p + side].reshape(256, 128)
             pieces.append(split(norm_silu(tile, gain)))
         high = jnp.concatenate([pieces[0][0], pieces[1][0]], axis=1)
         low = jnp.concatenate([pieces[0][1], pieces[1][1]], axis=1)
-        product = dot3(w_high, w_low, high, low)
-        outside = []
-        for half in range(2):
-            j = 2 * p + half
-            now = taps(product[:, 128 * half : 128 * half + 128])
-            done = in_time(now, before, mask_ref[0, pl.ds(j, 1)], mask_ref[1, pl.ds(j, 1)])
-            own_ref[j] = done[:16]
-            outside.append(done[16:])
+        for g in range(2):
+            product_ref[g] = dot3(high_ref[g], low_ref[g], high, low)
+        for side in range(2):
+            now = [taps(product_ref[g, :, 128 * side : 128 * side + 128]) for g in range(2)]
+            finish(2 * p + side, now, before)
             before = now
-        up_ref[p] = jnp.where(first_row, outside[0], pltpu.roll(outside[1], 32, 1))
-        down_ref[p] = jnp.where(first_row, pltpu.roll(outside[0], 96, 1), outside[1])
         return before
 
-    zero = jnp.zeros((32, 128), f32)
-    lax.fori_loop(0, 8, step, [zero, zero, zero])
-
-
-def join1_kernel(own_ref, from_above_ref, from_below_ref, out_ref):
+    zeros = [[jnp.zeros((32, 128), f32)] * 3] * 2
+    last = lax.fori_loop(0, 4, step, zeros)
+    finish(8, zeros, last)
+
+
+def join1_kernel(place_ref, own_ref, beside_ref, beyond_ref, out_ref, history_ref):
     _, _, row = lanes()
     first_row = row == 0
-    out_ref[0:4, 0] = jnp.zeros((4, 16, 128), f32)
-    for p in range(8):
-        above, below = from_above_ref[p], from_below_ref[p]
+    on_even = place_ref[3] == 0
+    for j in range(9):
+        beside, beyond = beside_ref[j], beyond_ref[j]
+        above = jnp.where(on_even, beyond, beside)
+        below = jnp.where(on_even, beside, beyond)
         added = (
             jnp.where(first_row, above, pltpu.roll(below, 32, 1)),
             jnp.where(first_row, pltpu.roll(above, 96, 1), below),
         )
-        for half in range(2):
-            j = 2 * p + half
-            tile = own_ref[j] + added[half]
-            y, q = j // 4, j % 4
+        half = place_ref[0]
+        for g in range(2):
+            slot = half if g == 0 else 1 - half
+            tile = own_ref[j, slot] + added[g]
+            if j < 8:
+                out_ref[j, slot] = tile
+            if j >= 7:
+                history_ref[j - 7, slot] = tile
+
+
+def send1_kernel(tiles_ref, history_ref, out_ref):
+    for w in range(W):
+        for q in range(5):
+            j = 4 * w + q - 1
+            tile = history_ref[0] if j < 0 else tiles_ref[j]
+            if j == 0:
+                tile = tile + history_ref[1]
             for x in range(X):
-                out_ref[4 * y + x, q + 1] = tile
-                if q == 3 and y < 3:
-                    out_ref[4 * (y + 1) + x, 0] = tile
+                out_ref[X * w + x, q] = tile
 
 
 def conv2_kernel(
-    place_ref, second_ref, weight_ref, gain_ref, mask_ref, kept_ref, out_ref, high_ref, low_ref
+    place_ref, second_ref, weight_ref, partner_ref, others_ref, gain_ref, mask_ref, kept_ref,
+    out_ref, high_ref, low_ref, w_high_ref, w_low_ref,
 ):
     lane, _, _ = lanes()
     low_half = lane < 64
     gain = column(gain_ref[...])
+    half, inner = place_ref[0], place_ref[1]
     for q in range(5):
-        tile = second_ref[:, q].reshape(256, 128)
-        high, low = split(norm_silu(tile, gain))
+        blocks = []
+        for slot in range(2):
+            for u in range(W):
+                source = jnp.where(half == slot, u, 1 - u)
+                blocks += [second_ref[X * source + x, q, slot] for x in range(X)]
+        high, low = split(norm_silu(jnp.concatenate(blocks, axis=0), gain))
         high_ref[:, 128 * q : 128 * q + 128] = high
         low_ref[:, 128 * q : 128 * q + 128] = low
-    first = 4 * place_ref[0]
+    mine = 2 * half + inner
+    beside = 2 * half + 1 - inner
+    for slot, value in (
+        (mine, weight_ref[...]),
+        (3 - mine, partner_ref[...]),
+        (beside, others_ref[0]),
+        (3 - beside, others_ref[1]),
+    ):
+        w_high_ref[slot], w_low_ref[slot] = split(value)
+    first = 4 * mine
 
     def step(g, _):
-        w_high, w_low = split(weight_ref[g])
-        product = dot3(w_high, w_low, high_ref[...], low_ref[...])
+        product = dot3(w_high_ref[g], w_low_ref[g], high_ref[...], low_ref[...])
         before = taps(product[:, :128])
         for q in range(4):
             now = taps(product[:, 128 * (q + 1) : 128 * (q + 2)])
@@ -203,7 +242,7 @@
     blocked_ref, normed_ref, high_ref, low_ref,
 ):
     gain = column(gain_ref[...])
-    even = place_ref[2] == 0
+    even = place_ref[3] == 0
     for p in range(16):
         mine, other = mine_ref[:, p], other_ref[:, p]
         on_0 = jnp.where(even, mine, other)
@@ -219,7 +258,7 @@
         high, low = split(normed)
         high_ref[:, 128 * p : 128 * p + 128] = high
         low_ref[:, 128 * p : 128 * p + 128] = low
-    at = place_ref[3]
+    at = place_ref[4]
     rows = blocked_ref[at].T
     normed_rows = rows * lax.rsqrt(jnp.mean(rows * rows, axis=1, keepdims=True) + epsilon) * gain_ref[...]
     queries = jnp.dot(normed_rows, qk_ref[0], precision=highest, preferred_element_type=f32)
@@ -234,7 +273,7 @@
     attended = jnp.dot(attended, value_ref[...], precision=highest, preferred_element_type=f32)
     attended = jnp.dot(attended, proj_ref[...], precision=highest, preferred_element_type=f32)
     result = rows + attended
-    swapped = place_ref[4]
+    swapped = place_ref[5]
     out_ref[swapped] = result[:64]
     out_ref[1 - swapped] = result[64:]
 
@@ -266,41 +305,62 @@
     proj_weight,
 ):
     space = ("k", "l", "c")
-    y, x, k, l, c = (lax.axis_index(n) for n in ("y", "x", "k", "l", "c"))
+    h, w, x, k, l, c = (lax.axis_index(n) for n in ("h", "w", "x", "k", "l", "c"))
     offset = jnp.where(c == 0, jnp.where(x == 0, 0, 2 * x), jnp.where(x == 0, 8, -2 * x))
-    place = jnp.stack([y, x, c, (2 * k + l + offset) % (K * L), k // 4]).astype(jnp.int32)
+    place = jnp.stack([h, w, x, c, (2 * k + l + offset) % (K * L), k // 4]).astype(jnp.int32)
 
     earlier = jnp.concatenate([jnp.full((2,), -1, jnp.int32), clip_ids])
     same = jnp.stack([earlier[1:-1] == clip_ids, earlier[:-2] == clip_ids]).astype(f32)
     masks = jnp.repeat(same, 64, axis=1).reshape(2, 16, 128)
-
-    weight_2 = lax.all_gather(conv2_weight.reshape(432, 256), "y", axis=0)
-
-    spread = call(spread_kernel, shape(Y * X, 256, 128), [], video.reshape(128, 256))
-    everywhere = lax.all_to_all(spread, ("y", "x"), 0, 0)
-    own, up, down, kept = call(
+    masks = jnp.concatenate([masks, jnp.zeros((2, 1, 128), f32)], axis=1)
+
+    mirror = [(i, 3 - i) for i in range(H * W)]
+    weight_1 = conv1_weight.reshape(432, 256)
+    weight_2 = conv2_weight.reshape(432, 256)
+    partner_1 = lax.ppermute(weight_1, ("h", "w"), mirror)
+    partner_2 = lax.ppermute(weight_2, ("h", "w"), mirror)
+    others_2 = lax.ppermute(jnp.stack([weight_2, partner_2]), "w", [(0, 1), (1, 0)])
+
+    spread = call(spread_kernel, shape(W * X, 256, 128), [], video.reshape(128, 256))
+    gathered = lax.all_to_all(spread, ("w", "x"), 0, 0)
+    weights_scratch = [pltpu.VMEM((2, 432, 256), bf16)] * 2
+    own, beside, beyond, kept = call(
         conv1_kernel,
-        [shape(16, 16, 128), shape(8, 16, 128), shape(8, 16, 128), shape(4, Y, 16, 128)],
-        [],
+        [shape(9, 2, 16, 128), shape(9, 16, 128), shape(9, 16, 128), shape(4, H * W, 16, 128)],
+        weights_scratch + [pltpu.VMEM((2, 432, 256), f32)],
         place,
-        everywhere.reshape(16, Y, X, 16, 128),
-        conv1_weight.reshape(432, 256),
+        gathered.reshape(W * X, H * W, X, 16, 128),
+        weight_1,
+        partner_1,
         norm1_gain.reshape(1, 256),
         masks,
         smem=1,
     )
-    onward = [(i, i + 1) for i in range(SPACE - 1)]
-    from_above = lax.ppermute(down, space, onward)
-    from_below = lax.ppermute(up, space, [(j, i) for i, j in onward])
-    second = call(join1_kernel, shape(Y * X, 5, 16, 128), [], own, from_above, from_below)
-    second = lax.all_to_all(second, ("y", "x"), 0, 0)
+    between_chips = [(i, i + 1) for i in range(1, SPACE - 1, 2)]
+    beyond = lax.ppermute(beyond, space, between_chips + [(j, i) for i, j in between_chips])
+    beside = lax.ppermute(beside, "c", [(0, 1), (1, 0)])
+    tiles, history = call(
+        join1_kernel,
+        [shape(8, 2, 16, 128), shape(2, 2, 16, 128)],
+        [],
+        place,
+        own,
+        beside,
+        beyond,
+        smem=1,
+    )
+    history = lax.ppermute(history, ("h", "w"), mirror[: H * W // 2])
+    second = call(send1_kernel, shape(W * X, 5, 2, 16, 128), [], tiles, history)
+    second = lax.all_to_all(second, ("w", "x"), 0, 0)
     parts = call(
         conv2_kernel,
         shape(K, 4, 16, 128),
-        [pltpu.VMEM((256, 640), bf16)] * 2,
+        [pltpu.VMEM((256, 640), bf16)] * 2 + [pltpu.VMEM((4, 432, 256), bf16)] * 2,
         place,
         second,
         weight_2,
+        partner_2,
+        others_2,
         norm2_gain.reshape(1, 256),
         masks,
         kept,
@@ -337,8 +397,8 @@
 
 
 def solution(mesh):
-    grid = Mesh(mesh.devices.reshape(Y, X, K, L, CORES), ("y", "x", "k", "l", "c"))
-    tm, space = ("y", "x"), ("k", "l", "c")
+    grid = Mesh(mesh.devices.reshape(H, W, X, K, L, CORES), ("h", "w", "x", "k", "l", "c"))
+    tm, space = ("h", "w", "x"), ("k", "l", "c")
     in_specs = (
         P(tm, space, None, None),
         P(),

time: 181 us -> 164 us (0.906)
  the two profiles are of different devices: /device:TPU:34 before, /device:TPU:50 now
where the time goes in v2:
time: 164 us; the launch traced here: 163 us
  blocking collectives  55.2 us (34%)
  waiting for transfers between devices  46.3 us (28%)
  starting transfers between devices  38.7 us (24%)
  Pallas kernels  18.7 us (11%)
  local copies, waits for them, and re-layouts  2.55 us (2%)
  other arithmetic  1.75 us (1%)
    all_to_all x1, blocking collectives, body(): parts = lax.all_to_all(parts.reshape(SPACE, 16, 128), space, 0, 0)  36.4 us
    all_to_all x1, blocking collectives, body(): mine = lax.all_to_all(frame, ('x', 'l'), 0, 0)  18.8 us
    pallas_call x7, Pallas kernels, call(): pl.pallas_call(kernel, out_shape=out_shape, in_specs=[pl.BlockSpec(memory...  18.7 us
    ppermute x1, waiting for transfers between devices, body(): other_core = lax.ppermute(encoded[1], ('x', 'k', 'l', 'c'), route_1)  14.6 us
    all_to_all x1, waiting for transfers between devices, body(): second = lax.all_to_all(second, ('w', 'x'), 0, 0)  9.83 us
    ppermute x1, waiting for transfers between devices, body(): partner_2 = lax.ppermute(weight_2, ('h', 'w'), mirror)  9.13 us
    all_to_all x1, starting transfers between devices, body(): second = lax.all_to_all(second, ('w', 'x'), 0, 0)  7.95 us
    all_to_all x1, starting transfers between devices, body(): gathered = lax.all_to_all(spread, ('w', 'x'), 0, 0)  5.68 us
  transfers between devices with their start and end apart: 11, of which 7 were waited for; matrix products, arithmetic and copies ran while one was open for 1% of the time, Pallas kernels for 4%

profile of v2, /device:TPU:50, one launch (start us, length us, event | category | flops | bytes accessed | tf_op | source)
XLA Modules:
  0.0 163.4 jit_solution(13997470770797591419)
XLA Ops:
  0.0 0.9 copy-done.5
  0.9 1.2 shard_map.100
  2.1 5.7 %all-to-all-start = ((f32[8,256,128]{2,1,0:T(8,128)}), f32[8,256,128]{2,1,0:T(8,128)S(1)}, u32[]{:S(2)}, u32[]{:S(2)}) async-start(f32[8,256,128]{2,1,0:T(8,128)} %shard_map.100), calls=%async_computation | async-start | bytes 2097152 | tf_op jit(solution)/shard_map/all_to_all | solution.py:325
  7.8 0.0 copy-done
  7.8 2.5 %collective-permute-start.4 = (f32[432,256]{1,0:T(8,128)S(1)}, f32[432,256]{1,0:T(8,128)S(1)}, u32[]{:S(2)}, u32[]{:S(2)}) collective-permute-start(f32[432,256]{1,0:T(8,128)S(1)} %bitcast.27), channel_id=1, source_target_pairs={{0,384},{128,256},{256,128},{384,0},{1,385},{129,257},{257,129},{3... | collective-permute-start | bytes 1327112 | tf_op jit(solution)/shard_map/ppermute | solution.py:321
  10.3 0.0 copy-done.2
  10.3 3.3 %collective-permute-start = (f32[432,256]{1,0:T(8,128)S(1)}, f32[432,256]{1,0:T(8,128)}, u32[]{:S(2)}, u32[]{:S(2)}) collective-permute-start(f32[432,256]{1,0:T(8,128)S(1)} %bitcast.32), channel_id=1, source_target_pairs={{0,384},{128,256},{256,128},{384,0},{1,385},{129,257},{257,129},{3... | collective-permute-start | bytes 1327112 | tf_op jit(solution)/shard_map/ppermute | solution.py:320
  13.6 9.1 %collective-permute-done.4.partner_ref = f32[432,256]{1,0:T(8,128)S(1)} collective-permute-done((f32[432,256]{1,0:T(8,128)S(1)}, f32[432,256]{1,0:T(8,128)S(1)}, u32[]{:S(2)}, u32[]{:S(2)}) %collective-permute-start.4) | collective-permute-done | bytes 442400 | tf_op jit(solution)/shard_map/ppermute | solution.py:321
  22.8 1.0 pad_maximum_fusion
  23.8 4.6 %collective-permute-start.5 = (f32[2,432,256]{2,1,0:T(8,128)}, f32[2,432,256]{2,1,0:T(8,128)S(1)}, u32[]{:S(2)}, u32[]{:S(2)}) collective-permute-start(f32[2,432,256]{2,1,0:T(8,128)} %pad_maximum_fusion), channel_id=1, source_target_pairs={{0,128},{128,0},{1,129},{129,1},{2,130},{130,2},{3,131},{131,3},{4... | collective-permute-start | bytes 2654216 | tf_op jit(solution)/shard_map/ppermute | solution.py:322
  28.3 0.0 copy-done.9
  28.3 0.1 compare_bitcast_fusion.1
  28.4 0.1 broadcast_in_dim.4
  28.5 0.1 reshape_reshape.3
  28.6 0.1 stack.51.place_ref
  28.7 1.9 %collective-permute-done.partner_ref = f32[432,256]{1,0:T(8,128)} collective-permute-done((f32[432,256]{1,0:T(8,128)S(1)}, f32[432,256]{1,0:T(8,128)}, u32[]{:S(2)}, u32[]{:S(2)}) %collective-permute-start) | collective-permute-done | bytes 442400 | tf_op jit(solution)/shard_map/ppermute | solution.py:320
  30.6 0.0 all-to-all-done
  30.6 0.7 copy-done.7
  31.3 4.7 %shard_map.101 = (f32[9,2,16,128]{3,2,1,0:T(8,128)S(1)}, f32[9,16,128]{2,1,0:T(8,128)S(1)}, f32[9,16,128]{2,1,0:T(8,128)S(1)}, f32[4,4,16,128]{3,2,1,0:T(8,128)S(1)}) custom-call(s32[6]{0:T(128)S(1)} %stack.51.place_ref, f32[8,4,4,16,128]{4,3,2,1,0:T(8,128)S(1)} %bitcast.26, f32[432,256]{1,0:T(8,128)S(1)} %bitcast.33, ...), custom_call_target="tpu_custom_call" | custom-call | tf_op jit(solution)/shard_map/pallas_call | solution.py:24
  36.0 1.9 %collective-permute-start.1 = (f32[9,16,128]{2,1,0:T(8,128)S(1)}, f32[9,16,128]{2,1,0:T(8,128)S(1)}, u32[]{:S(2)}, u32[]{:S(2)}) collective-permute-start(f32[9,16,128]{2,1,0:T(8,128)S(1)} %get-tuple-element.12), channel_id=1, source_target_pairs={{0,1},{1,0},{2,3},{3,2},{4,5},{5,4},{6,7},{7,6},{8,9},{9,8},{10,11... | collective-permute-start | bytes 221192 | tf_op jit(solution)/shard_map/ppermute | solution.py:341
  37.9 2.1 %collective-permute-start.2 = (f32[9,16,128]{2,1,0:T(8,128)S(1)}, f32[9,16,128]{2,1,0:T(8,128)S(1)}, u32[]{:S(2)}, u32[]{:S(2)}) collective-permute-start(f32[9,16,128]{2,1,0:T(8,128)S(1)} %get-tuple-element.13), channel_id=1, source_target_pairs={{1,2},{3,4},{5,6},{7,8},{9,10},{11,12},{13,14},{15,16},{17,18},{19... | collective-permute-start | bytes 221192 | tf_op jit(solution)/shard_map/ppermute | solution.py:340
  40.1 0.0 collective-permute-done.1.beside_ref
  40.1 3.5 %collective-permute-done.2.beyond_ref = f32[9,16,128]{2,1,0:T(8,128)S(1)} collective-permute-done((f32[9,16,128]{2,1,0:T(8,128)S(1)}, f32[9,16,128]{2,1,0:T(8,128)S(1)}, u32[]{:S(2)}, u32[]{:S(2)}) %collective-permute-start.2) | collective-permute-done | bytes 73760 | tf_op jit(solution)/shard_map/ppermute | solution.py:340
  43.6 0.6 shard_map.102
  44.3 1.3 collective-permute-start.3
  45.6 4.7 %collective-permute-done.3.history_ref = f32[2,2,16,128]{3,2,1,0:T(8,128)S(1)} collective-permute-done((f32[2,2,16,128]{3,2,1,0:T(8,128)S(1)}, f32[2,2,16,128]{3,2,1,0:T(8,128)S(1)}, u32[]{:S(2)}, u32[]{:S(2)}) %collective-permute-start.3) | collective-permute-done | bytes 32800 | tf_op jit(solution)/shard_map/ppermute | solution.py:352
  50.2 0.9 shard_map.103
  51.1 7.9 %all-to-all-start.1 = ((f32[8,5,2,16,128]{4,3,2,1,0:T(8,128)}), f32[8,5,2,16,128]{4,3,2,1,0:T(8,128)S(1)}, u32[]{:S(2)}, u32[]{:S(2)}) async-start(f32[8,5,2,16,128]{4,3,2,1,0:T(8,128)} %shard_map.103), calls=%async_computation.1 | async-start | bytes 1310720 | tf_op jit(solution)/shard_map/all_to_all | solution.py:354
  59.1 0.0 collective-permute-done.5.others_ref
  59.1 9.8 %all-to-all-done.1.second_ref = f32[8,5,2,16,128]{4,3,2,1,0:T(8,128)S(1)} async-done(((f32[8,5,2,16,128]{4,3,2,1,0:T(8,128)}), f32[8,5,2,16,128]{4,3,2,1,0:T(8,128)S(1)}, u32[]{:S(2)}, u32[]{:S(2)}) %all-to-all-start.1) | async-done | bytes 655392 | tf_op jit(solution)/shard_map/all_to_all | solution.py:354
  68.9 0.7 copy-done.8
  69.6 5.2 %shard_map.104 = f32[8,4,16,128]{3,2,1,0:T(8,128)S(1)} custom-call(s32[6]{0:T(128)S(1)} %stack.51.place_ref, f32[8,5,2,16,128]{4,3,2,1,0:T(8,128)S(1)} %all-to-all-done.1.second_ref, f32[432,256]{1,0:T(8,128)S(1)} %bitcast.29, f32[432,256]{1,0:T(8,128)S(1)} %collective-permute-done.4.partner_ref, f32[2,432,256]{2,1,0:T(8,128)S(1)} %collective-permute-done.5.others_ref, ...), custom_call_target="tpu_custom_call" | custom-call | tf_op jit(solution)/shard_map/pallas_call | solution.py:24
  74.8 36.4 %all_to_all.20.parts_ref = f32[32,16,128]{2,1,0:T(8,128)S(1)} all-to-all(f32[32,16,128]{2,1,0:T(8,128)S(1)} %bitcast.31), channel_id=1, replica_groups=mesh['h'=2,'w'=2,'x'=4,'k'=8,'l'=2,'c'=2] {'k','l','c'}, dimensions={0} | all-to-all | bytes 524288 | tf_op jit(solution)/shard_map/all_to_all | solution.py:369
  111.2 0.5 shard_map.105
  111.7 0.0 copy-start.1
  111.7 0.0 copy-start.3
  111.7 0.0 copy-start.4
  111.7 18.8 %all_to_all.21.mine_ref = f32[8,16,16,128]{3,2,1,0:T(8,128)S(1)} all-to-all(f32[8,16,16,128]{3,2,1,0:T(8,128)S(1)} %shard_map.105), channel_id=1, replica_groups=mesh['h'=2,'w'=2,'x'=4,'k'=8,'l'=2,'c'=2] {'x','l'}, dimensions={0} | all-to-all | bytes 2097152 | tf_op jit(solution)/shard_map/all_to_all | solution.py:371
  130.5 2.0 %collective-permute-start.6 = (f32[8,16,16,128]{3,2,1,0:T(8,128)S(1)}, f32[8,16,16,128]{3,2,1,0:T(8,128)S(1)}, u32[]{:S(2)}, u32[]{:S(2)}) collective-permute-start(f32[8,16,16,128]{3,2,1,0:T(8,128)S(1)} %all_to_all.21.mine_ref), channel_id=1, source_target_pairs={{0,1},{1,0},{2,3},{3,2},{4,5},{5,4},{6,7},{7,6},{8,9},{9,8},{10,11... | collective-permute-start | bytes 3145736 | tf_op jit(solution)/shard_map/ppermute | solution.py:372
  132.6 2.6 %collective-permute-done.6.other_ref = f32[8,16,16,128]{3,2,1,0:T(8,128)S(1)} collective-permute-done((f32[8,16,16,128]{3,2,1,0:T(8,128)S(1)}, f32[8,16,16,128]{3,2,1,0:T(8,128)S(1)}, u32[]{:S(2)}, u32[]{:S(2)}) %collective-permute-start.6) | collective-permute-done | bytes 1048608 | tf_op jit(solution)/shard_map/ppermute | solution.py:372
  135.2 0.0 copy-done.1
  135.2 0.0 copy-done.3
  135.2 5.6 %shard_map.106 = f32[2,64,256]{2,1,0:T(8,128)S(1)} custom-call(s32[6]{0:T(128)S(1)} %stack.51.place_ref, f32[8,16,16,128]{3,2,1,0:T(8,128)S(1)} %all_to_all.21.mine_ref, f32[8,16,16,128]{3,2,1,0:T(8,128)S(1)} %collective-permute-done.6.other_ref, f32[1,256]{1,0:T(1,128)S(1)} %bitcast.35, f32[2,256,256]{2,1,0:T(8,128)S(1)} %copy-done.1, ...), custom_call_target="tpu_custom_call" | custom-call | tf_op jit(solution)/shard_map/pallas_call | solution.py:24
  140.8 3.4 %collective-permute-start.7 = (f32[64,256]{1,0:T(8,128)S(1)}, f32[64,256]{1,0:T(8,128)S(1)}, u32[]{:S(2)}, u32[]{:S(2)}) collective-permute-start(f32[64,256]{1,0:T(8,128)S(1)} %get-tuple-element.19), channel_id=1, source_target_pairs={{0,0},{1,16},{2,2},{3,18},{4,36},{5,52},{6,38},{7,54},{8,72},{9,88... | collective-permute-start | bytes 196616 | tf_op jit(solution)/shard_map/ppermute | solution.py:392
  144.2 3.9 %collective-permute-start.8 = (f32[64,256]{1,0:T(8,128)S(1)}, f32[64,256]{1,0:T(8,128)S(1)}, u32[]{:S(2)}, u32[]{:S(2)}) collective-permute-start(f32[64,256]{1,0:T(8,128)S(1)} %get-tuple-element.20), channel_id=1, source_target_pairs={{0,1},{1,17},{2,3},{3,19},{4,37},{5,53},{6,39},{7,55},{8,73},{9,89... | collective-permute-start | bytes 196616 | tf_op jit(solution)/shard_map/ppermute | solution.py:393
  148.1 0.0 collective-permute-done.7
  148.1 14.6 %collective-permute-done.8 = f32[64,256]{1,0:T(8,128)S(1)} collective-permute-done((f32[64,256]{1,0:T(8,128)S(1)}, f32[64,256]{1,0:T(8,128)S(1)}, u32[]{:S(2)}, u32[]{:S(2)}) %collective-permute-start.8) | collective-permute-done | bytes 65568 | tf_op jit(solution)/shard_map/ppermute | solution.py:393
  162.7 0.7 pad_maximum_fusion.1
  (13 shorter events, 0.1 us)
Async XLA Ops:
  0.0 0.9 copy-start.5
  2.1 5.7 %copy-start = (f32[3,3,3,16,256]{4,3,2,1,0:T(8,128)S(1)}, f32[3,3,3,16,256]{4,3,2,1,0:T(8,128)}, u32[]{:S(2)}) copy-start(f32[3,3,3,16,256]{4,3,2,1,0:T(8,128)} %param.15) | copy-start | bytes 1327108
  2.1 8.2 %copy-start.2 = (f32[3,3,3,16,256]{4,3,2,1,0:T(8,128)S(1)}, f32[3,3,3,16,256]{4,3,2,1,0:T(8,128)}, u32[]{:S(2)}) copy-start(f32[3,3,3,16,256]{4,3,2,1,0:T(8,128)} %param.13) | copy-start | bytes 1327108
  2.1 28.5 %all-to-all-start = ((f32[8,256,128]{2,1,0:T(8,128)}), f32[8,256,128]{2,1,0:T(8,128)S(1)}, u32[]{:S(2)}, u32[]{:S(2)}) async-start(f32[8,256,128]{2,1,0:T(8,128)} %shard_map.100), calls=%async_computation | async-start | bytes 2097152 | tf_op jit(solution)/shard_map/all_to_all | solution.py:325
  7.8 15.0 %collective-permute-start.4 = (f32[432,256]{1,0:T(8,128)S(1)}, f32[432,256]{1,0:T(8,128)S(1)}, u32[]{:S(2)}, u32[]{:S(2)}) collective-permute-start(f32[432,256]{1,0:T(8,128)S(1)} %bitcast.27), channel_id=1, source_target_pairs={{0,384},{128,256},{256,128},{384,0},{1,385},{129,257},{257,129},{3... | collective-permute-start | bytes 1327112 | tf_op jit(solution)/shard_map/ppermute | solution.py:321
  10.3 20.3 %collective-permute-start = (f32[432,256]{1,0:T(8,128)S(1)}, f32[432,256]{1,0:T(8,128)}, u32[]{:S(2)}, u32[]{:S(2)}) collective-permute-start(f32[432,256]{1,0:T(8,128)S(1)} %bitcast.32), channel_id=1, source_target_pairs={{0,384},{128,256},{256,128},{384,0},{1,385},{129,257},{257,129},{3... | collective-permute-start | bytes 1327112 | tf_op jit(solution)/shard_map/ppermute | solution.py:320
  22.8 5.6 %copy-start.9 = (s32[32]{0:T(128)S(1)}, s32[32]{0:T(128)}, u32[]{:S(2)}) copy-start(s32[32]{0:T(128)} %param.11) | copy-start | bytes 388
  23.8 35.3 %collective-permute-start.5 = (f32[2,432,256]{2,1,0:T(8,128)}, f32[2,432,256]{2,1,0:T(8,128)S(1)}, u32[]{:S(2)}, u32[]{:S(2)}) collective-permute-start(f32[2,432,256]{2,1,0:T(8,128)} %pad_maximum_fusion), channel_id=1, source_target_pairs={{0,128},{128,0},{1,129},{129,1},{2,130},{130,2},{3,131},{131,3},{4... | collective-permute-start | bytes 2654216 | tf_op jit(solution)/shard_map/ppermute | solution.py:322
  30.6 0.7 copy-start.7
  36.0 4.1 %collective-permute-start.1 = (f32[9,16,128]{2,1,0:T(8,128)S(1)}, f32[9,16,128]{2,1,0:T(8,128)S(1)}, u32[]{:S(2)}, u32[]{:S(2)}) collective-permute-start(f32[9,16,128]{2,1,0:T(8,128)S(1)} %get-tuple-element.12), channel_id=1, source_target_pairs={{0,1},{1,0},{2,3},{3,2},{4,5},{5,4},{6,7},{7,6},{8,9},{9,8},{10,11... | collective-permute-start | bytes 221192 | tf_op jit(solution)/shard_map/ppermute | solution.py:341
  37.9 5.7 %collective-permute-start.2 = (f32[9,16,128]{2,1,0:T(8,128)S(1)}, f32[9,16,128]{2,1,0:T(8,128)S(1)}, u32[]{:S(2)}, u32[]{:S(2)}) collective-permute-start(f32[9,16,128]{2,1,0:T(8,128)S(1)} %get-tuple-element.13), channel_id=1, source_target_pairs={{1,2},{3,4},{5,6},{7,8},{9,10},{11,12},{13,14},{15,16},{17,18},{19... | collective-permute-start | bytes 221192 | tf_op jit(solution)/shard_map/ppermute | solution.py:340
  44.3 6.0 %collective-permute-start.3 = (f32[2,2,16,128]{3,2,1,0:T(8,128)S(1)}, f32[2,2,16,128]{3,2,1,0:T(8,128)S(1)}, u32[]{:S(2)}, u32[]{:S(2)}) collective-permute-start(f32[2,2,16,128]{3,2,1,0:T(8,128)S(1)} %get-tuple-element.15), channel_id=1, source_target_pairs={{0,384},{128,256},{1,385},{129,257},{2,386},{130,258},{3,387},{131... | collective-permute-start | bytes 98312 | tf_op jit(solution)/shard_map/ppermute | solution.py:352
  51.1 17.8 %all-to-all-start.1 = ((f32[8,5,2,16,128]{4,3,2,1,0:T(8,128)}), f32[8,5,2,16,128]{4,3,2,1,0:T(8,128)S(1)}, u32[]{:S(2)}, u32[]{:S(2)}) async-start(f32[8,5,2,16,128]{4,3,2,1,0:T(8,128)} %shard_map.103), calls=%async_computation.1 | async-start | bytes 1310720 | tf_op jit(solution)/shard_map/all_to_all | solution.py:354
  68.9 0.7 copy-start.8
  111.7 23.5 %copy-start.1 = (f32[2,256,256]{2,1,0:T(8,128)S(1)}, f32[2,256,256]{2,1,0:T(8,128)}, u32[]{:S(2)}) copy-start(f32[2,256,256]{2,1,0:T(8,128)} %qk_ref.1) | copy-start | bytes 1572868
  111.7 23.5 %copy-start.3 = (f32[256,256]{1,0:T(8,128)S(1)}, f32[256,256]{1,0:T(8,128)}, u32[]{:S(2)}) copy-start(f32[256,256]{1,0:T(8,128)} %value_ref.1) | copy-start | bytes 786436
  111.7 23.5 %copy-start.4 = (f32[256,256]{1,0:T(8,128)S(1)}, f32[256,256]{1,0:T(8,128)}, u32[]{:S(2)}) copy-start(f32[256,256]{1,0:T(8,128)} %proj_ref.1) | copy-start | bytes 786436
  130.5 4.7 %copy-start.6 = (f32[256]{0:T(256)S(1)}, f32[256]{0:T(256)}, u32[]{:S(2)}) copy-start(f32[256]{0:T(256)} %param.16) | copy-start | bytes 3076
  130.5 4.7 %collective-permute-start.6 = (f32[8,16,16,128]{3,2,1,0:T(8,128)S(1)}, f32[8,16,16,128]{3,2,1,0:T(8,128)S(1)}, u32[]{:S(2)}, u32[]{:S(2)}) collective-permute-start(f32[8,16,16,128]{3,2,1,0:T(8,128)S(1)} %all_to_all.21.mine_ref), channel_id=1, source_target_pairs={{0,1},{1,0},{2,3},{3,2},{4,5},{5,4},{6,7},{7,6},{8,9},{9,8},{10,11... | collective-permute-start | bytes 3145736 | tf_op jit(solution)/shard_map/ppermute | solution.py:372
  140.8 7.3 %collective-permute-start.7 = (f32[64,256]{1,0:T(8,128)S(1)}, f32[64,256]{1,0:T(8,128)S(1)}, u32[]{:S(2)}, u32[]{:S(2)}) collective-permute-start(f32[64,256]{1,0:T(8,128)S(1)} %get-tuple-element.19), channel_id=1, source_target_pairs={{0,0},{1,16},{2,2},{3,18},{4,36},{5,52},{6,38},{7,54},{8,72},{9,88... | collective-permute-start | bytes 196616 | tf_op jit(solution)/shard_map/ppermute | solution.py:392
  144.2 18.5 %collective-permute-start.8 = (f32[64,256]{1,0:T(8,128)S(1)}, f32[64,256]{1,0:T(8,128)S(1)}, u32[]{:S(2)}, u32[]{:S(2)}) collective-permute-start(f32[64,256]{1,0:T(8,128)S(1)} %get-tuple-element.20), channel_id=1, source_target_pairs={{0,1},{1,17},{2,3},{3,19},{4,37},{5,53},{6,39},{7,55},{8,73},{9,89... | collective-permute-start | bytes 196616 | tf_op jit(solution)/shard_map/ppermute | solution.py:393

commit v3 on v2

--- a/solution.py
+++ b/solution.py
@@ -15,7 +15,7 @@
 
 H, W, X, K, L, CORES = 2, 2, 4, 8, 2, 2
 SPACE = K * L * CORES
-OFFSETS = ((0, 8), (2, -2), (4, -4), (6, -6))
+TILES = 8
 
 VMEM_LIMIT = 48 * 1024 * 1024
 
@@ -101,11 +101,14 @@
 ):
     _, _, row = lanes()
     first_row = row == 0
-    gain = column(gain_ref[...])
+    gain = column(gain_ref[0:1])
     for g, ref in enumerate((weight_ref, partner_ref)):
         high_ref[g], low_ref[g] = split(ref[...])
     half, across, core = place_ref[0], place_ref[2], place_ref[3]
-    kept_ref[...] = video_ref[pl.ds(4 * place_ref[1], 4), :, across]
+    mine = 2 * half + place_ref[1]
+    for j in range(TILES):
+        kept_ref[j, half] = video_ref[j, mine, across]
+        kept_ref[j, 1 - half] = video_ref[j, 3 - mine, across]
 
     def finish(j, now, before):
         masks = mask_ref[0, pl.ds(8 * half + j, 1)], mask_ref[1, pl.ds(8 * half + j, 1)]
@@ -163,25 +166,23 @@
 
 
 def send1_kernel(tiles_ref, history_ref, out_ref):
-    for w in range(W):
-        for q in range(5):
-            j = 4 * w + q - 1
-            tile = history_ref[0] if j < 0 else tiles_ref[j]
-            if j == 0:
-                tile = tile + history_ref[1]
-            for x in range(X):
-                out_ref[X * w + x, q] = tile
+    for q in range(TILES + 1):
+        tile = history_ref[0] if q == 0 else tiles_ref[q - 1]
+        if q == 1:
+            tile = tile + history_ref[1]
+        for i in range(W * X):
+            out_ref[i, q] = tile
 
 
 def conv2_kernel(
-    place_ref, second_ref, weight_ref, partner_ref, others_ref, gain_ref, mask_ref, kept_ref,
-    out_ref, high_ref, low_ref, w_high_ref, w_low_ref,
+    place_ref, second_ref, weight_ref, partner_ref, gain_ref, mask_ref, kept_ref,
+    out_ref, high_ref, low_ref, product_ref,
 ):
     lane, _, _ = lanes()
     low_half = lane < 64
-    gain = column(gain_ref[...])
-    half, inner = place_ref[0], place_ref[1]
-    for q in range(5):
+    gain = column(gain_ref[1:2])
+    half = place_ref[0]
+    for q in range(TILES + 1):
         blocks = []
         for slot in range(2):
             for u in range(W):
@@ -190,33 +191,20 @@
         high, low = split(norm_silu(jnp.concatenate(blocks, axis=0), gain))
         high_ref[:, 128 * q : 128 * q + 128] = high
         low_ref[:, 128 * q : 128 * q + 128] = low
-    mine = 2 * half + inner
-    beside = 2 * half + 1 - inner
-    for slot, value in (
-        (mine, weight_ref[...]),
-        (3 - mine, partner_ref[...]),
-        (beside, others_ref[0]),
-        (3 - beside, others_ref[1]),
-    ):
-        w_high_ref[slot], w_low_ref[slot] = split(value)
-    first = 4 * mine
-
-    def step(g, _):
-        product = dot3(w_high_ref[g], w_low_ref[g], high_ref[...], low_ref[...])
-        before = taps(product[:, :128])
-        for q in range(4):
-            now = taps(product[:, 128 * (q + 1) : 128 * (q + 2)])
-            done = in_time(
-                now, before, mask_ref[0, pl.ds(first + q, 1)], mask_ref[1, pl.ds(first + q, 1)]
-            )
-            own = done[:16] + kept_ref[q, g]
+    for g, ref in enumerate((weight_ref, partner_ref)):
+        slot = half if g == 0 else 1 - half
+        w_high, w_low = split(ref[...])
+        product_ref[...] = dot3(w_high, w_low, high_ref[...], low_ref[...])
+        before = taps(product_ref[:, :128])
+        for q in range(TILES):
+            now = taps(product_ref[:, 128 * (q + 1) : 128 * (q + 2)])
+            at = TILES * half + q
+            done = in_time(now, before, mask_ref[0, pl.ds(at, 1)], mask_ref[1, pl.ds(at, 1)])
+            own = done[:16] + kept_ref[q, slot]
             leave = done[16:]
-            out_ref[q, g] = jnp.where(low_half, own, pltpu.roll(leave, 64, 1))
-            out_ref[q + 4, g] = jnp.where(low_half, pltpu.roll(own, 64, 1), leave)
+            out_ref[q, slot] = jnp.where(low_half, own, pltpu.roll(leave, 64, 1))
+            out_ref[q + TILES, slot] = jnp.where(low_half, pltpu.roll(own, 64, 1), leave)
             before = now
-        return 0
-
-    lax.fori_loop(0, 4, step, 0)
 
 
 def join2_kernel(parts_ref, out_ref):
@@ -233,7 +221,7 @@
 
     for p in range(16):
         tile = jnp.where(low_half, band(2 * p), pltpu.roll(band(2 * p + 1), 64, 1))
-        for i in range(X * L):
+        for i in range(W * X):
             out_ref[i, p] = tile
 
 
@@ -241,16 +229,16 @@
     place_ref, mine_ref, other_ref, gain_ref, qk_ref, value_ref, proj_ref, out_ref,
     blocked_ref, normed_ref, high_ref, low_ref,
 ):
-    gain = column(gain_ref[...])
-    even = place_ref[3] == 0
+    gain = column(gain_ref[2:3])
+    half, core = place_ref[0], place_ref[3]
     for p in range(16):
-        mine, other = mine_ref[:, p], other_ref[:, p]
-        on_0 = jnp.where(even, mine, other)
-        on_1 = jnp.where(even, other, mine)
         blocks = []
-        for l in range(L):
-            for part in (on_0, on_1):
-                blocks += [part[2 * x + l] for x in range(X)]
+        for slot in range(2):
+            for u in range(W):
+                source = X * jnp.where(half == slot, u, 1 - u)
+                for x in range(X):
+                    mine, other = mine_ref[source + x, p], other_ref[source + x, p]
+                    blocks.append(jnp.where(core == slot, mine, other))
         tile = jnp.concatenate(blocks, axis=0)
         blocked_ref[p] = tile
         normed = tile * lax.rsqrt(jnp.mean(tile * tile, axis=0, keepdims=True) + epsilon) * gain
@@ -260,7 +248,7 @@
         low_ref[:, 128 * p : 128 * p + 128] = low
     at = place_ref[4]
     rows = blocked_ref[at].T
-    normed_rows = rows * lax.rsqrt(jnp.mean(rows * rows, axis=1, keepdims=True) + epsilon) * gain_ref[...]
+    normed_rows = rows * lax.rsqrt(jnp.mean(rows * rows, axis=1, keepdims=True) + epsilon) * gain_ref[2:3]
     queries = jnp.dot(normed_rows, qk_ref[0], precision=highest, preferred_element_type=f32)
     queries = lax.dot_general(
         queries, qk_ref[1], (((1,), (1,)), ((), ())), precision=highest, preferred_element_type=f32
@@ -280,15 +268,14 @@
 
 def delivery():
     routes = ([], [])
-    for x in range(X):
-        for k in range(K):
-            for l in range(L):
-                for c in range(CORES):
-                    source = ((x * K + k) * L + l) * CORES + c
-                    chip = (2 * k + l + OFFSETS[x][c]) % (K * L)
-                    f = k // 4
-                    for route, core in zip(routes, (f, 1 - f)):
-                        route.append((source, ((k % 4) * K * L + chip) * CORES + core))
+    for i in range(W * X):
+        for z in range(K * L):
+            for c in range(CORES):
+                source = (i * K * L + z) * CORES + c
+                chip = (z + (i if c == 0 else -i if i else 8)) % (K * L)
+                f = z // TILES
+                for route, core in zip(routes, (f, 1 - f)):
+                    route.append((source, ((z % TILES) * K * L + chip) * CORES + core))
     return routes
 
 
@@ -306,8 +293,9 @@
 ):
     space = ("k", "l", "c")
     h, w, x, k, l, c = (lax.axis_index(n) for n in ("h", "w", "x", "k", "l", "c"))
-    offset = jnp.where(c == 0, jnp.where(x == 0, 0, 2 * x), jnp.where(x == 0, 8, -2 * x))
-    place = jnp.stack([h, w, x, c, (2 * k + l + offset) % (K * L), k // 4]).astype(jnp.int32)
+    z, i = 2 * k + l, X * w + x
+    offset = jnp.where(c == 0, i, jnp.where(i == 0, 8, K * L - i))
+    place = jnp.stack([h, w, x, c, (z + offset) % (K * L), z // TILES]).astype(jnp.int32)
 
     earlier = jnp.concatenate([jnp.full((2,), -1, jnp.int32), clip_ids])
     same = jnp.stack([earlier[1:-1] == clip_ids, earlier[:-2] == clip_ids]).astype(f32)
@@ -319,26 +307,27 @@
     weight_2 = conv2_weight.reshape(432, 256)
     partner_1 = lax.ppermute(weight_1, ("h", "w"), mirror)
     partner_2 = lax.ppermute(weight_2, ("h", "w"), mirror)
-    others_2 = lax.ppermute(jnp.stack([weight_2, partner_2]), "w", [(0, 1), (1, 0)])
+    swap = [(0, 1), (1, 0)]
+    gains = jnp.stack([norm1_gain, norm2_gain, norm3_gain])
 
     spread = call(spread_kernel, shape(W * X, 256, 128), [], video.reshape(128, 256))
     gathered = lax.all_to_all(spread, ("w", "x"), 0, 0)
     weights_scratch = [pltpu.VMEM((2, 432, 256), bf16)] * 2
     own, beside, beyond, kept = call(
         conv1_kernel,
-        [shape(9, 2, 16, 128), shape(9, 16, 128), shape(9, 16, 128), shape(4, H * W, 16, 128)],
+        [shape(9, 2, 16, 128), shape(9, 16, 128), shape(9, 16, 128), shape(TILES, 2, 16, 128)],
         weights_scratch + [pltpu.VMEM((2, 432, 256), f32)],
         place,
         gathered.reshape(W * X, H * W, X, 16, 128),
         weight_1,
         partner_1,
-        norm1_gain.reshape(1, 256),
+        gains,
         masks,
         smem=1,
     )
     between_chips = [(i, i + 1) for i in range(1, SPACE - 1, 2)]
     beyond = lax.ppermute(beyond, space, between_chips + [(j, i) for i, j in between_chips])
-    beside = lax.ppermute(beside, "c", [(0, 1), (1, 0)])
+    beside = lax.ppermute(beside, "c", swap)
     tiles, history = call(
         join1_kernel,
         [shape(8, 2, 16, 128), shape(2, 2, 16, 128)],
@@ -350,26 +339,25 @@
         smem=1,
     )
     history = lax.ppermute(history, ("h", "w"), mirror[: H * W // 2])
-    second = call(send1_kernel, shape(W * X, 5, 2, 16, 128), [], tiles, history)
+    second = call(send1_kernel, shape(W * X, TILES + 1, 2, 16, 128), [], tiles, history)
     second = lax.all_to_all(second, ("w", "x"), 0, 0)
     parts = call(
         conv2_kernel,
-        shape(K, 4, 16, 128),
-        [pltpu.VMEM((256, 640), bf16)] * 2 + [pltpu.VMEM((4, 432, 256), bf16)] * 2,
+        shape(K * L, CORES, 16, 128),
+        [pltpu.VMEM((256, 1152), bf16)] * 2 + [pltpu.VMEM((432, 1152), f32)],
         place,
         second,
         weight_2,
         partner_2,
-        others_2,
-        norm2_gain.reshape(1, 256),
+        gains,
         masks,
         kept,
         smem=1,
     )
     parts = lax.all_to_all(parts.reshape(SPACE, 16, 128), space, 0, 0)
-    frame = call(join2_kernel, shape(X * L, 16, 16, 128), [], parts)
-    mine = lax.all_to_all(frame, ("x", "l"), 0, 0)
-    other = lax.ppermute(mine, "c", [(0, 1), (1, 0)])
+    frame = call(join2_kernel, shape(W * X, 16, 16, 128), [], parts)
+    mine = lax.all_to_all(frame, ("w", "x"), 0, 0)
+    other = lax.ppermute(mine, "c", swap)
     encoded = call(
         attend_kernel,
         shape(2, 64, 256),
@@ -382,15 +370,15 @@
         place,
         mine,
         other,
-        norm3_gain.reshape(1, 256),
+        gains,
         qk_weight,
         value_weight,
         proj_weight,
         smem=1,
     )
     route_0, route_1 = delivery()
-    same_core = lax.ppermute(encoded[0], ("x", "k", "l", "c"), route_0)
-    other_core = lax.ppermute(encoded[1], ("x", "k", "l", "c"), route_1)
+    same_core = lax.ppermute(encoded[0], ("w", "x", "k", "l", "c"), route_0)
+    other_core = lax.ppermute(encoded[1], ("w", "x", "k", "l", "c"), route_1)
     first_frame = jnp.where(c == 0, same_core, other_core)
     second_frame = jnp.where(c == 0, other_core, same_core)
     return jnp.stack([first_frame, second_frame]).reshape(video.shape)

time: 164 us -> 158 us (0.963)
  the two profiles are of different devices: /device:TPU:50 before, /device:TPU:48 now
where the time goes in v3:
time: 158 us; the launch traced here: 157 us
  blocking collectives  54.5 us (34%)
  waiting for transfers between devices  54 us (34%)
  starting transfers between devices  29.9 us (19%)
  Pallas kernels  16.7 us (11%)
    all_to_all x1, blocking collectives, body(): parts = lax.all_to_all(parts.reshape(SPACE, 16, 128), space, 0, 0)  36.4 us
    all_to_all x1, blocking collectives, body(): mine = lax.all_to_all(frame, ('w', 'x'), 0, 0)  18.1 us
    pallas_call x7, Pallas kernels, call(): pl.pallas_call(kernel, out_shape=out_shape, in_specs=[pl.BlockSpec(memory...  16.7 us
    ppermute x1, waiting for transfers between devices, body(): other_core = lax.ppermute(encoded[1], ('w', 'x', 'k', 'l', 'c'), route_1)  16.1 us
    ppermute x1, waiting for transfers between devices, body(): partner_2 = lax.ppermute(weight_2, ('h', 'w'), mirror)  11.1 us
    ppermute x1, waiting for transfers between devices, body(): partner_1 = lax.ppermute(weight_1, ('h', 'w'), mirror)  10 us
    all_to_all x1, starting transfers between devices, body(): second = lax.all_to_all(second, ('w', 'x'), 0, 0)  5.79 us
    all_to_all x1, starting transfers between devices, body(): gathered = lax.all_to_all(spread, ('w', 'x'), 0, 0)  5.16 us
  transfers between devices with their start and end apart: 10, of which 9 were waited for; matrix products, arithmetic and copies ran while one was open for 0% of the time, Pallas kernels for 0%

profile of v3, /device:TPU:48, one launch (start us, length us, event | category | flops | bytes accessed | tf_op | source)
XLA Modules:
  0.0 157.3 jit_solution(3117749677917703817)
XLA Ops:
  0.0 0.9 copy-done.5
  0.9 1.2 shard_map.100
  2.1 0.0 copy-start.8
  2.1 5.2 %all-to-all-start = ((f32[8,256,128]{2,1,0:T(8,128)}), f32[8,256,128]{2,1,0:T(8,128)S(1)}, u32[]{:S(2)}, u32[]{:S(2)}) async-start(f32[8,256,128]{2,1,0:T(8,128)} %shard_map.100), calls=%async_computation | async-start | bytes 2097152 | tf_op jit(solution)/shard_map/all_to_all | solution.py:314
  7.3 0.0 copy-done.1
  7.3 3.1 %collective-permute-start = (f32[432,256]{1,0:T(8,128)S(1)}, f32[432,256]{1,0:T(8,128)S(1)}, u32[]{:S(2)}, u32[]{:S(2)}) collective-permute-start(f32[432,256]{1,0:T(8,128)S(1)} %bitcast.26), channel_id=1, source_target_pairs={{0,384},{128,256},{256,128},{384,0},{1,385},{129,257},{257,129},{3... | collective-permute-start | bytes 1327112 | tf_op jit(solution)/shard_map/ppermute | solution.py:308
  10.4 0.0 copy-done.9
  10.4 0.1 compare_bitcast_fusion.1
  10.5 0.1 broadcast_in_dim.4
  10.6 0.1 reshape_reshape.3
  10.7 0.1 stack.57.place_ref
  10.8 0.0 copy-done.6
  10.8 0.0 copy-done.7
  10.8 0.0 copy-done.8
  10.8 10.0 %collective-permute-done.partner_ref = f32[432,256]{1,0:T(8,128)S(1)} collective-permute-done((f32[432,256]{1,0:T(8,128)S(1)}, f32[432,256]{1,0:T(8,128)S(1)}, u32[]{:S(2)}, u32[]{:S(2)}) %collective-permute-start) | collective-permute-done | bytes 442400 | tf_op jit(solution)/shard_map/ppermute | solution.py:308
  20.8 2.2 %all-to-all-done = f32[8,256,128]{2,1,0:T(8,128)S(1)} async-done(((f32[8,256,128]{2,1,0:T(8,128)}), f32[8,256,128]{2,1,0:T(8,128)S(1)}, u32[]{:S(2)}, u32[]{:S(2)}) %all-to-all-start) | async-done | bytes 1048608 | tf_op jit(solution)/shard_map/all_to_all | solution.py:314
  23.0 4.3 %shard_map.101 = (f32[9,2,16,128]{3,2,1,0:T(8,128)S(1)}, f32[9,16,128]{2,1,0:T(8,128)S(1)}, f32[9,16,128]{2,1,0:T(8,128)S(1)}, f32[8,2,16,128]{3,2,1,0:T(8,128)S(1)}) custom-call(s32[6]{0:T(128)S(1)} %stack.57.place_ref, f32[8,4,4,16,128]{4,3,2,1,0:T(8,128)S(1)} %bitcast.24, f32[432,256]{1,0:T(8,128)S(1)} %bitcast.27, ...), custom_call_target="tpu_custom_call" | custom-call | tf_op jit(solution)/shard_map/pallas_call | solution.py:24
  27.2 1.9 %collective-permute-start.1 = (f32[9,16,128]{2,1,0:T(8,128)S(1)}, f32[9,16,128]{2,1,0:T(8,128)S(1)}, u32[]{:S(2)}, u32[]{:S(2)}) collective-permute-start(f32[9,16,128]{2,1,0:T(8,128)S(1)} %get-tuple-element.12), channel_id=1, source_target_pairs={{0,1},{1,0},{2,3},{3,2},{4,5},{5,4},{6,7},{7,6},{8,9},{9,8},{10,11... | collective-permute-start | bytes 221192 | tf_op jit(solution)/shard_map/ppermute | solution.py:330
  29.2 2.1 %collective-permute-start.2 = (f32[9,16,128]{2,1,0:T(8,128)S(1)}, f32[9,16,128]{2,1,0:T(8,128)S(1)}, u32[]{:S(2)}, u32[]{:S(2)}) collective-permute-start(f32[9,16,128]{2,1,0:T(8,128)S(1)} %get-tuple-element.13), channel_id=1, source_target_pairs={{1,2},{3,4},{5,6},{7,8},{9,10},{11,12},{13,14},{15,16},{17,18},{19... | collective-permute-start | bytes 221192 | tf_op jit(solution)/shard_map/ppermute | solution.py:329
  31.3 0.0 collective-permute-done.1.beside_ref
  31.3 3.5 %collective-permute-done.2.beyond_ref = f32[9,16,128]{2,1,0:T(8,128)S(1)} collective-permute-done((f32[9,16,128]{2,1,0:T(8,128)S(1)}, f32[9,16,128]{2,1,0:T(8,128)S(1)}, u32[]{:S(2)}, u32[]{:S(2)}) %collective-permute-start.2) | collective-permute-done | bytes 73760 | tf_op jit(solution)/shard_map/ppermute | solution.py:329
  34.8 0.6 shard_map.102
  35.5 1.3 collective-permute-start.3
  36.8 4.5 %collective-permute-done.3.history_ref = f32[2,2,16,128]{3,2,1,0:T(8,128)S(1)} collective-permute-done((f32[2,2,16,128]{3,2,1,0:T(8,128)S(1)}, f32[2,2,16,128]{3,2,1,0:T(8,128)S(1)}, u32[]{:S(2)}, u32[]{:S(2)}) %collective-permute-start.3) | collective-permute-done | bytes 32800 | tf_op jit(solution)/shard_map/ppermute | solution.py:341
  41.3 1.1 shard_map.103
  42.4 5.8 %all-to-all-start.1 = ((f32[8,9,2,16,128]{4,3,2,1,0:T(8,128)}), f32[8,9,2,16,128]{4,3,2,1,0:T(8,128)S(1)}, u32[]{:S(2)}, u32[]{:S(2)}) async-start(f32[8,9,2,16,128]{4,3,2,1,0:T(8,128)} %shard_map.103), calls=%async_computation.1 | async-start | bytes 2359296 | tf_op jit(solution)/shard_map/all_to_all | solution.py:343
  48.2 0.0 copy-done.2
  48.2 1.9 %collective-permute-start.4 = (f32[432,256]{1,0:T(8,128)S(1)}, f32[432,256]{1,0:T(8,128)S(1)}, u32[]{:S(2)}, u32[]{:S(2)}) collective-permute-start(f32[432,256]{1,0:T(8,128)S(1)} %bitcast.28), channel_id=1, source_target_pairs={{0,384},{128,256},{256,128},{384,0},{1,385},{129,257},{257,129},{3... | collective-permute-start | bytes 1327112 | tf_op jit(solution)/shard_map/ppermute | solution.py:309
  50.2 11.1 %collective-permute-done.4.partner_ref = f32[432,256]{1,0:T(8,128)S(1)} collective-permute-done((f32[432,256]{1,0:T(8,128)S(1)}, f32[432,256]{1,0:T(8,128)S(1)}, u32[]{:S(2)}, u32[]{:S(2)}) %collective-permute-start.4) | collective-permute-done | bytes 442400 | tf_op jit(solution)/shard_map/ppermute | solution.py:309
  61.3 3.6 %all-to-all-done.1.second_ref = f32[8,9,2,16,128]{4,3,2,1,0:T(8,128)S(1)} async-done(((f32[8,9,2,16,128]{4,3,2,1,0:T(8,128)}), f32[8,9,2,16,128]{4,3,2,1,0:T(8,128)S(1)}, u32[]{:S(2)}, u32[]{:S(2)}) %all-to-all-start.1) | async-done | bytes 1179680 | tf_op jit(solution)/shard_map/all_to_all | solution.py:343
  64.9 3.3 %shard_map.104 = f32[16,2,16,128]{3,2,1,0:T(8,128)S(1)} custom-call(s32[6]{0:T(128)S(1)} %stack.57.place_ref, f32[8,9,2,16,128]{4,3,2,1,0:T(8,128)S(1)} %all-to-all-done.1.second_ref, f32[432,256]{1,0:T(8,128)S(1)} %bitcast.29, f32[432,256]{1,0:T(8,128)S(1)} %collective-permute-done.4.partner_ref, f32[3,256]{1,0:T(4,128)S(1)} %pad_maximum_fusion.1.gain_ref, ...), custom_call_target="tpu_custom_call" | custom-call | tf_op jit(solution)/shard_map/pallas_call | solution.py:24
  68.2 36.4 %all_to_all.20.parts_ref = f32[32,16,128]{2,1,0:T(8,128)S(1)} all-to-all(f32[32,16,128]{2,1,0:T(8,128)S(1)} %bitcast.25), channel_id=1, replica_groups=mesh['h'=2,'w'=2,'x'=4,'k'=8,'l'=2,'c'=2] {'k','l','c'}, dimensions={0} | all-to-all | bytes 524288 | tf_op jit(solution)/shard_map/all_to_all | solution.py:357
  104.6 0.5 shard_map.105
  105.1 0.0 copy-start
  105.1 0.0 copy-start.3
  105.1 0.0 copy-start.4
  105.1 18.1 %all_to_all.21.mine_ref = f32[8,16,16,128]{3,2,1,0:T(8,128)S(1)} all-to-all(f32[8,16,16,128]{3,2,1,0:T(8,128)S(1)} %shard_map.105), channel_id=1, replica_groups=mesh['h'=2,'w'=2,'x'=4,'k'=8,'l'=2,'c'=2] {'w','x'}, dimensions={0} | all-to-all | bytes 2097152 | tf_op jit(solution)/shard_map/all_to_all | solution.py:359
  123.2 1.9 %collective-permute-start.5 = (f32[8,16,16,128]{3,2,1,0:T(8,128)S(1)}, f32[8,16,16,128]{3,2,1,0:T(8,128)S(1)}, u32[]{:S(2)}, u32[]{:S(2)}) collective-permute-start(f32[8,16,16,128]{3,2,1,0:T(8,128)S(1)} %all_to_all.21.mine_ref), channel_id=1, source_target_pairs={{0,1},{1,0},{2,3},{3,2},{4,5},{5,4},{6,7},{7,6},{8,9},{9,8},{10,11... | collective-permute-start | bytes 3145736 | tf_op jit(solution)/shard_map/ppermute | solution.py:360
  125.1 2.6 %collective-permute-done.5.other_ref = f32[8,16,16,128]{3,2,1,0:T(8,128)S(1)} collective-permute-done((f32[8,16,16,128]{3,2,1,0:T(8,128)S(1)}, f32[8,16,16,128]{3,2,1,0:T(8,128)S(1)}, u32[]{:S(2)}, u32[]{:S(2)}) %collective-permute-start.5) | collective-permute-done | bytes 1048608 | tf_op jit(solution)/shard_map/ppermute | solution.py:360
  127.8 0.0 copy-done
  127.8 0.0 copy-done.3
  127.8 0.0 copy-done.4
  127.8 5.7 %shard_map.106 = f32[2,64,256]{2,1,0:T(8,128)S(1)} custom-call(s32[6]{0:T(128)S(1)} %stack.57.place_ref, f32[8,16,16,128]{3,2,1,0:T(8,128)S(1)} %all_to_all.21.mine_ref, f32[8,16,16,128]{3,2,1,0:T(8,128)S(1)} %collective-permute-done.5.other_ref, f32[3,256]{1,0:T(4,128)S(1)} %pad_maximum_fusion.1.gain_ref, f32[2,256,256]{2,1,0:T(8,128)S(1)} %copy-done, ...), custom_call_target="tpu_custom_call" | custom-call | tf_op jit(solution)/shard_map/pallas_call | solution.py:24
  133.4 2.8 %collective-permute-start.6 = (f32[64,256]{1,0:T(8,128)S(1)}, f32[64,256]{1,0:T(8,128)S(1)}, u32[]{:S(2)}, u32[]{:S(2)}) collective-permute-start(f32[64,256]{1,0:T(8,128)S(1)} %get-tuple-element.19), channel_id=1, source_target_pairs={{0,0},{1,16},{2,34},{3,50},{4,68},{5,84},{6,102},{7,118},{8,136},{... | collective-permute-start | bytes 196616 | tf_op jit(solution)/shard_map/ppermute | solution.py:380
  136.2 3.9 %collective-permute-start.7 = (f32[64,256]{1,0:T(8,128)S(1)}, f32[64,256]{1,0:T(8,128)S(1)}, u32[]{:S(2)}, u32[]{:S(2)}) collective-permute-start(f32[64,256]{1,0:T(8,128)S(1)} %get-tuple-element.20), channel_id=1, source_target_pairs={{0,1},{1,17},{2,35},{3,51},{4,69},{5,85},{6,103},{7,119},{8,137},{... | collective-permute-start | bytes 196616 | tf_op jit(solution)/shard_map/ppermute | solution.py:381
  140.2 0.4 collective-permute-done.6
  140.5 16.1 %collective-permute-done.7 = f32[64,256]{1,0:T(8,128)S(1)} collective-permute-done((f32[64,256]{1,0:T(8,128)S(1)}, f32[64,256]{1,0:T(8,128)S(1)}, u32[]{:S(2)}, u32[]{:S(2)}) %collective-permute-start.7) | collective-permute-done | bytes 65568 | tf_op jit(solution)/shard_map/ppermute | solution.py:381
  156.6 0.7 pad_maximum_fusion
  (11 shorter events, 0.1 us)
Async XLA Ops:
  0.0 0.9 copy-start.5
  2.1 5.2 %copy-start.1 = (f32[3,3,3,16,256]{4,3,2,1,0:T(8,128)S(1)}, f32[3,3,3,16,256]{4,3,2,1,0:T(8,128)}, u32[]{:S(2)}) copy-start(f32[3,3,3,16,256]{4,3,2,1,0:T(8,128)} %param.13) | copy-start | bytes 1327108
  2.1 8.3 %copy-start.9 = (s32[32]{0:T(128)S(1)}, s32[32]{0:T(128)}, u32[]{:S(2)}) copy-start(s32[32]{0:T(128)} %param.11) | copy-start | bytes 388
  2.1 8.7 %copy-start.6 = (f32[256]{0:T(256)S(1)}, f32[256]{0:T(256)}, u32[]{:S(2)}) copy-start(f32[256]{0:T(256)} %param.16) | copy-start | bytes 3076
  2.1 8.7 %copy-start.7 = (f32[256]{0:T(256)S(1)}, f32[256]{0:T(256)}, u32[]{:S(2)}) copy-start(f32[256]{0:T(256)} %param.14) | copy-start | bytes 3076
  2.1 8.7 %copy-start.8 = (f32[256]{0:T(256)S(1)}, f32[256]{0:T(256)}, u32[]{:S(2)}) copy-start(f32[256]{0:T(256)} %param.12) | copy-start | bytes 3076
  2.1 20.9 %all-to-all-start = ((f32[8,256,128]{2,1,0:T(8,128)}), f32[8,256,128]{2,1,0:T(8,128)S(1)}, u32[]{:S(2)}, u32[]{:S(2)}) async-start(f32[8,256,128]{2,1,0:T(8,128)} %shard_map.100), calls=%async_computation | async-start | bytes 2097152 | tf_op jit(solution)/shard_map/all_to_all | solution.py:314
  7.3 13.5 %collective-permute-start = (f32[432,256]{1,0:T(8,128)S(1)}, f32[432,256]{1,0:T(8,128)S(1)}, u32[]{:S(2)}, u32[]{:S(2)}) collective-permute-start(f32[432,256]{1,0:T(8,128)S(1)} %bitcast.26), channel_id=1, source_target_pairs={{0,384},{128,256},{256,128},{384,0},{1,385},{129,257},{257,129},{3... | collective-permute-start | bytes 1327112 | tf_op jit(solution)/shard_map/ppermute | solution.py:308
  27.2 4.1 %collective-permute-start.1 = (f32[9,16,128]{2,1,0:T(8,128)S(1)}, f32[9,16,128]{2,1,0:T(8,128)S(1)}, u32[]{:S(2)}, u32[]{:S(2)}) collective-permute-start(f32[9,16,128]{2,1,0:T(8,128)S(1)} %get-tuple-element.12), channel_id=1, source_target_pairs={{0,1},{1,0},{2,3},{3,2},{4,5},{5,4},{6,7},{7,6},{8,9},{9,8},{10,11... | collective-permute-start | bytes 221192 | tf_op jit(solution)/shard_map/ppermute | solution.py:330
  29.2 5.7 %collective-permute-start.2 = (f32[9,16,128]{2,1,0:T(8,128)S(1)}, f32[9,16,128]{2,1,0:T(8,128)S(1)}, u32[]{:S(2)}, u32[]{:S(2)}) collective-permute-start(f32[9,16,128]{2,1,0:T(8,128)S(1)} %get-tuple-element.13), channel_id=1, source_target_pairs={{1,2},{3,4},{5,6},{7,8},{9,10},{11,12},{13,14},{15,16},{17,18},{19... | collective-permute-start | bytes 221192 | tf_op jit(solution)/shard_map/ppermute | solution.py:329
  35.5 5.8 %collective-permute-start.3 = (f32[2,2,16,128]{3,2,1,0:T(8,128)S(1)}, f32[2,2,16,128]{3,2,1,0:T(8,128)S(1)}, u32[]{:S(2)}, u32[]{:S(2)}) collective-permute-start(f32[2,2,16,128]{3,2,1,0:T(8,128)S(1)} %get-tuple-element.15), channel_id=1, source_target_pairs={{0,384},{128,256},{1,385},{129,257},{2,386},{130,258},{3,387},{131... | collective-permute-start | bytes 98312 | tf_op jit(solution)/shard_map/ppermute | solution.py:341
  42.4 5.8 %copy-start.2 = (f32[3,3,3,16,256]{4,3,2,1,0:T(8,128)S(1)}, f32[3,3,3,16,256]{4,3,2,1,0:T(8,128)}, u32[]{:S(2)}) copy-start(f32[3,3,3,16,256]{4,3,2,1,0:T(8,128)} %param.15) | copy-start | bytes 1327108
  42.4 22.4 %all-to-all-start.1 = ((f32[8,9,2,16,128]{4,3,2,1,0:T(8,128)}), f32[8,9,2,16,128]{4,3,2,1,0:T(8,128)S(1)}, u32[]{:S(2)}, u32[]{:S(2)}) async-start(f32[8,9,2,16,128]{4,3,2,1,0:T(8,128)} %shard_map.103), calls=%async_computation.1 | async-start | bytes 2359296 | tf_op jit(solution)/shard_map/all_to_all | solution.py:343
  48.2 13.0 %collective-permute-start.4 = (f32[432,256]{1,0:T(8,128)S(1)}, f32[432,256]{1,0:T(8,128)S(1)}, u32[]{:S(2)}, u32[]{:S(2)}) collective-permute-start(f32[432,256]{1,0:T(8,128)S(1)} %bitcast.28), channel_id=1, source_target_pairs={{0,384},{128,256},{256,128},{384,0},{1,385},{129,257},{257,129},{3... | collective-permute-start | bytes 1327112 | tf_op jit(solution)/shard_map/ppermute | solution.py:309
  105.1 22.7 %copy-start = (f32[2,256,256]{2,1,0:T(8,128)S(1)}, f32[2,256,256]{2,1,0:T(8,128)}, u32[]{:S(2)}) copy-start(f32[2,256,256]{2,1,0:T(8,128)} %qk_ref.1) | copy-start | bytes 1572868
  105.1 22.7 %copy-start.3 = (f32[256,256]{1,0:T(8,128)S(1)}, f32[256,256]{1,0:T(8,128)}, u32[]{:S(2)}) copy-start(f32[256,256]{1,0:T(8,128)} %value_ref.1) | copy-start | bytes 786436
  105.1 22.7 %copy-start.4 = (f32[256,256]{1,0:T(8,128)S(1)}, f32[256,256]{1,0:T(8,128)}, u32[]{:S(2)}) copy-start(f32[256,256]{1,0:T(8,128)} %proj_ref.1) | copy-start | bytes 786436
  123.2 4.5 %collective-permute-start.5 = (f32[8,16,16,128]{3,2,1,0:T(8,128)S(1)}, f32[8,16,16,128]{3,2,1,0:T(8,128)S(1)}, u32[]{:S(2)}, u32[]{:S(2)}) collective-permute-start(f32[8,16,16,128]{3,2,1,0:T(8,128)S(1)} %all_to_all.21.mine_ref), channel_id=1, source_target_pairs={{0,1},{1,0},{2,3},{3,2},{4,5},{5,4},{6,7},{7,6},{8,9},{9,8},{10,11... | collective-permute-start | bytes 3145736 | tf_op jit(solution)/shard_map/ppermute | solution.py:360
  133.4 7.1 %collective-permute-start.6 = (f32[64,256]{1,0:T(8,128)S(1)}, f32[64,256]{1,0:T(8,128)S(1)}, u32[]{:S(2)}, u32[]{:S(2)}) collective-permute-start(f32[64,256]{1,0:T(8,128)S(1)} %get-tuple-element.19), channel_id=1, source_target_pairs={{0,0},{1,16},{2,34},{3,50},{4,68},{5,84},{6,102},{7,118},{8,136},{... | collective-permute-start | bytes 196616 | tf_op jit(solution)/shard_map/ppermute | solution.py:380
  136.2 20.4 %collective-permute-start.7 = (f32[64,256]{1,0:T(8,128)S(1)}, f32[64,256]{1,0:T(8,128)S(1)}, u32[]{:S(2)}, u32[]{:S(2)}) collective-permute-start(f32[64,256]{1,0:T(8,128)S(1)} %get-tuple-element.20), channel_id=1, source_target_pairs={{0,1},{1,17},{2,35},{3,51},{4,69},{5,85},{6,103},{7,119},{8,137},{... | collective-permute-start | bytes 196616 | tf_op jit(solution)/shard_map/ppermute | solution.py:381

commit v4 on v3

--- a/solution.py
+++ b/solution.py
@@ -139,8 +139,10 @@
         return before
 
     zeros = [[jnp.zeros((32, 128), f32)] * 3] * 2
-    last = lax.fori_loop(0, 4, step, zeros)
-    finish(8, zeros, last)
+    last = zeros
+    for p in range(TILES // 2):
+        last = step(p, last)
+    finish(TILES, zeros, last)
 
 
 def join1_kernel(place_ref, own_ref, beside_ref, beyond_ref, out_ref, history_ref):
@@ -225,9 +227,19 @@
             out_ref[i, p] = tile
 
 
+def fold_kernel(qk_ref, value_ref, proj_ref, out_ref):
+    scores = lax.dot_general(
+        qk_ref[0], qk_ref[1], (((1,), (1,)), ((), ())), precision=highest, preferred_element_type=f32
+    )
+    out_ref[0] = scores * (1.0 / math.sqrt(256))
+    out_ref[1] = jnp.dot(
+        value_ref[...], proj_ref[...], precision=highest, preferred_element_type=f32
+    )
+
+
 def attend_kernel(
-    place_ref, mine_ref, other_ref, gain_ref, qk_ref, value_ref, proj_ref, out_ref,
-    blocked_ref, normed_ref, high_ref, low_ref,
+    place_ref, mine_ref, other_ref, gain_ref, folded_ref, same_ref, cross_ref,
+    blocked_ref, high_ref, low_ref,
 ):
     gain = column(gain_ref[2:3])
     half, core = place_ref[0], place_ref[3]
@@ -242,28 +254,21 @@
         tile = jnp.concatenate(blocks, axis=0)
         blocked_ref[p] = tile
         normed = tile * lax.rsqrt(jnp.mean(tile * tile, axis=0, keepdims=True) + epsilon) * gain
-        normed_ref[:, 128 * p : 128 * p + 128] = normed
         high, low = split(normed)
         high_ref[:, 128 * p : 128 * p + 128] = high
         low_ref[:, 128 * p : 128 * p + 128] = low
     at = place_ref[4]
     rows = blocked_ref[at].T
-    normed_rows = rows * lax.rsqrt(jnp.mean(rows * rows, axis=1, keepdims=True) + epsilon) * gain_ref[2:3]
-    queries = jnp.dot(normed_rows, qk_ref[0], precision=highest, preferred_element_type=f32)
-    queries = lax.dot_general(
-        queries, qk_ref[1], (((1,), (1,)), ((), ())), precision=highest, preferred_element_type=f32
-    ) * (1.0 / math.sqrt(256))
-    scores = jnp.dot(queries, normed_ref[...], precision=highest, preferred_element_type=f32)
+    normed = rows * lax.rsqrt(jnp.mean(rows * rows, axis=1, keepdims=True) + epsilon) * gain_ref[2:3]
+    queries = dot3(*split(normed), *split(folded_ref[0]))
+    scores = dot3(*split(queries), high_ref[...], low_ref[...])
     weights = jnp.exp(scores - jnp.max(scores, axis=1, keepdims=True))
     total = jnp.sum(weights, axis=1, keepdims=True)
-    e_high, e_low = split(weights)
-    attended = dot3(e_high, e_low, high_ref[...], low_ref[...], ((1,), (1,))) / total
-    attended = jnp.dot(attended, value_ref[...], precision=highest, preferred_element_type=f32)
-    attended = jnp.dot(attended, proj_ref[...], precision=highest, preferred_element_type=f32)
-    result = rows + attended
-    swapped = place_ref[5]
-    out_ref[swapped] = result[:64]
-    out_ref[1 - swapped] = result[64:]
+    attended = dot3(*split(weights), high_ref[...], low_ref[...], ((1,), (1,))) / total
+    result = rows + dot3(*split(attended), *split(folded_ref[1]))
+    first_core = place_ref[5] == 0
+    same_ref[...] = jnp.where(first_core, result[:64], result[64:])
+    cross_ref[...] = jnp.where(first_core, result[64:], result[:64])
 
 
 def delivery():
@@ -310,6 +315,7 @@
     swap = [(0, 1), (1, 0)]
     gains = jnp.stack([norm1_gain, norm2_gain, norm3_gain])
 
+    folded = call(fold_kernel, shape(2, 256, 256), [], qk_weight, value_weight, proj_weight)
     spread = call(spread_kernel, shape(W * X, 256, 128), [], video.reshape(128, 256))
     gathered = lax.all_to_all(spread, ("w", "x"), 0, 0)
     weights_scratch = [pltpu.VMEM((2, 432, 256), bf16)] * 2
@@ -358,12 +364,11 @@
     frame = call(join2_kernel, shape(W * X, 16, 16, 128), [], parts)
     mine = lax.all_to_all(frame, ("w", "x"), 0, 0)
     other = lax.ppermute(mine, "c", swap)
-    encoded = call(
+    same_core, other_core = call(
         attend_kernel,
-        shape(2, 64, 256),
+        [shape(64, 256), shape(64, 256)],
         [
             pltpu.VMEM((16, 256, 128), f32),
-            pltpu.VMEM((256, 2048), f32),
             pltpu.VMEM((256, 2048), bf16),
             pltpu.VMEM((256, 2048), bf16),
         ],
@@ -371,14 +376,12 @@
         mine,
         other,
         gains,
-        qk_weight,
-        value_weight,
-        proj_weight,
+        folded,
         smem=1,
     )
     route_0, route_1 = delivery()
-    same_core = lax.ppermute(encoded[0], ("w", "x", "k", "l", "c"), route_0)
-    other_core = lax.ppermute(encoded[1], ("w", "x", "k", "l", "c"), route_1)
+    same_core = lax.ppermute(same_core, ("w", "x", "k", "l", "c"), route_0)
+    other_core = lax.ppermute(other_core, ("w", "x", "k", "l", "c"), route_1)
     first_frame = jnp.where(c == 0, same_core, other_core)
     second_frame = jnp.where(c == 0, other_core, same_core)
     return jnp.stack([first_frame, second_frame]).reshape(video.shape)

time: 158 us -> 154 us (0.975)
  Pallas kernels: 16.7 us -> 13.8 us
    pallas_call x7 -> x8, Pallas kernels: 16.7 us -> 13.8 us  [call(): pl.pallas_call(kernel, out_shape=out_shape, in_specs=[pl.BlockSpec(memory...]
where the time goes in v4:
time: 154 us
  blocking collectives  54.5 us (35%)
  waiting for transfers between devices  53.3 us (35%)
  starting transfers between devices  29.9 us (19%)
  Pallas kernels  13.8 us (9%)
    all_to_all x1, blocking collectives, body(): parts = lax.all_to_all(parts.reshape(SPACE, 16, 128), space, 0, 0)  36.4 us
    all_to_all x1, blocking collectives, body(): mine = lax.all_to_all(frame, ('w', 'x'), 0, 0)  18.1 us
    ppermute x1, waiting for transfers between devices, body(): other_core = lax.ppermute(other_core, ('w', 'x', 'k', 'l', 'c'), route_1)  16.1 us
    pallas_call x8, Pallas kernels, call(): pl.pallas_call(kernel, out_shape=out_shape, in_specs=[pl.BlockSpec(memory...  13.8 us
    ppermute x1, waiting for transfers between devices, body(): partner_2 = lax.ppermute(weight_2, ('h', 'w'), mirror)  11.1 us
    ppermute x1, waiting for transfers between devices, body(): partner_1 = lax.ppermute(weight_1, ('h', 'w'), mirror)  10 us
    all_to_all x1, starting transfers between devices, body(): second = lax.all_to_all(second, ('w', 'x'), 0, 0)  5.79 us
    all_to_all x1, starting transfers between devices, body(): gathered = lax.all_to_all(spread, ('w', 'x'), 0, 0)  5.16 us
  transfers between devices with their start and end apart: 10, of which 9 were waited for; matrix products, arithmetic and copies ran while one was open for 0% of the time, Pallas kernels for 0%

profile of v4, /device:TPU:48, one launch (start us, length us, event | category | flops | bytes accessed | tf_op | source)
XLA Modules:
  0.0 153.7 jit_solution(6336555414635163306)
XLA Ops:
  0.0 0.9 copy-done.5
  0.9 1.2 shard_map.100
  2.1 0.0 copy-start.8
  2.1 5.2 %all-to-all-start = ((f32[8,256,128]{2,1,0:T(8,128)}), f32[8,256,128]{2,1,0:T(8,128)S(1)}, u32[]{:S(2)}, u32[]{:S(2)}) async-start(f32[8,256,128]{2,1,0:T(8,128)} %shard_map.100), calls=%async_computation | async-start | bytes 2097152 | tf_op jit(solution)/shard_map/all_to_all | solution.py:320
  7.3 0.0 copy-done.1
  7.3 3.1 %collective-permute-start = (f32[432,256]{1,0:T(8,128)S(1)}, f32[432,256]{1,0:T(8,128)S(1)}, u32[]{:S(2)}, u32[]{:S(2)}) collective-permute-start(f32[432,256]{1,0:T(8,128)S(1)} %bitcast.22), channel_id=1, source_target_pairs={{0,384},{128,256},{256,128},{384,0},{1,385},{129,257},{257,129},{3... | collective-permute-start | bytes 1327112 | tf_op jit(solution)/shard_map/ppermute | solution.py:313
  10.4 0.0 copy-done.9
  10.4 0.1 compare_bitcast_fusion.1
  10.5 0.1 broadcast_in_dim.4
  10.6 0.1 reshape_reshape.3
  10.7 0.1 stack.57.place_ref
  10.8 0.0 copy-done.6
  10.8 0.0 copy-done.7
  10.8 0.0 copy-done.8
  10.8 10.0 %collective-permute-done.partner_ref = f32[432,256]{1,0:T(8,128)S(1)} collective-permute-done((f32[432,256]{1,0:T(8,128)S(1)}, f32[432,256]{1,0:T(8,128)S(1)}, u32[]{:S(2)}, u32[]{:S(2)}) %collective-permute-start) | collective-permute-done | bytes 442400 | tf_op jit(solution)/shard_map/ppermute | solution.py:313
  20.8 2.2 %all-to-all-done = f32[8,256,128]{2,1,0:T(8,128)S(1)} async-done(((f32[8,256,128]{2,1,0:T(8,128)}), f32[8,256,128]{2,1,0:T(8,128)S(1)}, u32[]{:S(2)}, u32[]{:S(2)}) %all-to-all-start) | async-done | bytes 1048608 | tf_op jit(solution)/shard_map/all_to_all | solution.py:320
  23.0 2.5 %shard_map.101 = (f32[9,2,16,128]{3,2,1,0:T(8,128)S(1)}, f32[9,16,128]{2,1,0:T(8,128)S(1)}, f32[9,16,128]{2,1,0:T(8,128)S(1)}, f32[8,2,16,128]{3,2,1,0:T(8,128)S(1)}) custom-call(s32[6]{0:T(128)S(1)} %stack.57.place_ref, f32[8,4,4,16,128]{4,3,2,1,0:T(8,128)S(1)} %bitcast.20, f32[432,256]{1,0:T(8,128)S(1)} %bitcast.23, ...), custom_call_target="tpu_custom_call" | custom-call | tf_op jit(solution)/shard_map/pallas_call | solution.py:24
  25.4 1.9 %collective-permute-start.1 = (f32[9,16,128]{2,1,0:T(8,128)S(1)}, f32[9,16,128]{2,1,0:T(8,128)S(1)}, u32[]{:S(2)}, u32[]{:S(2)}) collective-permute-start(f32[9,16,128]{2,1,0:T(8,128)S(1)} %get-tuple-element.14), channel_id=1, source_target_pairs={{0,1},{1,0},{2,3},{3,2},{4,5},{5,4},{6,7},{7,6},{8,9},{9,8},{10,11... | collective-permute-start | bytes 221192 | tf_op jit(solution)/shard_map/ppermute | solution.py:336
  27.4 2.1 %collective-permute-start.2 = (f32[9,16,128]{2,1,0:T(8,128)S(1)}, f32[9,16,128]{2,1,0:T(8,128)S(1)}, u32[]{:S(2)}, u32[]{:S(2)}) collective-permute-start(f32[9,16,128]{2,1,0:T(8,128)S(1)} %get-tuple-element.15), channel_id=1, source_target_pairs={{1,2},{3,4},{5,6},{7,8},{9,10},{11,12},{13,14},{15,16},{17,18},{19... | collective-permute-start | bytes 221192 | tf_op jit(solution)/shard_map/ppermute | solution.py:335
  29.5 0.0 collective-permute-done.1.beside_ref
  29.5 3.5 %collective-permute-done.2.beyond_ref = f32[9,16,128]{2,1,0:T(8,128)S(1)} collective-permute-done((f32[9,16,128]{2,1,0:T(8,128)S(1)}, f32[9,16,128]{2,1,0:T(8,128)S(1)}, u32[]{:S(2)}, u32[]{:S(2)}) %collective-permute-start.2) | collective-permute-done | bytes 73760 | tf_op jit(solution)/shard_map/ppermute | solution.py:335
  33.0 0.6 shard_map.102
  33.7 1.3 collective-permute-start.3
  35.0 4.5 %collective-permute-done.3.history_ref = f32[2,2,16,128]{3,2,1,0:T(8,128)S(1)} collective-permute-done((f32[2,2,16,128]{3,2,1,0:T(8,128)S(1)}, f32[2,2,16,128]{3,2,1,0:T(8,128)S(1)}, u32[]{:S(2)}, u32[]{:S(2)}) %collective-permute-start.3) | collective-permute-done | bytes 32800 | tf_op jit(solution)/shard_map/ppermute | solution.py:347
  39.5 1.1 shard_map.103
  40.6 5.8 %all-to-all-start.1 = ((f32[8,9,2,16,128]{4,3,2,1,0:T(8,128)}), f32[8,9,2,16,128]{4,3,2,1,0:T(8,128)S(1)}, u32[]{:S(2)}, u32[]{:S(2)}) async-start(f32[8,9,2,16,128]{4,3,2,1,0:T(8,128)} %shard_map.103), calls=%async_computation.1 | async-start | bytes 2359296 | tf_op jit(solution)/shard_map/all_to_all | solution.py:349
  46.4 0.0 copy-done.2
  46.4 1.9 %collective-permute-start.4 = (f32[432,256]{1,0:T(8,128)S(1)}, f32[432,256]{1,0:T(8,128)S(1)}, u32[]{:S(2)}, u32[]{:S(2)}) collective-permute-start(f32[432,256]{1,0:T(8,128)S(1)} %bitcast.24), channel_id=1, source_target_pairs={{0,384},{128,256},{256,128},{384,0},{1,385},{129,257},{257,129},{3... | collective-permute-start | bytes 1327112 | tf_op jit(solution)/shard_map/ppermute | solution.py:314
  48.4 11.1 %collective-permute-done.4.partner_ref = f32[432,256]{1,0:T(8,128)S(1)} collective-permute-done((f32[432,256]{1,0:T(8,128)S(1)}, f32[432,256]{1,0:T(8,128)S(1)}, u32[]{:S(2)}, u32[]{:S(2)}) %collective-permute-start.4) | collective-permute-done | bytes 442400 | tf_op jit(solution)/shard_map/ppermute | solution.py:314
  59.5 3.6 %all-to-all-done.1.second_ref = f32[8,9,2,16,128]{4,3,2,1,0:T(8,128)S(1)} async-done(((f32[8,9,2,16,128]{4,3,2,1,0:T(8,128)}), f32[8,9,2,16,128]{4,3,2,1,0:T(8,128)S(1)}, u32[]{:S(2)}, u32[]{:S(2)}) %all-to-all-start.1) | async-done | bytes 1179680 | tf_op jit(solution)/shard_map/all_to_all | solution.py:349
  63.1 3.3 %shard_map.104 = f32[16,2,16,128]{3,2,1,0:T(8,128)S(1)} custom-call(s32[6]{0:T(128)S(1)} %stack.57.place_ref, f32[8,9,2,16,128]{4,3,2,1,0:T(8,128)S(1)} %all-to-all-done.1.second_ref, f32[432,256]{1,0:T(8,128)S(1)} %bitcast.25, f32[432,256]{1,0:T(8,128)S(1)} %collective-permute-done.4.partner_ref, f32[3,256]{1,0:T(4,128)S(1)} %pad_maximum_fusion.1.gain_ref, ...), custom_call_target="tpu_custom_call" | custom-call | tf_op jit(solution)/shard_map/pallas_call | solution.py:24
  66.4 36.4 %all_to_all.20.parts_ref = f32[32,16,128]{2,1,0:T(8,128)S(1)} all-to-all(f32[32,16,128]{2,1,0:T(8,128)S(1)} %bitcast.21), channel_id=1, replica_groups=mesh['h'=2,'w'=2,'x'=4,'k'=8,'l'=2,'c'=2] {'k','l','c'}, dimensions={0} | all-to-all | bytes 524288 | tf_op jit(solution)/shard_map/all_to_all | solution.py:363
  102.8 0.5 shard_map.105
  103.3 0.0 copy-start
  103.3 0.0 copy-start.3
  103.3 0.0 copy-start.4
  103.3 18.1 %all_to_all.21.mine_ref = f32[8,16,16,128]{3,2,1,0:T(8,128)S(1)} all-to-all(f32[8,16,16,128]{3,2,1,0:T(8,128)S(1)} %shard_map.105), channel_id=1, replica_groups=mesh['h'=2,'w'=2,'x'=4,'k'=8,'l'=2,'c'=2] {'w','x'}, dimensions={0} | all-to-all | bytes 2097152 | tf_op jit(solution)/shard_map/all_to_all | solution.py:365
  121.4 1.9 %collective-permute-start.5 = (f32[8,16,16,128]{3,2,1,0:T(8,128)S(1)}, f32[8,16,16,128]{3,2,1,0:T(8,128)S(1)}, u32[]{:S(2)}, u32[]{:S(2)}) collective-permute-start(f32[8,16,16,128]{3,2,1,0:T(8,128)S(1)} %all_to_all.21.mine_ref), channel_id=1, source_target_pairs={{0,1},{1,0},{2,3},{3,2},{4,5},{5,4},{6,7},{7,6},{8,9},{9,8},{10,11... | collective-permute-start | bytes 3145736 | tf_op jit(solution)/shard_map/ppermute | solution.py:366
  123.3 0.0 copy-done
  123.3 0.0 copy-done.3
  123.4 0.7 shard_map.106.folded_ref
  124.0 1.9 %collective-permute-done.5.other_ref = f32[8,16,16,128]{3,2,1,0:T(8,128)S(1)} collective-permute-done((f32[8,16,16,128]{3,2,1,0:T(8,128)S(1)}, f32[8,16,16,128]{3,2,1,0:T(8,128)S(1)}, u32[]{:S(2)}, u32[]{:S(2)}) %collective-permute-start.5) | collective-permute-done | bytes 1048608 | tf_op jit(solution)/shard_map/ppermute | solution.py:366
  126.0 3.9 %shard_map.107 = (f32[64,256]{1,0:T(8,128)S(1)}, f32[64,256]{1,0:T(8,128)S(1)}) custom-call(s32[6]{0:T(128)S(1)} %stack.57.place_ref, f32[8,16,16,128]{3,2,1,0:T(8,128)S(1)} %all_to_all.21.mine_ref, f32[8,16,16,128]{3,2,1,0:T(8,128)S(1)} %collective-permute-done.5.other_ref, f32[3,256]{1,0:T(4,128)S(1)} %pad_maximum_fusion.1.gain_ref, ...), custom_call_target="tpu_custom_call" | custom-call | tf_op jit(solution)/shard_map/pallas_call | solution.py:24
  129.9 2.8 %collective-permute-start.6 = (f32[64,256]{1,0:T(8,128)S(1)}, f32[64,256]{1,0:T(8,128)S(1)}, u32[]{:S(2)}, u32[]{:S(2)}) collective-permute-start(f32[64,256]{1,0:T(8,128)S(1)} %get-tuple-element.19), channel_id=1, source_target_pairs={{0,0},{1,16},{2,34},{3,50},{4,68},{5,84},{6,102},{7,118},{8,136},{... | collective-permute-start | bytes 196616 | tf_op jit(solution)/shard_map/ppermute | solution.py:383
  132.7 3.9 %collective-permute-start.7 = (f32[64,256]{1,0:T(8,128)S(1)}, f32[64,256]{1,0:T(8,128)S(1)}, u32[]{:S(2)}, u32[]{:S(2)}) collective-permute-start(f32[64,256]{1,0:T(8,128)S(1)} %get-tuple-element.20), channel_id=1, source_target_pairs={{0,1},{1,17},{2,35},{3,51},{4,69},{5,85},{6,103},{7,119},{8,137},{... | collective-permute-start | bytes 196616 | tf_op jit(solution)/shard_map/ppermute | solution.py:384
  136.6 0.4 collective-permute-done.6
  136.9 16.1 %collective-permute-done.7 = f32[64,256]{1,0:T(8,128)S(1)} collective-permute-done((f32[64,256]{1,0:T(8,128)S(1)}, f32[64,256]{1,0:T(8,128)S(1)}, u32[]{:S(2)}, u32[]{:S(2)}) %collective-permute-start.7) | collective-permute-done | bytes 65568 | tf_op jit(solution)/shard_map/ppermute | solution.py:384
  153.0 0.7 pad_maximum_fusion
  (11 shorter events, 0.1 us)
Async XLA Ops:
  0.0 0.9 copy-start.5
  2.1 5.2 %copy-start.1 = (f32[3,3,3,16,256]{4,3,2,1,0:T(8,128)S(1)}, f32[3,3,3,16,256]{4,3,2,1,0:T(8,128)}, u32[]{:S(2)}) copy-start(f32[3,3,3,16,256]{4,3,2,1,0:T(8,128)} %param.13) | copy-start | bytes 1327108
  2.1 8.3 %copy-start.9 = (s32[32]{0:T(128)S(1)}, s32[32]{0:T(128)}, u32[]{:S(2)}) copy-start(s32[32]{0:T(128)} %param.11) | copy-start | bytes 388
  2.1 8.7 %copy-start.6 = (f32[256]{0:T(256)S(1)}, f32[256]{0:T(256)}, u32[]{:S(2)}) copy-start(f32[256]{0:T(256)} %param.16) | copy-start | bytes 3076
  2.1 8.7 %copy-start.7 = (f32[256]{0:T(256)S(1)}, f32[256]{0:T(256)}, u32[]{:S(2)}) copy-start(f32[256]{0:T(256)} %param.14) | copy-start | bytes 3076
  2.1 8.7 %copy-start.8 = (f32[256]{0:T(256)S(1)}, f32[256]{0:T(256)}, u32[]{:S(2)}) copy-start(f32[256]{0:T(256)} %param.12) | copy-start | bytes 3076
  2.1 20.9 %all-to-all-start = ((f32[8,256,128]{2,1,0:T(8,128)}), f32[8,256,128]{2,1,0:T(8,128)S(1)}, u32[]{:S(2)}, u32[]{:S(2)}) async-start(f32[8,256,128]{2,1,0:T(8,128)} %shard_map.100), calls=%async_computation | async-start | bytes 2097152 | tf_op jit(solution)/shard_map/all_to_all | solution.py:320
  7.3 13.5 %collective-permute-start = (f32[432,256]{1,0:T(8,128)S(1)}, f32[432,256]{1,0:T(8,128)S(1)}, u32[]{:S(2)}, u32[]{:S(2)}) collective-permute-start(f32[432,256]{1,0:T(8,128)S(1)} %bitcast.22), channel_id=1, source_target_pairs={{0,384},{128,256},{256,128},{384,0},{1,385},{129,257},{257,129},{3... | collective-permute-start | bytes 1327112 | tf_op jit(solution)/shard_map/ppermute | solution.py:313
  25.4 4.1 %collective-permute-start.1 = (f32[9,16,128]{2,1,0:T(8,128)S(1)}, f32[9,16,128]{2,1,0:T(8,128)S(1)}, u32[]{:S(2)}, u32[]{:S(2)}) collective-permute-start(f32[9,16,128]{2,1,0:T(8,128)S(1)} %get-tuple-element.14), channel_id=1, source_target_pairs={{0,1},{1,0},{2,3},{3,2},{4,5},{5,4},{6,7},{7,6},{8,9},{9,8},{10,11... | collective-permute-start | bytes 221192 | tf_op jit(solution)/shard_map/ppermute | solution.py:336
  27.4 5.7 %collective-permute-start.2 = (f32[9,16,128]{2,1,0:T(8,128)S(1)}, f32[9,16,128]{2,1,0:T(8,128)S(1)}, u32[]{:S(2)}, u32[]{:S(2)}) collective-permute-start(f32[9,16,128]{2,1,0:T(8,128)S(1)} %get-tuple-element.15), channel_id=1, source_target_pairs={{1,2},{3,4},{5,6},{7,8},{9,10},{11,12},{13,14},{15,16},{17,18},{19... | collective-permute-start | bytes 221192 | tf_op jit(solution)/shard_map/ppermute | solution.py:335
  33.7 5.8 %collective-permute-start.3 = (f32[2,2,16,128]{3,2,1,0:T(8,128)S(1)}, f32[2,2,16,128]{3,2,1,0:T(8,128)S(1)}, u32[]{:S(2)}, u32[]{:S(2)}) collective-permute-start(f32[2,2,16,128]{3,2,1,0:T(8,128)S(1)} %get-tuple-element.17), channel_id=1, source_target_pairs={{0,384},{128,256},{1,385},{129,257},{2,386},{130,258},{3,387},{131... | collective-permute-start | bytes 98312 | tf_op jit(solution)/shard_map/ppermute | solution.py:347
  40.6 5.8 %copy-start.2 = (f32[3,3,3,16,256]{4,3,2,1,0:T(8,128)S(1)}, f32[3,3,3,16,256]{4,3,2,1,0:T(8,128)}, u32[]{:S(2)}) copy-start(f32[3,3,3,16,256]{4,3,2,1,0:T(8,128)} %param.15) | copy-start | bytes 1327108
  40.6 22.4 %all-to-all-start.1 = ((f32[8,9,2,16,128]{4,3,2,1,0:T(8,128)}), f32[8,9,2,16,128]{4,3,2,1,0:T(8,128)S(1)}, u32[]{:S(2)}, u32[]{:S(2)}) async-start(f32[8,9,2,16,128]{4,3,2,1,0:T(8,128)} %shard_map.103), calls=%async_computation.1 | async-start | bytes 2359296 | tf_op jit(solution)/shard_map/all_to_all | solution.py:349
  46.4 13.0 %collective-permute-start.4 = (f32[432,256]{1,0:T(8,128)S(1)}, f32[432,256]{1,0:T(8,128)S(1)}, u32[]{:S(2)}, u32[]{:S(2)}) collective-permute-start(f32[432,256]{1,0:T(8,128)S(1)} %bitcast.24), channel_id=1, source_target_pairs={{0,384},{128,256},{256,128},{384,0},{1,385},{129,257},{257,129},{3... | collective-permute-start | bytes 1327112 | tf_op jit(solution)/shard_map/ppermute | solution.py:314
  103.3 20.1 %copy-start = (f32[2,256,256]{2,1,0:T(8,128)S(1)}, f32[2,256,256]{2,1,0:T(8,128)}, u32[]{:S(2)}) copy-start(f32[2,256,256]{2,1,0:T(8,128)} %qk_ref.1) | copy-start | bytes 1572868
  103.3 20.1 %copy-start.3 = (f32[256,256]{1,0:T(8,128)S(1)}, f32[256,256]{1,0:T(8,128)}, u32[]{:S(2)}) copy-start(f32[256,256]{1,0:T(8,128)} %value_ref.1) | copy-start | bytes 786436
  103.3 20.1 %copy-start.4 = (f32[256,256]{1,0:T(8,128)S(1)}, f32[256,256]{1,0:T(8,128)}, u32[]{:S(2)}) copy-start(f32[256,256]{1,0:T(8,128)} %proj_ref.1) | copy-start | bytes 786436
  121.4 4.5 %collective-permute-start.5 = (f32[8,16,16,128]{3,2,1,0:T(8,128)S(1)}, f32[8,16,16,128]{3,2,1,0:T(8,128)S(1)}, u32[]{:S(2)}, u32[]{:S(2)}) collective-permute-start(f32[8,16,16,128]{3,2,1,0:T(8,128)S(1)} %all_to_all.21.mine_ref), channel_id=1, source_target_pairs={{0,1},{1,0},{2,3},{3,2},{4,5},{5,4},{6,7},{7,6},{8,9},{9,8},{10,11... | collective-permute-start | bytes 3145736 | tf_op jit(solution)/shard_map/ppermute | solution.py:366
  129.9 7.1 %collective-permute-start.6 = (f32[64,256]{1,0:T(8,128)S(1)}, f32[64,256]{1,0:T(8,128)S(1)}, u32[]{:S(2)}, u32[]{:S(2)}) collective-permute-start(f32[64,256]{1,0:T(8,128)S(1)} %get-tuple-element.19), channel_id=1, source_target_pairs={{0,0},{1,16},{2,34},{3,50},{4,68},{5,84},{6,102},{7,118},{8,136},{... | collective-permute-start | bytes 196616 | tf_op jit(solution)/shard_map/ppermute | solution.py:383
  132.7 20.4 %collective-permute-start.7 = (f32[64,256]{1,0:T(8,128)S(1)}, f32[64,256]{1,0:T(8,128)S(1)}, u32[]{:S(2)}, u32[]{:S(2)}) collective-permute-start(f32[64,256]{1,0:T(8,128)S(1)} %get-tuple-element.20), channel_id=1, source_target_pairs={{0,1},{1,17},{2,35},{3,51},{4,69},{5,85},{6,103},{7,119},{8,137},{... | collective-permute-start | bytes 196616 | tf_op jit(solution)/shard_map/ppermute | solution.py:384

commit v5 on v4

--- a/solution.py
+++ b/solution.py
@@ -2,6 +2,7 @@
 
 import jax
 import jax.numpy as jnp
+import numpy as np
 from jax import lax
 from jax.experimental import pallas as pl
 from jax.experimental.pallas import tpu as pltpu
@@ -52,6 +53,15 @@
     return one(a_high, b_low) + one(a_low, b_high) + one(a_high, b_high)
 
 
+def dot3_stacked(a_high, a_low, b_high, b_low, dims=((1,), (0,))):
+    def one(a, b):
+        return lax.dot_general(a, b, (dims, ((), ())), preferred_element_type=f32)
+
+    rows = a_high.shape[0]
+    both = one(jnp.concatenate([a_high, a_low], axis=0), b_high)
+    return both[:rows] + (both[rows:] + one(a_high, b_low))
+
+
 def norm_silu(value, gain):
     scale = lax.rsqrt(jnp.mean(value * value, axis=0, keepdims=True) + epsilon)
     value = value * scale * gain
@@ -63,21 +73,41 @@
     return lane, lane % 32, (lane // 32) % 2
 
 
-def taps(product):
-    _, across, row = lanes()
-    left, right, first_row = across >= 1, across <= 30, row == 0
+def row_taps(product, a):
+    _, across, _ = lanes()
+    left, right = across >= 1, across <= 30
+    rows = []
+    for b in range(3):
+        base = (a * 9 + b * 3) * 16
+        rows.append(
+            product[base + 16 : base + 32]
+            + jnp.where(left, pltpu.roll(product[base : base + 16], 1, 1), 0.0)
+            + jnp.where(right, pltpu.roll(product[base + 32 : base + 48], 127, 1), 0.0)
+        )
+    return rows
+
+
+def taps_shifted(product):
+    _, _, row = lanes()
+    first_row = row == 0
     result = []
     for a in range(3):
-        rows = []
-        for b in range(3):
-            base = (a * 9 + b * 3) * 16
-            rows.append(
-                product[base + 16 : base + 32]
-                + jnp.where(left, pltpu.roll(product[base : base + 16], 1, 1), 0.0)
-                + jnp.where(right, pltpu.roll(product[base + 32 : base + 48], 127, 1), 0.0)
-            )
-        stay = jnp.where(first_row, rows[0], rows[2])
-        own = rows[1] + jnp.where(first_row, pltpu.roll(stay, 96, 1), pltpu.roll(stay, 32, 1))
+        rows = row_taps(product, a)
+        stay = rows[2] + jnp.where(first_row, 0.0, pltpu.roll(rows[1], 32, 1))
+        go = rows[0] + jnp.where(first_row, pltpu.roll(rows[1], 96, 1), 0.0)
+        result.append(jnp.concatenate([stay, go], axis=0))
+    return result
+
+
+def taps(product, adjacent):
+    _, _, row = lanes()
+    first_row = row == 0
+    result = []
+    for a in range(3):
+        rows = row_taps(product, a)
+        cross = jnp.where(first_row, rows[0], rows[2])
+        cross = jnp.where(first_row, pltpu.roll(cross, 96, 1), pltpu.roll(cross, 32, 1))
+        own = rows[1] + jnp.where(adjacent, cross, 0.0)
         leave = jnp.where(first_row, rows[2], rows[0])
         result.append(jnp.concatenate([own, leave], axis=0))
     return result
@@ -97,43 +127,36 @@
 
 def conv1_kernel(
     place_ref, video_ref, weight_ref, partner_ref, gain_ref, mask_ref,
-    own_ref, beside_ref, beyond_ref, kept_ref, high_ref, low_ref, product_ref,
+    own_ref, onward_ref, kept_ref, high_ref, low_ref, product_ref,
 ):
-    _, _, row = lanes()
-    first_row = row == 0
     gain = column(gain_ref[0:1])
     for g, ref in enumerate((weight_ref, partner_ref)):
         high_ref[g], low_ref[g] = split(ref[...])
-    half, across, core = place_ref[0], place_ref[2], place_ref[3]
+    half, across = place_ref[0], place_ref[2]
     mine = 2 * half + place_ref[1]
-    for j in range(TILES):
-        kept_ref[j, half] = video_ref[j, mine, across]
-        kept_ref[j, 1 - half] = video_ref[j, 3 - mine, across]
 
     def finish(j, now, before):
         masks = mask_ref[0, pl.ds(8 * half + j, 1)], mask_ref[1, pl.ds(8 * half + j, 1)]
-        outside = []
         for g in range(2):
+            slot = half if g == 0 else 1 - half
             done = in_time(now[g], before[g], *masks)
-            own_ref[j, half if g == 0 else 1 - half] = done[:16]
-            outside.append(done[16:])
-        up = jnp.where(first_row, outside[0], pltpu.roll(outside[1], 32, 1))
-        down = jnp.where(first_row, pltpu.roll(outside[0], 96, 1), outside[1])
-        on_even = core == 0
-        beside_ref[j] = jnp.where(on_even, down, up)
-        beyond_ref[j] = jnp.where(on_even, up, down)
+            own_ref[j, slot] = done[:16]
+            onward_ref[j, slot] = done[16:]
 
     def step(p, before):
         pieces = []
         for side in range(2):
-            tile = video_ref[2 * p + side].reshape(256, 128)
+            j = 2 * p + side
+            kept_ref[j, half] = video_ref[j, mine, across]
+            kept_ref[j, 1 - half] = video_ref[j, 3 - mine, across]
+            tile = video_ref[j].reshape(256, 128)
             pieces.append(split(norm_silu(tile, gain)))
         high = jnp.concatenate([pieces[0][0], pieces[1][0]], axis=1)
         low = jnp.concatenate([pieces[0][1], pieces[1][1]], axis=1)
         for g in range(2):
             product_ref[g] = dot3(high_ref[g], low_ref[g], high, low)
         for side in range(2):
-            now = [taps(product_ref[g, :, 128 * side : 128 * side + 128]) for g in range(2)]
+            now = [taps_shifted(product_ref[g, :, 128 * side : 128 * side + 128]) for g in range(2)]
             finish(2 * p + side, now, before)
             before = now
         return before
@@ -145,26 +168,19 @@
     finish(TILES, zeros, last)
 
 
-def join1_kernel(place_ref, own_ref, beside_ref, beyond_ref, out_ref, history_ref):
+def join1_kernel(place_ref, own_ref, arrived_ref, out_ref, history_ref):
     _, _, row = lanes()
     first_row = row == 0
-    on_even = place_ref[3] == 0
-    for j in range(9):
-        beside, beyond = beside_ref[j], beyond_ref[j]
-        above = jnp.where(on_even, beyond, beside)
-        below = jnp.where(on_even, beside, beyond)
-        added = (
-            jnp.where(first_row, above, pltpu.roll(below, 32, 1)),
-            jnp.where(first_row, pltpu.roll(above, 96, 1), below),
-        )
-        half = place_ref[0]
-        for g in range(2):
-            slot = half if g == 0 else 1 - half
-            tile = own_ref[j, slot] + added[g]
-            if j < 8:
+    at_edge = place_ref[6] == 0
+    for j in range(TILES + 1):
+        for slot in range(2):
+            own, arrived = own_ref[j, slot], arrived_ref[j, slot]
+            edge = jnp.where(first_row, arrived, own)
+            tile = jnp.where(at_edge, edge, own + arrived)
+            if j < TILES:
                 out_ref[j, slot] = tile
-            if j >= 7:
-                history_ref[j - 7, slot] = tile
+            if j >= TILES - 1:
+                history_ref[j - TILES + 1, slot] = tile
 
 
 def send1_kernel(tiles_ref, history_ref, out_ref):
@@ -180,8 +196,9 @@
     place_ref, second_ref, weight_ref, partner_ref, gain_ref, mask_ref, kept_ref,
     out_ref, high_ref, low_ref, product_ref,
 ):
-    lane, _, _ = lanes()
-    low_half = lane < 64
+    lane, _, row = lanes()
+    low_half, second_row = lane < 64, row == 1
+    adjacent = place_ref[6] != 0
     gain = column(gain_ref[1:2])
     half = place_ref[0]
     for q in range(TILES + 1):
@@ -197,13 +214,14 @@
         slot = half if g == 0 else 1 - half
         w_high, w_low = split(ref[...])
         product_ref[...] = dot3(w_high, w_low, high_ref[...], low_ref[...])
-        before = taps(product_ref[:, :128])
+        before = taps(product_ref[:, :128], adjacent)
         for q in range(TILES):
-            now = taps(product_ref[:, 128 * (q + 1) : 128 * (q + 2)])
+            now = taps(product_ref[:, 128 * (q + 1) : 128 * (q + 2)], adjacent)
             at = TILES * half + q
             done = in_time(now, before, mask_ref[0, pl.ds(at, 1)], mask_ref[1, pl.ds(at, 1)])
-            own = done[:16] + kept_ref[q, slot]
-            leave = done[16:]
+            kept = kept_ref[q, slot]
+            own = done[:16] + jnp.where(second_row, pltpu.roll(kept, 32, 1), 0.0)
+            leave = done[16:] + jnp.where(second_row, kept, 0.0)
             out_ref[q, slot] = jnp.where(low_half, own, pltpu.roll(leave, 64, 1))
             out_ref[q + TILES, slot] = jnp.where(low_half, pltpu.roll(own, 64, 1), leave)
             before = now
@@ -212,13 +230,13 @@
 def join2_kernel(parts_ref, out_ref):
     lane, _, _ = lanes()
     first_row, low_half = lane < 32, lane < 64
-    zero = jnp.zeros((16, 128), f32)
 
     def band(s):
-        above = parts_ref[s - 1] if s > 0 else zero
-        below = parts_ref[s + 1] if s < SPACE - 1 else zero
-        return parts_ref[s] + jnp.where(
-            first_row, pltpu.roll(above, 32, 1), pltpu.roll(below, 96, 1)
+        here, after = parts_ref[s], parts_ref[(s + 1) % SPACE]
+        return jnp.where(
+            first_row,
+            pltpu.roll(here, 96, 1) + pltpu.roll(after, 64, 1),
+            pltpu.roll(here, 64, 1) + pltpu.roll(after, 32, 1),
         )
 
     for p in range(16):
@@ -239,11 +257,12 @@
 
 def attend_kernel(
     place_ref, mine_ref, other_ref, gain_ref, folded_ref, same_ref, cross_ref,
-    blocked_ref, high_ref, low_ref,
+    high_ref, low_ref,
 ):
     gain = column(gain_ref[2:3])
     half, core = place_ref[0], place_ref[3]
-    for p in range(16):
+
+    def gathered(p):
         blocks = []
         for slot in range(2):
             for u in range(W):
@@ -251,36 +270,52 @@
                 for x in range(X):
                     mine, other = mine_ref[source + x, p], other_ref[source + x, p]
                     blocks.append(jnp.where(core == slot, mine, other))
-        tile = jnp.concatenate(blocks, axis=0)
-        blocked_ref[p] = tile
+        return jnp.concatenate(blocks, axis=0)
+
+    rows = gathered(place_ref[5]).T
+    normed = rows * lax.rsqrt(jnp.mean(rows * rows, axis=1, keepdims=True) + epsilon) * gain_ref[2:3]
+    queries = dot3_stacked(*split(normed), *split(folded_ref[0]))
+    for p in range(16):
+        tile = gathered(p)
         normed = tile * lax.rsqrt(jnp.mean(tile * tile, axis=0, keepdims=True) + epsilon) * gain
         high, low = split(normed)
         high_ref[:, 128 * p : 128 * p + 128] = high
         low_ref[:, 128 * p : 128 * p + 128] = low
-    at = place_ref[4]
-    rows = blocked_ref[at].T
-    normed = rows * lax.rsqrt(jnp.mean(rows * rows, axis=1, keepdims=True) + epsilon) * gain_ref[2:3]
-    queries = dot3(*split(normed), *split(folded_ref[0]))
-    scores = dot3(*split(queries), high_ref[...], low_ref[...])
+    scores = dot3_stacked(*split(queries), high_ref[...], low_ref[...])
     weights = jnp.exp(scores - jnp.max(scores, axis=1, keepdims=True))
     total = jnp.sum(weights, axis=1, keepdims=True)
-    attended = dot3(*split(weights), high_ref[...], low_ref[...], ((1,), (1,))) / total
-    result = rows + dot3(*split(attended), *split(folded_ref[1]))
-    first_core = place_ref[5] == 0
+    attended = dot3_stacked(*split(weights), high_ref[...], low_ref[...], ((1,), (1,))) / total
+    result = rows + dot3_stacked(*split(attended), *split(folded_ref[1]))
+    first_core = place_ref[4] == 0
     same_ref[...] = jnp.where(first_core, result[:64], result[64:])
     cross_ref[...] = jnp.where(first_core, result[64:], result[:64])
 
 
-def delivery():
+AWAY = ((8, 7), (-7, 6), (-6, 5), (-5, 4), (-4, 3), (-3, 2), (-2, 1), (-1, 0))
+
+
+def offsets():
+    table = np.zeros((W * X, W * X, CORES), np.int32)
+    for home in range(W * X):
+        def hops(chip):
+            across = abs(chip % X - home % X)
+            return abs(chip // X - home // X) + min(across, X - across)
+
+        for rank, chip in enumerate(sorted(range(W * X), key=hops)):
+            table[chip, home] = AWAY[rank]
+    return table % (K * L)
+
+
+def delivery(table):
     routes = ([], [])
     for i in range(W * X):
         for z in range(K * L):
             for c in range(CORES):
                 source = (i * K * L + z) * CORES + c
-                chip = (z + (i if c == 0 else -i if i else 8)) % (K * L)
-                f = z // TILES
+                home, f = z % TILES, z // TILES
+                chip = (z + int(table[i, home, c])) % (K * L)
                 for route, core in zip(routes, (f, 1 - f)):
-                    route.append((source, ((z % TILES) * K * L + chip) * CORES + core))
+                    route.append((source, (home * K * L + chip) * CORES + core))
     return routes
 
 
@@ -299,8 +334,9 @@
     space = ("k", "l", "c")
     h, w, x, k, l, c = (lax.axis_index(n) for n in ("h", "w", "x", "k", "l", "c"))
     z, i = 2 * k + l, X * w + x
-    offset = jnp.where(c == 0, i, jnp.where(i == 0, 8, K * L - i))
-    place = jnp.stack([h, w, x, c, (z + offset) % (K * L), z // TILES]).astype(jnp.int32)
+    table = offsets()
+    rows_at = (z + jnp.asarray(table)[i, z % TILES, c]) % (K * L)
+    place = jnp.stack([h, w, x, c, z // TILES, rows_at, CORES * z + c]).astype(jnp.int32)
 
     earlier = jnp.concatenate([jnp.full((2,), -1, jnp.int32), clip_ids])
     same = jnp.stack([earlier[1:-1] == clip_ids, earlier[:-2] == clip_ids]).astype(f32)
@@ -319,9 +355,9 @@
     spread = call(spread_kernel, shape(W * X, 256, 128), [], video.reshape(128, 256))
     gathered = lax.all_to_all(spread, ("w", "x"), 0, 0)
     weights_scratch = [pltpu.VMEM((2, 432, 256), bf16)] * 2
-    own, beside, beyond, kept = call(
+    own, onward, kept = call(
         conv1_kernel,
-        [shape(9, 2, 16, 128), shape(9, 16, 128), shape(9, 16, 128), shape(TILES, 2, 16, 128)],
+        [shape(9, 2, 16, 128), shape(9, 2, 16, 128), shape(TILES, 2, 16, 128)],
         weights_scratch + [pltpu.VMEM((2, 432, 256), f32)],
         place,
         gathered.reshape(W * X, H * W, X, 16, 128),
@@ -331,17 +367,14 @@
         masks,
         smem=1,
     )
-    between_chips = [(i, i + 1) for i in range(1, SPACE - 1, 2)]
-    beyond = lax.ppermute(beyond, space, between_chips + [(j, i) for i, j in between_chips])
-    beside = lax.ppermute(beside, "c", swap)
+    arrived = lax.ppermute(onward, space, [(i, (i + 1) % SPACE) for i in range(SPACE)])
     tiles, history = call(
         join1_kernel,
         [shape(8, 2, 16, 128), shape(2, 2, 16, 128)],
         [],
         place,
         own,
-        beside,
-        beyond,
+        arrived,
         smem=1,
     )
     history = lax.ppermute(history, ("h", "w"), mirror[: H * W // 2])
@@ -368,7 +401,6 @@
         attend_kernel,
         [shape(64, 256), shape(64, 256)],
         [
-            pltpu.VMEM((16, 256, 128), f32),
             pltpu.VMEM((256, 2048), bf16),
             pltpu.VMEM((256, 2048), bf16),
         ],
@@ -379,7 +411,7 @@
         folded,
         smem=1,
     )
-    route_0, route_1 = delivery()
+    route_0, route_1 = delivery(table)
     same_core = lax.ppermute(same_core, ("w", "x", "k", "l", "c"), route_0)
     other_core = lax.ppermute(other_core, ("w", "x", "k", "l", "c"), route_1)
     first_frame = jnp.where(c == 0, same_core, other_core)

time: 154 us -> 147 us (0.955)
  the two profiles are of different devices: /device:TPU:48 before, /device:TPU:80 now
where the time goes in v5:
time: 147 us
  blocking collectives  53.2 us (36%)
  waiting for transfers between devices  46.6 us (32%)
  starting transfers between devices  29.2 us (20%)
  Pallas kernels  13.8 us (9%)
  local copies, waits for them, and re-layouts  2.47 us (2%)
    all_to_all x1, blocking collectives, body(): parts = lax.all_to_all(parts.reshape(SPACE, 16, 128), space, 0, 0)  32.7 us
    all_to_all x1, blocking collectives, body(): mine = lax.all_to_all(frame, ('w', 'x'), 0, 0)  20.5 us
    pallas_call x8, Pallas kernels, call(): pl.pallas_call(kernel, out_shape=out_shape, in_specs=[pl.BlockSpec(memory...  13.8 us
    ppermute x1, waiting for transfers between devices, body(): other_core = lax.ppermute(other_core, ('w', 'x', 'k', 'l', 'c'), route_1)  11.7 us
    ppermute x1, waiting for transfers between devices, body(): partner_2 = lax.ppermute(weight_2, ('h', 'w'), mirror)  10.2 us
    ppermute x1, waiting for transfers between devices, body(): partner_1 = lax.ppermute(weight_1, ('h', 'w'), mirror)  8.06 us
    all_to_all x1, starting transfers between devices, body(): second = lax.all_to_all(second, ('w', 'x'), 0, 0)  5.79 us
    ppermute x1, starting transfers between devices, body(): same_core = lax.ppermute(same_core, ('w', 'x', 'k', 'l', 'c'), route_0)  5.23 us
  transfers between devices with their start and end apart: 9, of which 8 were waited for; matrix products, arithmetic and copies ran while one was open for 1% of the time, Pallas kernels for 0%

profile of v5, /device:TPU:80, one launch (start us, length us, event | category | flops | bytes accessed | tf_op | source)
XLA Modules:
  0.0 146.9 jit_solution(1907610780173575530)
XLA Ops:
  0.0 0.9 copy-done.5
  0.9 1.2 shard_map.109
  2.1 0.0 copy-start.8
  2.1 5.2 %all-to-all-start = ((f32[8,256,128]{2,1,0:T(8,128)}), f32[8,256,128]{2,1,0:T(8,128)S(1)}, u32[]{:S(2)}, u32[]{:S(2)}) async-start(f32[8,256,128]{2,1,0:T(8,128)} %shard_map.109), calls=%async_computation | async-start | bytes 2097152 | tf_op jit(solution)/shard_map/all_to_all | solution.py:356
  7.3 0.0 copy-done.1
  7.3 3.1 %collective-permute-start = (f32[432,256]{1,0:T(8,128)S(1)}, f32[432,256]{1,0:T(8,128)S(1)}, u32[]{:S(2)}, u32[]{:S(2)}) collective-permute-start(f32[432,256]{1,0:T(8,128)S(1)} %bitcast.24), channel_id=1, source_target_pairs={{0,384},{128,256},{256,128},{384,0},{1,385},{129,257},{257,129},{3... | collective-permute-start | bytes 1327112 | tf_op jit(solution)/shard_map/ppermute | solution.py:349
  10.4 1.3 dynamic_slice.3
  12.4 0.0 copy-done.9
  12.4 0.1 compare_bitcast_fusion.1
  12.5 0.1 broadcast_in_dim.4
  12.5 0.1 reshape_reshape.3
  12.6 0.1 stack.61.place_ref
  12.7 0.0 copy-done.6
  12.7 0.0 copy-done.7
  12.7 0.0 copy-done.8
  12.7 8.1 %collective-permute-done.partner_ref = f32[432,256]{1,0:T(8,128)S(1)} collective-permute-done((f32[432,256]{1,0:T(8,128)S(1)}, f32[432,256]{1,0:T(8,128)S(1)}, u32[]{:S(2)}, u32[]{:S(2)}) %collective-permute-start) | collective-permute-done | bytes 442400 | tf_op jit(solution)/shard_map/ppermute | solution.py:349
  20.8 2.2 %all-to-all-done = f32[8,256,128]{2,1,0:T(8,128)S(1)} async-done(((f32[8,256,128]{2,1,0:T(8,128)}), f32[8,256,128]{2,1,0:T(8,128)S(1)}, u32[]{:S(2)}, u32[]{:S(2)}) %all-to-all-start) | async-done | bytes 1048608 | tf_op jit(solution)/shard_map/all_to_all | solution.py:356
  23.0 2.4 %shard_map.110 = (f32[9,2,16,128]{3,2,1,0:T(8,128)S(1)}, f32[9,2,16,128]{3,2,1,0:T(8,128)S(1)}, f32[8,2,16,128]{3,2,1,0:T(8,128)S(1)}) custom-call(s32[7]{0:T(128)S(1)} %stack.61.place_ref, f32[8,4,4,16,128]{4,3,2,1,0:T(8,128)S(1)} %bitcast.22, f32[432,256]{1,0:T(8,128)S(1)} %bitcast.25, f32[432,256]{1,0:T(8,128)S(1)} %collective-permute-done.partner_ref, ...), custom_call_target="tpu_custom_call" | custom-call | tf_op jit(solution)/shard_map/pallas_call | solution.py:25
  25.4 0.0 collective-permute-start.1
  25.4 4.6 %collective-permute-done.1.arrived_ref = f32[9,2,16,128]{3,2,1,0:T(8,128)S(1)} collective-permute-done((f32[9,2,16,128]{3,2,1,0:T(8,128)S(1)}, f32[9,2,16,128]{3,2,1,0:T(8,128)S(1)}, u32[]{:S(2)}, u32[]{:S(2)}) %collective-permute-start.1) | collective-permute-done | bytes 147488 | tf_op jit(solution)/shard_map/ppermute | solution.py:370
  30.0 0.6 shard_map.111
  30.6 1.3 collective-permute-start.2
  31.9 4.5 %collective-permute-done.2.history_ref = f32[2,2,16,128]{3,2,1,0:T(8,128)S(1)} collective-permute-done((f32[2,2,16,128]{3,2,1,0:T(8,128)S(1)}, f32[2,2,16,128]{3,2,1,0:T(8,128)S(1)}, u32[]{:S(2)}, u32[]{:S(2)}) %collective-permute-start.2) | collective-permute-done | bytes 32800 | tf_op jit(solution)/shard_map/ppermute | solution.py:380
  36.4 1.1 shard_map.112
  37.5 5.8 %all-to-all-start.1 = ((f32[8,9,2,16,128]{4,3,2,1,0:T(8,128)}), f32[8,9,2,16,128]{4,3,2,1,0:T(8,128)S(1)}, u32[]{:S(2)}, u32[]{:S(2)}) async-start(f32[8,9,2,16,128]{4,3,2,1,0:T(8,128)} %shard_map.112), calls=%async_computation.1 | async-start | bytes 2359296 | tf_op jit(solution)/shard_map/all_to_all | solution.py:382
  43.3 0.0 copy-done.2
  43.3 1.9 %collective-permute-start.3 = (f32[432,256]{1,0:T(8,128)S(1)}, f32[432,256]{1,0:T(8,128)S(1)}, u32[]{:S(2)}, u32[]{:S(2)}) collective-permute-start(f32[432,256]{1,0:T(8,128)S(1)} %bitcast.26), channel_id=1, source_target_pairs={{0,384},{128,256},{256,128},{384,0},{1,385},{129,257},{257,129},{3... | collective-permute-start | bytes 1327112 | tf_op jit(solution)/shard_map/ppermute | solution.py:350
  45.2 10.2 %collective-permute-done.3.partner_ref = f32[432,256]{1,0:T(8,128)S(1)} collective-permute-done((f32[432,256]{1,0:T(8,128)S(1)}, f32[432,256]{1,0:T(8,128)S(1)}, u32[]{:S(2)}, u32[]{:S(2)}) %collective-permute-start.3) | collective-permute-done | bytes 442400 | tf_op jit(solution)/shard_map/ppermute | solution.py:350
  55.4 3.6 %all-to-all-done.1.second_ref = f32[8,9,2,16,128]{4,3,2,1,0:T(8,128)S(1)} async-done(((f32[8,9,2,16,128]{4,3,2,1,0:T(8,128)}), f32[8,9,2,16,128]{4,3,2,1,0:T(8,128)S(1)}, u32[]{:S(2)}, u32[]{:S(2)}) %all-to-all-start.1) | async-done | bytes 1179680 | tf_op jit(solution)/shard_map/all_to_all | solution.py:382
  59.0 3.3 %shard_map.113 = f32[16,2,16,128]{3,2,1,0:T(8,128)S(1)} custom-call(s32[7]{0:T(128)S(1)} %stack.61.place_ref, f32[8,9,2,16,128]{4,3,2,1,0:T(8,128)S(1)} %all-to-all-done.1.second_ref, f32[432,256]{1,0:T(8,128)S(1)} %bitcast.27, f32[432,256]{1,0:T(8,128)S(1)} %collective-permute-done.3.partner_ref, f32[3,256]{1,0:T(4,128)S(1)} %pad_maximum_fusion.1.gain_ref, ...), custom_call_target="tpu_custom_call" | custom-call | tf_op jit(solution)/shard_map/pallas_call | solution.py:25
  62.3 32.7 %all_to_all.20.parts_ref = f32[32,16,128]{2,1,0:T(8,128)S(1)} all-to-all(f32[32,16,128]{2,1,0:T(8,128)S(1)} %bitcast.23), channel_id=1, replica_groups=mesh['h'=2,'w'=2,'x'=4,'k'=8,'l'=2,'c'=2] {'k','l','c'}, dimensions={0} | all-to-all | bytes 524288 | tf_op jit(solution)/shard_map/all_to_all | solution.py:396
  95.0 0.9 shard_map.114
  95.9 0.0 copy-start
  95.9 0.0 copy-start.3
  95.9 0.0 copy-start.4
  95.9 20.5 %all_to_all.21.mine_ref = f32[8,16,16,128]{3,2,1,0:T(8,128)S(1)} all-to-all(f32[8,16,16,128]{3,2,1,0:T(8,128)S(1)} %shard_map.114), channel_id=1, replica_groups=mesh['h'=2,'w'=2,'x'=4,'k'=8,'l'=2,'c'=2] {'w','x'}, dimensions={0} | all-to-all | bytes 2097152 | tf_op jit(solution)/shard_map/all_to_all | solution.py:398
  116.4 2.0 %collective-permute-start.4 = (f32[8,16,16,128]{3,2,1,0:T(8,128)S(1)}, f32[8,16,16,128]{3,2,1,0:T(8,128)S(1)}, u32[]{:S(2)}, u32[]{:S(2)}) collective-permute-start(f32[8,16,16,128]{3,2,1,0:T(8,128)S(1)} %all_to_all.21.mine_ref), channel_id=1, source_target_pairs={{0,1},{1,0},{2,3},{3,2},{4,5},{5,4},{6,7},{7,6},{8,9},{9,8},{10,11... | collective-permute-start | bytes 3145736 | tf_op jit(solution)/shard_map/ppermute | solution.py:399
  118.5 0.0 copy-done
  118.5 0.0 copy-done.3
  118.5 0.0 copy-done.4
  118.5 0.7 shard_map.115.folded_ref
  119.2 1.8 %collective-permute-done.4.other_ref = f32[8,16,16,128]{3,2,1,0:T(8,128)S(1)} collective-permute-done((f32[8,16,16,128]{3,2,1,0:T(8,128)S(1)}, f32[8,16,16,128]{3,2,1,0:T(8,128)S(1)}, u32[]{:S(2)}, u32[]{:S(2)}) %collective-permute-start.4) | collective-permute-done | bytes 1048608 | tf_op jit(solution)/shard_map/ppermute | solution.py:399
  121.0 3.6 %shard_map.116 = (f32[64,256]{1,0:T(8,128)S(1)}, f32[64,256]{1,0:T(8,128)S(1)}) custom-call(s32[7]{0:T(128)S(1)} %stack.61.place_ref, f32[8,16,16,128]{3,2,1,0:T(8,128)S(1)} %all_to_all.21.mine_ref, f32[8,16,16,128]{3,2,1,0:T(8,128)S(1)} %collective-permute-done.4.other_ref, f32[3,256]{1,0:T(4,128)S(1)} %pad_maximum_fusion.1.gain_ref, ...), custom_call_target="tpu_custom_call" | custom-call | tf_op jit(solution)/shard_map/pallas_call | solution.py:25
  124.6 5.2 %collective-permute-start.5 = (f32[64,256]{1,0:T(8,128)S(1)}, f32[64,256]{1,0:T(8,128)S(1)}, u32[]{:S(2)}, u32[]{:S(2)}) collective-permute-start(f32[64,256]{1,0:T(8,128)S(1)} %get-tuple-element.17), channel_id=1, source_target_pairs={{0,16},{1,14},{2,52},{3,46},{4,92},{5,74},{6,120},{7,114},{8,154},... | collective-permute-start | bytes 196616 | tf_op jit(solution)/shard_map/ppermute | solution.py:415
  129.9 4.7 %collective-permute-start.6 = (f32[64,256]{1,0:T(8,128)S(1)}, f32[64,256]{1,0:T(8,128)S(1)}, u32[]{:S(2)}, u32[]{:S(2)}) collective-permute-start(f32[64,256]{1,0:T(8,128)S(1)} %get-tuple-element.18), channel_id=1, source_target_pairs={{0,17},{1,15},{2,53},{3,47},{4,93},{5,75},{6,121},{7,115},{8,155},... | collective-permute-start | bytes 196616 | tf_op jit(solution)/shard_map/ppermute | solution.py:416
  134.5 0.0 collective-permute-done.5
  134.5 11.7 %collective-permute-done.6 = f32[64,256]{1,0:T(8,128)S(1)} collective-permute-done((f32[64,256]{1,0:T(8,128)S(1)}, f32[64,256]{1,0:T(8,128)S(1)}, u32[]{:S(2)}, u32[]{:S(2)}) %collective-permute-start.6) | collective-permute-done | bytes 65568 | tf_op jit(solution)/shard_map/ppermute | solution.py:416
  146.3 0.7 pad_maximum_fusion
  (10 shorter events, 0.0 us)
Async XLA Ops:
  0.0 0.9 copy-start.5
  2.1 5.2 %copy-start.1 = (f32[3,3,3,16,256]{4,3,2,1,0:T(8,128)S(1)}, f32[3,3,3,16,256]{4,3,2,1,0:T(8,128)}, u32[]{:S(2)}) copy-start(f32[3,3,3,16,256]{4,3,2,1,0:T(8,128)} %param.14) | copy-start | bytes 1327108
  2.1 10.3 %copy-start.9 = (s32[32]{0:T(128)S(1)}, s32[32]{0:T(128)}, u32[]{:S(2)}) copy-start(s32[32]{0:T(128)} %param.12) | copy-start | bytes 388
  2.1 10.6 %copy-start.6 = (f32[256]{0:T(256)S(1)}, f32[256]{0:T(256)}, u32[]{:S(2)}) copy-start(f32[256]{0:T(256)} %param.17) | copy-start | bytes 3076
  2.1 10.6 %copy-start.7 = (f32[256]{0:T(256)S(1)}, f32[256]{0:T(256)}, u32[]{:S(2)}) copy-start(f32[256]{0:T(256)} %param.15) | copy-start | bytes 3076
  2.1 10.6 %copy-start.8 = (f32[256]{0:T(256)S(1)}, f32[256]{0:T(256)}, u32[]{:S(2)}) copy-start(f32[256]{0:T(256)} %param.13) | copy-start | bytes 3076
  2.1 20.9 %all-to-all-start = ((f32[8,256,128]{2,1,0:T(8,128)}), f32[8,256,128]{2,1,0:T(8,128)S(1)}, u32[]{:S(2)}, u32[]{:S(2)}) async-start(f32[8,256,128]{2,1,0:T(8,128)} %shard_map.109), calls=%async_computation | async-start | bytes 2097152 | tf_op jit(solution)/shard_map/all_to_all | solution.py:356
  7.3 13.5 %collective-permute-start = (f32[432,256]{1,0:T(8,128)S(1)}, f32[432,256]{1,0:T(8,128)S(1)}, u32[]{:S(2)}, u32[]{:S(2)}) collective-permute-start(f32[432,256]{1,0:T(8,128)S(1)} %bitcast.24), channel_id=1, source_target_pairs={{0,384},{128,256},{256,128},{384,0},{1,385},{129,257},{257,129},{3... | collective-permute-start | bytes 1327112 | tf_op jit(solution)/shard_map/ppermute | solution.py:349
  25.4 4.6 %collective-permute-start.1 = (f32[9,2,16,128]{3,2,1,0:T(8,128)S(1)}, f32[9,2,16,128]{3,2,1,0:T(8,128)S(1)}, u32[]{:S(2)}, u32[]{:S(2)}) collective-permute-start(f32[9,2,16,128]{3,2,1,0:T(8,128)S(1)} %get-tuple-element.13), channel_id=1, source_target_pairs={{0,1},{1,2},{2,3},{3,4},{4,5},{5,6},{6,7},{7,8},{8,9},{9,10},{10,1... | collective-permute-start | bytes 442376 | tf_op jit(solution)/shard_map/ppermute | solution.py:370
  30.6 5.8 %collective-permute-start.2 = (f32[2,2,16,128]{3,2,1,0:T(8,128)S(1)}, f32[2,2,16,128]{3,2,1,0:T(8,128)S(1)}, u32[]{:S(2)}, u32[]{:S(2)}) collective-permute-start(f32[2,2,16,128]{3,2,1,0:T(8,128)S(1)} %get-tuple-element.15), channel_id=1, source_target_pairs={{0,384},{128,256},{1,385},{129,257},{2,386},{130,258},{3,387},{131... | collective-permute-start | bytes 98312 | tf_op jit(solution)/shard_map/ppermute | solution.py:380
  37.5 5.8 %copy-start.2 = (f32[3,3,3,16,256]{4,3,2,1,0:T(8,128)S(1)}, f32[3,3,3,16,256]{4,3,2,1,0:T(8,128)}, u32[]{:S(2)}) copy-start(f32[3,3,3,16,256]{4,3,2,1,0:T(8,128)} %param.16) | copy-start | bytes 1327108
  37.5 21.5 %all-to-all-start.1 = ((f32[8,9,2,16,128]{4,3,2,1,0:T(8,128)}), f32[8,9,2,16,128]{4,3,2,1,0:T(8,128)S(1)}, u32[]{:S(2)}, u32[]{:S(2)}) async-start(f32[8,9,2,16,128]{4,3,2,1,0:T(8,128)} %shard_map.112), calls=%async_computation.1 | async-start | bytes 2359296 | tf_op jit(solution)/shard_map/all_to_all | solution.py:382
  43.3 12.1 %collective-permute-start.3 = (f32[432,256]{1,0:T(8,128)S(1)}, f32[432,256]{1,0:T(8,128)S(1)}, u32[]{:S(2)}, u32[]{:S(2)}) collective-permute-start(f32[432,256]{1,0:T(8,128)S(1)} %bitcast.26), channel_id=1, source_target_pairs={{0,384},{128,256},{256,128},{384,0},{1,385},{129,257},{257,129},{3... | collective-permute-start | bytes 1327112 | tf_op jit(solution)/shard_map/ppermute | solution.py:350
  95.9 22.6 %copy-start = (f32[2,256,256]{2,1,0:T(8,128)S(1)}, f32[2,256,256]{2,1,0:T(8,128)}, u32[]{:S(2)}) copy-start(f32[2,256,256]{2,1,0:T(8,128)} %qk_ref.1) | copy-start | bytes 1572868
  95.9 22.6 %copy-start.3 = (f32[256,256]{1,0:T(8,128)S(1)}, f32[256,256]{1,0:T(8,128)}, u32[]{:S(2)}) copy-start(f32[256,256]{1,0:T(8,128)} %value_ref.1) | copy-start | bytes 786436
  95.9 22.6 %copy-start.4 = (f32[256,256]{1,0:T(8,128)S(1)}, f32[256,256]{1,0:T(8,128)}, u32[]{:S(2)}) copy-start(f32[256,256]{1,0:T(8,128)} %proj_ref.1) | copy-start | bytes 786436
  116.4 4.5 %collective-permute-start.4 = (f32[8,16,16,128]{3,2,1,0:T(8,128)S(1)}, f32[8,16,16,128]{3,2,1,0:T(8,128)S(1)}, u32[]{:S(2)}, u32[]{:S(2)}) collective-permute-start(f32[8,16,16,128]{3,2,1,0:T(8,128)S(1)} %all_to_all.21.mine_ref), channel_id=1, source_target_pairs={{0,1},{1,0},{2,3},{3,2},{4,5},{5,4},{6,7},{7,6},{8,9},{9,8},{10,11... | collective-permute-start | bytes 3145736 | tf_op jit(solution)/shard_map/ppermute | solution.py:399
  124.6 9.9 %collective-permute-start.5 = (f32[64,256]{1,0:T(8,128)S(1)}, f32[64,256]{1,0:T(8,128)S(1)}, u32[]{:S(2)}, u32[]{:S(2)}) collective-permute-start(f32[64,256]{1,0:T(8,128)S(1)} %get-tuple-element.17), channel_id=1, source_target_pairs={{0,16},{1,14},{2,52},{3,46},{4,92},{5,74},{6,120},{7,114},{8,154},... | collective-permute-start | bytes 196616 | tf_op jit(solution)/shard_map/ppermute | solution.py:415
  129.9 16.4 %collective-permute-start.6 = (f32[64,256]{1,0:T(8,128)S(1)}, f32[64,256]{1,0:T(8,128)S(1)}, u32[]{:S(2)}, u32[]{:S(2)}) collective-permute-start(f32[64,256]{1,0:T(8,128)S(1)} %get-tuple-element.18), channel_id=1, source_target_pairs={{0,17},{1,15},{2,53},{3,47},{4,93},{5,75},{6,121},{7,115},{8,155},... | collective-permute-start | bytes 196616 | tf_op jit(solution)/shard_map/ppermute | solution.py:416

commit v6 on v5

--- a/solution.py
+++ b/solution.py
@@ -127,7 +127,7 @@
 
 def conv1_kernel(
     place_ref, video_ref, weight_ref, partner_ref, gain_ref, mask_ref,
-    own_ref, onward_ref, kept_ref, high_ref, low_ref, product_ref,
+    own_ref, onward_ref, last_ref, last_onward_ref, kept_ref, high_ref, low_ref, product_ref,
 ):
     gain = column(gain_ref[0:1])
     for g, ref in enumerate((weight_ref, partner_ref)):
@@ -140,8 +140,12 @@
         for g in range(2):
             slot = half if g == 0 else 1 - half
             done = in_time(now[g], before[g], *masks)
-            own_ref[j, slot] = done[:16]
-            onward_ref[j, slot] = done[16:]
+            if j < TILES:
+                own_ref[j, slot] = done[:16]
+                onward_ref[j, slot] = done[16:]
+            if j >= TILES - 1:
+                last_ref[j - TILES + 1, slot] = done[:16]
+                last_onward_ref[j - TILES + 1, slot] = done[16:]
 
     def step(p, before):
         pieces = []
@@ -168,28 +172,26 @@
     finish(TILES, zeros, last)
 
 
-def join1_kernel(place_ref, own_ref, arrived_ref, out_ref, history_ref):
+def join1_kernel(
+    place_ref, own_ref, arrived_ref, last_ref, last_arrived_ref, out_ref
+):
     _, _, row = lanes()
     first_row = row == 0
     at_edge = place_ref[6] == 0
-    for j in range(TILES + 1):
+
+    def joined(own, arrived):
+        return jnp.where(at_edge, jnp.where(first_row, arrived, own), own + arrived)
+
+    for q in range(TILES + 1):
         for slot in range(2):
-            own, arrived = own_ref[j, slot], arrived_ref[j, slot]
-            edge = jnp.where(first_row, arrived, own)
-            tile = jnp.where(at_edge, edge, own + arrived)
-            if j < TILES:
-                out_ref[j, slot] = tile
-            if j >= TILES - 1:
-                history_ref[j - TILES + 1, slot] = tile
-
-
-def send1_kernel(tiles_ref, history_ref, out_ref):
-    for q in range(TILES + 1):
-        tile = history_ref[0] if q == 0 else tiles_ref[q - 1]
-        if q == 1:
-            tile = tile + history_ref[1]
-        for i in range(W * X):
-            out_ref[i, q] = tile
+            if q == 0:
+                tile = joined(last_ref[0, slot], last_arrived_ref[0, slot])
+            else:
+                tile = joined(own_ref[q - 1, slot], arrived_ref[q - 1, slot])
+            if q == 1:
+                tile = tile + joined(last_ref[1, slot], last_arrived_ref[1, slot])
+            for i in range(W * X):
+                out_ref[i, q, slot] = tile
 
 
 def conv2_kernel(
@@ -197,7 +199,7 @@
     out_ref, high_ref, low_ref, product_ref,
 ):
     lane, _, row = lanes()
-    low_half, second_row = lane < 64, row == 1
+    low_half, first_row = lane < 64, row == 0
     adjacent = place_ref[6] != 0
     gain = column(gain_ref[1:2])
     half = place_ref[0]
@@ -219,28 +221,20 @@
             now = taps(product_ref[:, 128 * (q + 1) : 128 * (q + 2)], adjacent)
             at = TILES * half + q
             done = in_time(now, before, mask_ref[0, pl.ds(at, 1)], mask_ref[1, pl.ds(at, 1)])
-            kept = kept_ref[q, slot]
-            own = done[:16] + jnp.where(second_row, pltpu.roll(kept, 32, 1), 0.0)
-            leave = done[16:] + jnp.where(second_row, kept, 0.0)
-            out_ref[q, slot] = jnp.where(low_half, own, pltpu.roll(leave, 64, 1))
-            out_ref[q + TILES, slot] = jnp.where(low_half, pltpu.roll(own, 64, 1), leave)
+            own, leave = done[:16], done[16:]
+            here = jnp.where(first_row, pltpu.roll(own, 96, 1), leave) + kept_ref[q, slot]
+            above = jnp.where(first_row, leave, pltpu.roll(own, 32, 1))
+            out_ref[q, slot] = jnp.where(low_half, here, pltpu.roll(above, 64, 1))
+            out_ref[q + TILES, slot] = jnp.where(low_half, pltpu.roll(here, 64, 1), above)
             before = now
 
 
 def join2_kernel(parts_ref, out_ref):
     lane, _, _ = lanes()
-    first_row, low_half = lane < 32, lane < 64
-
-    def band(s):
-        here, after = parts_ref[s], parts_ref[(s + 1) % SPACE]
-        return jnp.where(
-            first_row,
-            pltpu.roll(here, 96, 1) + pltpu.roll(after, 64, 1),
-            pltpu.roll(here, 64, 1) + pltpu.roll(after, 32, 1),
-        )
-
+    low_half = lane < 64
     for p in range(16):
-        tile = jnp.where(low_half, band(2 * p), pltpu.roll(band(2 * p + 1), 64, 1))
+        outer = jnp.where(low_half, parts_ref[2 * p], parts_ref[(2 * p + 2) % SPACE])
+        tile = outer + pltpu.roll(parts_ref[2 * p + 1], 64, 1)
         for i in range(W * X):
             out_ref[i, p] = tile
 
@@ -355,9 +349,15 @@
     spread = call(spread_kernel, shape(W * X, 256, 128), [], video.reshape(128, 256))
     gathered = lax.all_to_all(spread, ("w", "x"), 0, 0)
     weights_scratch = [pltpu.VMEM((2, 432, 256), bf16)] * 2
-    own, onward, kept = call(
+    own, onward, last, last_onward, kept = call(
         conv1_kernel,
-        [shape(9, 2, 16, 128), shape(9, 2, 16, 128), shape(TILES, 2, 16, 128)],
+        [
+            shape(TILES, 2, 16, 128),
+            shape(TILES, 2, 16, 128),
+            shape(2, 2, 16, 128),
+            shape(2, 2, 16, 128),
+            shape(TILES, 2, 16, 128),
+        ],
         weights_scratch + [pltpu.VMEM((2, 432, 256), f32)],
         place,
         gathered.reshape(W * X, H * W, X, 16, 128),
@@ -367,18 +367,25 @@
         masks,
         smem=1,
     )
+    onto_next = [
+        (i * SPACE + s, j * SPACE + (s + 1) % SPACE)
+        for i, j in mirror[: H * W // 2]
+        for s in range(SPACE)
+    ]
+    last = lax.ppermute(last, ("h", "w"), mirror[: H * W // 2])
+    last_arrived = lax.ppermute(last_onward, ("h", "w") + space, onto_next)
     arrived = lax.ppermute(onward, space, [(i, (i + 1) % SPACE) for i in range(SPACE)])
-    tiles, history = call(
+    second = call(
         join1_kernel,
-        [shape(8, 2, 16, 128), shape(2, 2, 16, 128)],
+        shape(W * X, TILES + 1, 2, 16, 128),
         [],
         place,
         own,
         arrived,
+        last,
+        last_arrived,
         smem=1,
     )
-    history = lax.ppermute(history, ("h", "w"), mirror[: H * W // 2])
-    second = call(send1_kernel, shape(W * X, TILES + 1, 2, 16, 128), [], tiles, history)
     second = lax.all_to_all(second, ("w", "x"), 0, 0)
     parts = call(
         conv2_kernel,

time: 147 us -> 146 us (level)
  waiting for transfers between devices: 46.6 us -> 44.4 us
  starting transfers between devices: 29.2 us -> 31.1 us
    ppermute x1, waiting for transfers between devices: 4.55 us -> 0.01 us  [body(): lax.ppermute(onward, space, [(i, (i + 1) % SPACE) for i in range(SPACE)])]
    ppermute x1, waiting for transfers between devices: 10.2 us -> 11.9 us  [body(): partner_2 = lax.ppermute(weight_2, ('h', 'w'), mirror)]
    pallas_call x8 -> x7, Pallas kernels: 13.8 us -> 13.1 us  [call(): pl.pallas_call(kernel, out_shape=out_shape, in_specs=[pl.BlockSpec(memory...]
    ppermute x1 -> x2, waiting for transfers between devices: 4.51 us -> 5.09 us  [the longest x1 3.21 us: body(): last = lax.ppermute(last, ('h', 'w'), mirror[:H * W // 2])]
  transfers between devices with their start and end apart: 9 -> 10, of which waited for: 8 -> 8; matrix products, arithmetic and copies ran while one was open for 1% -> 1% of each run, Pallas kernels for 0% -> 0%
where the time goes in v6:
time: 146 us
  blocking collectives  52.7 us (36%)
  waiting for transfers between devices  44.4 us (30%)
  starting transfers between devices  31.1 us (21%)
  Pallas kernels  13.1 us (9%)
  local copies, waits for them, and re-layouts  2.47 us (2%)
    all_to_all x1, blocking collectives, body(): parts = lax.all_to_all(parts.reshape(SPACE, 16, 128), space, 0, 0)  32.7 us
    all_to_all x1, blocking collectives, body(): mine = lax.all_to_all(frame, ('w', 'x'), 0, 0)  20.1 us
    pallas_call x7, Pallas kernels, call(): pl.pallas_call(kernel, out_shape=out_shape, in_specs=[pl.BlockSpec(memory...  13.1 us
    ppermute x1, waiting for transfers between devices, body(): partner_2 = lax.ppermute(weight_2, ('h', 'w'), mirror)  11.9 us
    ppermute x1, waiting for transfers between devices, body(): other_core = lax.ppermute(other_core, ('w', 'x', 'k', 'l', 'c'), route_1)  11.7 us
    ppermute x1, waiting for transfers between devices, body(): partner_1 = lax.ppermute(weight_1, ('h', 'w'), mirror)  8.06 us
    all_to_all x1, starting transfers between devices, body(): second = lax.all_to_all(second, ('w', 'x'), 0, 0)  5.79 us
    ppermute x1, starting transfers between devices, body(): same_core = lax.ppermute(same_core, ('w', 'x', 'k', 'l', 'c'), route_0)  5.23 us
  transfers between devices with their start and end apart: 10, of which 8 were waited for; matrix products, arithmetic and copies ran while one was open for 1% of the time, Pallas kernels for 0%

profile of v6, /device:TPU:80, one launch (start us, length us, event | category | flops | bytes accessed | tf_op | source)
XLA Modules:
  0.0 145.6 jit_solution(12680583541176007135)
XLA Ops:
  0.0 0.9 copy-done.5
  0.9 1.2 shard_map.109
  2.1 0.0 copy-start.8
  2.1 5.2 %all-to-all-start = ((f32[8,256,128]{2,1,0:T(8,128)}), f32[8,256,128]{2,1,0:T(8,128)S(1)}, u32[]{:S(2)}, u32[]{:S(2)}) async-start(f32[8,256,128]{2,1,0:T(8,128)} %shard_map.109), calls=%async_computation | async-start | bytes 2097152 | tf_op jit(solution)/shard_map/all_to_all | solution.py:350
  7.3 0.0 copy-done.1
  7.3 3.1 %collective-permute-start = (f32[432,256]{1,0:T(8,128)S(1)}, f32[432,256]{1,0:T(8,128)S(1)}, u32[]{:S(2)}, u32[]{:S(2)}) collective-permute-start(f32[432,256]{1,0:T(8,128)S(1)} %bitcast.24), channel_id=1, source_target_pairs={{0,384},{128,256},{256,128},{384,0},{1,385},{129,257},{257,129},{3... | collective-permute-start | bytes 1327112 | tf_op jit(solution)/shard_map/ppermute | solution.py:343
  10.4 1.3 dynamic_slice.3
  12.4 0.0 copy-done.9
  12.4 0.1 compare_bitcast_fusion.1
  12.5 0.1 broadcast_in_dim.4
  12.5 0.1 reshape_reshape.3
  12.6 0.1 stack.61.place_ref
  12.7 0.0 copy-done.6
  12.7 0.0 copy-done.7
  12.7 0.0 copy-done.8
  12.7 8.1 %collective-permute-done.partner_ref = f32[432,256]{1,0:T(8,128)S(1)} collective-permute-done((f32[432,256]{1,0:T(8,128)S(1)}, f32[432,256]{1,0:T(8,128)S(1)}, u32[]{:S(2)}, u32[]{:S(2)}) %collective-permute-start) | collective-permute-done | bytes 442400 | tf_op jit(solution)/shard_map/ppermute | solution.py:343
  20.8 2.2 %all-to-all-done = f32[8,256,128]{2,1,0:T(8,128)S(1)} async-done(((f32[8,256,128]{2,1,0:T(8,128)}), f32[8,256,128]{2,1,0:T(8,128)S(1)}, u32[]{:S(2)}, u32[]{:S(2)}) %all-to-all-start) | async-done | bytes 1048608 | tf_op jit(solution)/shard_map/all_to_all | solution.py:350
  23.0 2.4 %shard_map.110 = (f32[8,2,16,128]{3,2,1,0:T(8,128)S(1)}, f32[8,2,16,128]{3,2,1,0:T(8,128)S(1)}, f32[2,2,16,128]{3,2,1,0:T(8,128)S(1)}, f32[2,2,16,128]{3,2,1,0:T(8,128)S(1)}, f32[8,2,16,128]{3,2,1,0:T(8,128)S(1)}) custom-call(s32[7]{0:T(128)S(1)} %stack.61.place_ref, f32[8,4,4,16,128]{4,3,2,1,0:T(8,128)S(1)} %bitcast.22, f32[432,256]{1,0:T(8,128)S(1)} %bitcast.25, ...), custom_call_target="tpu_custom_call" | custom-call | tf_op jit(solution)/shard_map/pallas_call | solution.py:25
  25.4 0.0 collective-permute-start.1
  25.4 1.3 collective-permute-start.2
  26.7 1.3 collective-permute-start.3
  28.0 3.2 %collective-permute-done.2.last_ref = f32[2,2,16,128]{3,2,1,0:T(8,128)S(1)} collective-permute-done((f32[2,2,16,128]{3,2,1,0:T(8,128)S(1)}, f32[2,2,16,128]{3,2,1,0:T(8,128)S(1)}, u32[]{:S(2)}, u32[]{:S(2)}) %collective-permute-start.2) | collective-permute-done | bytes 32800 | tf_op jit(solution)/shard_map/ppermute | solution.py:375
  31.2 1.9 %collective-permute-done.3.last_arrived_ref = f32[2,2,16,128]{3,2,1,0:T(8,128)S(1)} collective-permute-done((f32[2,2,16,128]{3,2,1,0:T(8,128)S(1)}, f32[2,2,16,128]{3,2,1,0:T(8,128)S(1)}, u32[]{:S(2)}, u32[]{:S(2)}) %collective-permute-start.3) | collective-permute-done | bytes 32800 | tf_op jit(solution)/shard_map/ppermute | solution.py:376
  33.1 0.0 collective-permute-done.1.arrived_ref
  33.1 1.7 %shard_map.111 = f32[8,9,2,16,128]{4,3,2,1,0:T(8,128)} custom-call(s32[7]{0:T(128)S(1)} %stack.61.place_ref, f32[8,2,16,128]{3,2,1,0:T(8,128)S(1)} %get-tuple-element.12.own_ref, f32[8,2,16,128]{3,2,1,0:T(8,128)S(1)} %collective-permute-done.1.arrived_ref, f32[2,2,16,128]{3,2,1,0:T(8,128)S(1)} %collective-permute-done.2.last_ref, ...), custom_call_target="tpu_custom_call" | custom-call | tf_op jit(solution)/shard_map/pallas_call | solution.py:25
  34.8 5.8 %all-to-all-start.1 = ((f32[8,9,2,16,128]{4,3,2,1,0:T(8,128)}), f32[8,9,2,16,128]{4,3,2,1,0:T(8,128)S(1)}, u32[]{:S(2)}, u32[]{:S(2)}) async-start(f32[8,9,2,16,128]{4,3,2,1,0:T(8,128)} %shard_map.111), calls=%async_computation.1 | async-start | bytes 2359296 | tf_op jit(solution)/shard_map/all_to_all | solution.py:389
  40.6 0.0 copy-done.2
  40.6 2.6 %collective-permute-start.4 = (f32[432,256]{1,0:T(8,128)S(1)}, f32[432,256]{1,0:T(8,128)S(1)}, u32[]{:S(2)}, u32[]{:S(2)}) collective-permute-start(f32[432,256]{1,0:T(8,128)S(1)} %bitcast.26), channel_id=1, source_target_pairs={{0,384},{128,256},{256,128},{384,0},{1,385},{129,257},{257,129},{3... | collective-permute-start | bytes 1327112 | tf_op jit(solution)/shard_map/ppermute | solution.py:344
  43.2 11.9 %collective-permute-done.4.partner_ref = f32[432,256]{1,0:T(8,128)S(1)} collective-permute-done((f32[432,256]{1,0:T(8,128)S(1)}, f32[432,256]{1,0:T(8,128)S(1)}, u32[]{:S(2)}, u32[]{:S(2)}) %collective-permute-start.4) | collective-permute-done | bytes 442400 | tf_op jit(solution)/shard_map/ppermute | solution.py:344
  55.2 3.6 %all-to-all-done.1.second_ref = f32[8,9,2,16,128]{4,3,2,1,0:T(8,128)S(1)} async-done(((f32[8,9,2,16,128]{4,3,2,1,0:T(8,128)}), f32[8,9,2,16,128]{4,3,2,1,0:T(8,128)S(1)}, u32[]{:S(2)}, u32[]{:S(2)}) %all-to-all-start.1) | async-done | bytes 1179680 | tf_op jit(solution)/shard_map/all_to_all | solution.py:389
  58.7 3.4 %shard_map.112 = f32[16,2,16,128]{3,2,1,0:T(8,128)S(1)} custom-call(s32[7]{0:T(128)S(1)} %stack.61.place_ref, f32[8,9,2,16,128]{4,3,2,1,0:T(8,128)S(1)} %all-to-all-done.1.second_ref, f32[432,256]{1,0:T(8,128)S(1)} %bitcast.27, f32[432,256]{1,0:T(8,128)S(1)} %collective-permute-done.4.partner_ref, f32[3,256]{1,0:T(4,128)S(1)} %pad_maximum_fusion.1.gain_ref, ...), custom_call_target="tpu_custom_call" | custom-call | tf_op jit(solution)/shard_map/pallas_call | solution.py:25
  62.2 32.7 %all_to_all.20.parts_ref = f32[32,16,128]{2,1,0:T(8,128)S(1)} all-to-all(f32[32,16,128]{2,1,0:T(8,128)S(1)} %bitcast.23), channel_id=1, replica_groups=mesh['h'=2,'w'=2,'x'=4,'k'=8,'l'=2,'c'=2] {'k','l','c'}, dimensions={0} | all-to-all | bytes 524288 | tf_op jit(solution)/shard_map/all_to_all | solution.py:403
  94.8 0.1 shard_map.113
  95.0 0.0 copy-start
  95.0 0.0 copy-start.3
  95.0 0.0 copy-start.4
  95.0 20.1 %all_to_all.21.mine_ref = f32[8,16,16,128]{3,2,1,0:T(8,128)S(1)} all-to-all(f32[8,16,16,128]{3,2,1,0:T(8,128)S(1)} %shard_map.113), channel_id=1, replica_groups=mesh['h'=2,'w'=2,'x'=4,'k'=8,'l'=2,'c'=2] {'w','x'}, dimensions={0} | all-to-all | bytes 2097152 | tf_op jit(solution)/shard_map/all_to_all | solution.py:405
  115.1 2.0 %collective-permute-start.5 = (f32[8,16,16,128]{3,2,1,0:T(8,128)S(1)}, f32[8,16,16,128]{3,2,1,0:T(8,128)S(1)}, u32[]{:S(2)}, u32[]{:S(2)}) collective-permute-start(f32[8,16,16,128]{3,2,1,0:T(8,128)S(1)} %all_to_all.21.mine_ref), channel_id=1, source_target_pairs={{0,1},{1,0},{2,3},{3,2},{4,5},{5,4},{6,7},{7,6},{8,9},{9,8},{10,11... | collective-permute-start | bytes 3145736 | tf_op jit(solution)/shard_map/ppermute | solution.py:406
  117.1 0.0 copy-done
  117.1 0.0 copy-done.3
  117.1 0.7 shard_map.114.folded_ref
  117.8 1.8 %collective-permute-done.5.other_ref = f32[8,16,16,128]{3,2,1,0:T(8,128)S(1)} collective-permute-done((f32[8,16,16,128]{3,2,1,0:T(8,128)S(1)}, f32[8,16,16,128]{3,2,1,0:T(8,128)S(1)}, u32[]{:S(2)}, u32[]{:S(2)}) %collective-permute-start.5) | collective-permute-done | bytes 1048608 | tf_op jit(solution)/shard_map/ppermute | solution.py:406
  119.6 3.6 %shard_map.115 = (f32[64,256]{1,0:T(8,128)S(1)}, f32[64,256]{1,0:T(8,128)S(1)}) custom-call(s32[7]{0:T(128)S(1)} %stack.61.place_ref, f32[8,16,16,128]{3,2,1,0:T(8,128)S(1)} %all_to_all.21.mine_ref, f32[8,16,16,128]{3,2,1,0:T(8,128)S(1)} %collective-permute-done.5.other_ref, f32[3,256]{1,0:T(4,128)S(1)} %pad_maximum_fusion.1.gain_ref, ...), custom_call_target="tpu_custom_call" | custom-call | tf_op jit(solution)/shard_map/pallas_call | solution.py:25
  123.2 5.2 %collective-permute-start.6 = (f32[64,256]{1,0:T(8,128)S(1)}, f32[64,256]{1,0:T(8,128)S(1)}, u32[]{:S(2)}, u32[]{:S(2)}) collective-permute-start(f32[64,256]{1,0:T(8,128)S(1)} %get-tuple-element.17), channel_id=1, source_target_pairs={{0,16},{1,14},{2,52},{3,46},{4,92},{5,74},{6,120},{7,114},{8,154},... | collective-permute-start | bytes 196616 | tf_op jit(solution)/shard_map/ppermute | solution.py:422
  128.5 4.7 %collective-permute-start.7 = (f32[64,256]{1,0:T(8,128)S(1)}, f32[64,256]{1,0:T(8,128)S(1)}, u32[]{:S(2)}, u32[]{:S(2)}) collective-permute-start(f32[64,256]{1,0:T(8,128)S(1)} %get-tuple-element.18), channel_id=1, source_target_pairs={{0,17},{1,15},{2,53},{3,47},{4,93},{5,75},{6,121},{7,115},{8,155},... | collective-permute-start | bytes 196616 | tf_op jit(solution)/shard_map/ppermute | solution.py:423
  133.2 0.0 collective-permute-done.6
  133.2 11.7 %collective-permute-done.7 = f32[64,256]{1,0:T(8,128)S(1)} collective-permute-done((f32[64,256]{1,0:T(8,128)S(1)}, f32[64,256]{1,0:T(8,128)S(1)}, u32[]{:S(2)}, u32[]{:S(2)}) %collective-permute-start.7) | collective-permute-done | bytes 65568 | tf_op jit(solution)/shard_map/ppermute | solution.py:423
  144.9 0.7 pad_maximum_fusion
  (11 shorter events, 0.1 us)
Async XLA Ops:
  0.0 0.9 copy-start.5
  2.1 5.2 %copy-start.1 = (f32[3,3,3,16,256]{4,3,2,1,0:T(8,128)S(1)}, f32[3,3,3,16,256]{4,3,2,1,0:T(8,128)}, u32[]{:S(2)}) copy-start(f32[3,3,3,16,256]{4,3,2,1,0:T(8,128)} %param.14) | copy-start | bytes 1327108
  2.1 10.3 %copy-start.9 = (s32[32]{0:T(128)S(1)}, s32[32]{0:T(128)}, u32[]{:S(2)}) copy-start(s32[32]{0:T(128)} %param.12) | copy-start | bytes 388
  2.1 10.6 %copy-start.6 = (f32[256]{0:T(256)S(1)}, f32[256]{0:T(256)}, u32[]{:S(2)}) copy-start(f32[256]{0:T(256)} %param.17) | copy-start | bytes 3076
  2.1 10.6 %copy-start.7 = (f32[256]{0:T(256)S(1)}, f32[256]{0:T(256)}, u32[]{:S(2)}) copy-start(f32[256]{0:T(256)} %param.15) | copy-start | bytes 3076
  2.1 10.6 %copy-start.8 = (f32[256]{0:T(256)S(1)}, f32[256]{0:T(256)}, u32[]{:S(2)}) copy-start(f32[256]{0:T(256)} %param.13) | copy-start | bytes 3076
  2.1 20.9 %all-to-all-start = ((f32[8,256,128]{2,1,0:T(8,128)}), f32[8,256,128]{2,1,0:T(8,128)S(1)}, u32[]{:S(2)}, u32[]{:S(2)}) async-start(f32[8,256,128]{2,1,0:T(8,128)} %shard_map.109), calls=%async_computation | async-start | bytes 2097152 | tf_op jit(solution)/shard_map/all_to_all | solution.py:350
  7.3 13.5 %collective-permute-start = (f32[432,256]{1,0:T(8,128)S(1)}, f32[432,256]{1,0:T(8,128)S(1)}, u32[]{:S(2)}, u32[]{:S(2)}) collective-permute-start(f32[432,256]{1,0:T(8,128)S(1)} %bitcast.24), channel_id=1, source_target_pairs={{0,384},{128,256},{256,128},{384,0},{1,385},{129,257},{257,129},{3... | collective-permute-start | bytes 1327112 | tf_op jit(solution)/shard_map/ppermute | solution.py:343
  25.4 7.7 %collective-permute-start.1 = (f32[8,2,16,128]{3,2,1,0:T(8,128)S(1)}, f32[8,2,16,128]{3,2,1,0:T(8,128)S(1)}, u32[]{:S(2)}, u32[]{:S(2)}) collective-permute-start(f32[8,2,16,128]{3,2,1,0:T(8,128)S(1)} %get-tuple-element.13), channel_id=1, source_target_pairs={{0,1},{1,2},{2,3},{3,4},{4,5},{5,6},{6,7},{7,8},{8,9},{9,10},{10,1... | collective-permute-start | bytes 393224 | tf_op jit(solution)/shard_map/ppermute | solution.py:377
  25.4 5.8 %collective-permute-start.2 = (f32[2,2,16,128]{3,2,1,0:T(8,128)S(1)}, f32[2,2,16,128]{3,2,1,0:T(8,128)S(1)}, u32[]{:S(2)}, u32[]{:S(2)}) collective-permute-start(f32[2,2,16,128]{3,2,1,0:T(8,128)S(1)} %get-tuple-element.14), channel_id=1, source_target_pairs={{0,384},{128,256},{1,385},{129,257},{2,386},{130,258},{3,387},{131... | collective-permute-start | bytes 98312 | tf_op jit(solution)/shard_map/ppermute | solution.py:375
  26.7 6.4 %collective-permute-start.3 = (f32[2,2,16,128]{3,2,1,0:T(8,128)S(1)}, f32[2,2,16,128]{3,2,1,0:T(8,128)S(1)}, u32[]{:S(2)}, u32[]{:S(2)}) collective-permute-start(f32[2,2,16,128]{3,2,1,0:T(8,128)S(1)} %get-tuple-element.15), channel_id=1, source_target_pairs={{0,385},{1,386},{2,387},{3,388},{4,389},{5,390},{6,391},{7,392},{8... | collective-permute-start | bytes 98312 | tf_op jit(solution)/shard_map/ppermute | solution.py:376
  34.8 5.8 %copy-start.2 = (f32[3,3,3,16,256]{4,3,2,1,0:T(8,128)S(1)}, f32[3,3,3,16,256]{4,3,2,1,0:T(8,128)}, u32[]{:S(2)}) copy-start(f32[3,3,3,16,256]{4,3,2,1,0:T(8,128)} %param.16) | copy-start | bytes 1327108
  34.8 23.9 %all-to-all-start.1 = ((f32[8,9,2,16,128]{4,3,2,1,0:T(8,128)}), f32[8,9,2,16,128]{4,3,2,1,0:T(8,128)S(1)}, u32[]{:S(2)}, u32[]{:S(2)}) async-start(f32[8,9,2,16,128]{4,3,2,1,0:T(8,128)} %shard_map.111), calls=%async_computation.1 | async-start | bytes 2359296 | tf_op jit(solution)/shard_map/all_to_all | solution.py:389
  40.6 14.5 %collective-permute-start.4 = (f32[432,256]{1,0:T(8,128)S(1)}, f32[432,256]{1,0:T(8,128)S(1)}, u32[]{:S(2)}, u32[]{:S(2)}) collective-permute-start(f32[432,256]{1,0:T(8,128)S(1)} %bitcast.26), channel_id=1, source_target_pairs={{0,384},{128,256},{256,128},{384,0},{1,385},{129,257},{257,129},{3... | collective-permute-start | bytes 1327112 | tf_op jit(solution)/shard_map/ppermute | solution.py:344
  95.0 22.1 %copy-start = (f32[2,256,256]{2,1,0:T(8,128)S(1)}, f32[2,256,256]{2,1,0:T(8,128)}, u32[]{:S(2)}) copy-start(f32[2,256,256]{2,1,0:T(8,128)} %qk_ref.1) | copy-start | bytes 1572868
  95.0 22.1 %copy-start.3 = (f32[256,256]{1,0:T(8,128)S(1)}, f32[256,256]{1,0:T(8,128)}, u32[]{:S(2)}) copy-start(f32[256,256]{1,0:T(8,128)} %value_ref.1) | copy-start | bytes 786436
  95.0 22.1 %copy-start.4 = (f32[256,256]{1,0:T(8,128)S(1)}, f32[256,256]{1,0:T(8,128)}, u32[]{:S(2)}) copy-start(f32[256,256]{1,0:T(8,128)} %proj_ref.1) | copy-start | bytes 786436
  115.1 4.5 %collective-permute-start.5 = (f32[8,16,16,128]{3,2,1,0:T(8,128)S(1)}, f32[8,16,16,128]{3,2,1,0:T(8,128)S(1)}, u32[]{:S(2)}, u32[]{:S(2)}) collective-permute-start(f32[8,16,16,128]{3,2,1,0:T(8,128)S(1)} %all_to_all.21.mine_ref), channel_id=1, source_target_pairs={{0,1},{1,0},{2,3},{3,2},{4,5},{5,4},{6,7},{7,6},{8,9},{9,8},{10,11... | collective-permute-start | bytes 3145736 | tf_op jit(solution)/shard_map/ppermute | solution.py:406
  123.2 9.9 %collective-permute-start.6 = (f32[64,256]{1,0:T(8,128)S(1)}, f32[64,256]{1,0:T(8,128)S(1)}, u32[]{:S(2)}, u32[]{:S(2)}) collective-permute-start(f32[64,256]{1,0:T(8,128)S(1)} %get-tuple-element.17), channel_id=1, source_target_pairs={{0,16},{1,14},{2,52},{3,46},{4,92},{5,74},{6,120},{7,114},{8,154},... | collective-permute-start | bytes 196616 | tf_op jit(solution)/shard_map/ppermute | solution.py:422
  128.5 16.4 %collective-permute-start.7 = (f32[64,256]{1,0:T(8,128)S(1)}, f32[64,256]{1,0:T(8,128)S(1)}, u32[]{:S(2)}, u32[]{:S(2)}) collective-permute-start(f32[64,256]{1,0:T(8,128)S(1)} %get-tuple-element.18), channel_id=1, source_target_pairs={{0,17},{1,15},{2,53},{3,47},{4,93},{5,75},{6,121},{7,115},{8,155},... | collective-permute-start | bytes 196616 | tf_op jit(solution)/shard_map/ppermute | solution.py:423

commit v7 on v6

--- a/solution.py
+++ b/solution.py
@@ -87,29 +87,18 @@
     return rows
 
 
-def taps_shifted(product):
-    _, _, row = lanes()
-    first_row = row == 0
-    result = []
-    for a in range(3):
-        rows = row_taps(product, a)
-        stay = rows[2] + jnp.where(first_row, 0.0, pltpu.roll(rows[1], 32, 1))
-        go = rows[0] + jnp.where(first_row, pltpu.roll(rows[1], 96, 1), 0.0)
-        result.append(jnp.concatenate([stay, go], axis=0))
-    return result
-
-
 def taps(product, adjacent):
     _, _, row = lanes()
     first_row = row == 0
     result = []
     for a in range(3):
-        rows = row_taps(product, a)
-        cross = jnp.where(first_row, rows[0], rows[2])
-        cross = jnp.where(first_row, pltpu.roll(cross, 96, 1), pltpu.roll(cross, 32, 1))
-        own = rows[1] + jnp.where(adjacent, cross, 0.0)
-        leave = jnp.where(first_row, rows[2], rows[0])
-        result.append(jnp.concatenate([own, leave], axis=0))
+        above, same, below = row_taps(product, a)
+        if adjacent is not None:
+            below = jnp.where(first_row | adjacent, below, 0.0)
+            above = jnp.where(first_row & ~adjacent, 0.0, above)
+        stay = below + jnp.where(first_row, 0.0, pltpu.roll(same, 32, 1))
+        go = above + jnp.where(first_row, pltpu.roll(same, 96, 1), 0.0)
+        result.append(jnp.concatenate([stay, go], axis=0))
     return result
 
 
@@ -160,7 +149,7 @@
         for g in range(2):
             product_ref[g] = dot3(high_ref[g], low_ref[g], high, low)
         for side in range(2):
-            now = [taps_shifted(product_ref[g, :, 128 * side : 128 * side + 128]) for g in range(2)]
+            now = [taps(product_ref[g, :, 128 * side : 128 * side + 128], None) for g in range(2)]
             finish(2 * p + side, now, before)
             before = now
         return before
@@ -196,11 +185,9 @@
 
 def conv2_kernel(
     place_ref, second_ref, weight_ref, partner_ref, gain_ref, mask_ref, kept_ref,
-    out_ref, high_ref, low_ref, product_ref,
+    stay_ref, go_ref, high_ref, low_ref, product_ref,
 ):
-    lane, _, row = lanes()
-    low_half, first_row = lane < 64, row == 0
-    adjacent = place_ref[6] != 0
+    adjacent = jnp.full((16, 128), place_ref[6], jnp.int32) != 0
     gain = column(gain_ref[1:2])
     half = place_ref[0]
     for q in range(TILES + 1):
@@ -221,22 +208,32 @@
             now = taps(product_ref[:, 128 * (q + 1) : 128 * (q + 2)], adjacent)
             at = TILES * half + q
             done = in_time(now, before, mask_ref[0, pl.ds(at, 1)], mask_ref[1, pl.ds(at, 1)])
-            own, leave = done[:16], done[16:]
-            here = jnp.where(first_row, pltpu.roll(own, 96, 1), leave) + kept_ref[q, slot]
-            above = jnp.where(first_row, leave, pltpu.roll(own, 32, 1))
-            out_ref[q, slot] = jnp.where(low_half, here, pltpu.roll(above, 64, 1))
-            out_ref[q + TILES, slot] = jnp.where(low_half, pltpu.roll(here, 64, 1), above)
+            stay_ref[q, slot] = done[:16]
+            go_ref[q, slot] = done[16:] + kept_ref[q, slot]
             before = now
 
 
-def join2_kernel(parts_ref, out_ref):
+def join2_kernel(stay_ref, arrived_ref, out_ref):
     lane, _, _ = lanes()
     low_half = lane < 64
-    for p in range(16):
-        outer = jnp.where(low_half, parts_ref[2 * p], parts_ref[(2 * p + 2) % SPACE])
-        tile = outer + pltpu.roll(parts_ref[2 * p + 1], 64, 1)
+    for q in range(TILES):
+        first, second = (stay_ref[q, slot] + arrived_ref[q, slot] for slot in range(2))
+        out_ref[q] = jnp.where(low_half, first, pltpu.roll(second, 64, 1))
+        out_ref[q + TILES] = jnp.where(low_half, pltpu.roll(first, 64, 1), second)
+
+
+def pair_kernel(parts_ref, out_ref):
+    lane, _, _ = lanes()
+    low_half = lane < 64
+    for m in range(8):
+        first, second = parts_ref[2 * m], parts_ref[2 * m + 1]
+        tiles = (
+            jnp.where(low_half, first, pltpu.roll(second, 64, 1)),
+            jnp.where(low_half, pltpu.roll(first, 64, 1), second),
+        )
         for i in range(W * X):
-            out_ref[i, p] = tile
+            for slot in range(2):
+                out_ref[i, m, slot] = tiles[slot]
 
 
 def fold_kernel(qk_ref, value_ref, proj_ref, out_ref):
@@ -256,21 +253,33 @@
     gain = column(gain_ref[2:3])
     half, core = place_ref[0], place_ref[3]
 
-    def gathered(p):
+    def gathered(read):
         blocks = []
         for slot in range(2):
             for u in range(W):
                 source = X * jnp.where(half == slot, u, 1 - u)
-                for x in range(X):
-                    mine, other = mine_ref[source + x, p], other_ref[source + x, p]
-                    blocks.append(jnp.where(core == slot, mine, other))
+                blocks += [read(source + x, slot) for x in range(X)]
         return jnp.concatenate(blocks, axis=0)
 
-    rows = gathered(place_ref[5]).T
+    def of_core(which, m):
+        return gathered(
+            lambda source, slot: jnp.where(
+                core == which, mine_ref[source, m, slot], other_ref[source, m, slot]
+            )
+        )
+
+    even_at = place_ref[5]
+    odd_at = (even_at + 1) & (K * L - 1)
+    even, odd = of_core(1, even_at >> 1), of_core(0, odd_at >> 1)
+    even = jnp.where((even_at & 1) == 0, even, pltpu.roll(even, 64, 1))
+    odd = jnp.where((odd_at & 1) == 1, odd, pltpu.roll(odd, 64, 1))
+    low_half = lax.broadcasted_iota(jnp.int32, even.shape, 1) < 64
+    rows = jnp.where(low_half, even, odd).T
     normed = rows * lax.rsqrt(jnp.mean(rows * rows, axis=1, keepdims=True) + epsilon) * gain_ref[2:3]
     queries = dot3_stacked(*split(normed), *split(folded_ref[0]))
     for p in range(16):
-        tile = gathered(p)
+        ref, m = (mine_ref, p) if p < 8 else (other_ref, p - 8)
+        tile = gathered(lambda source, slot: ref[source, m, slot])
         normed = tile * lax.rsqrt(jnp.mean(tile * tile, axis=0, keepdims=True) + epsilon) * gain
         high, low = split(normed)
         high_ref[:, 128 * p : 128 * p + 128] = high
@@ -374,7 +383,8 @@
     ]
     last = lax.ppermute(last, ("h", "w"), mirror[: H * W // 2])
     last_arrived = lax.ppermute(last_onward, ("h", "w") + space, onto_next)
-    arrived = lax.ppermute(onward, space, [(i, (i + 1) % SPACE) for i in range(SPACE)])
+    ring = [(i, (i + 1) % SPACE) for i in range(SPACE)]
+    arrived = lax.ppermute(onward, space, ring)
     second = call(
         join1_kernel,
         shape(W * X, TILES + 1, 2, 16, 128),
@@ -387,9 +397,9 @@
         smem=1,
     )
     second = lax.all_to_all(second, ("w", "x"), 0, 0)
-    parts = call(
+    stay, go = call(
         conv2_kernel,
-        shape(K * L, CORES, 16, 128),
+        [shape(TILES, 2, 16, 128)] * 2,
         [pltpu.VMEM((256, 1152), bf16)] * 2 + [pltpu.VMEM((432, 1152), f32)],
         place,
         second,
@@ -400,8 +410,10 @@
         kept,
         smem=1,
     )
-    parts = lax.all_to_all(parts.reshape(SPACE, 16, 128), space, 0, 0)
-    frame = call(join2_kernel, shape(W * X, 16, 16, 128), [], parts)
+    arrived = lax.ppermute(go, space, ring)
+    parts = call(join2_kernel, shape(K * L, 16, 128), [], stay, arrived)
+    parts = lax.all_to_all(parts, ("k", "l"), 0, 0)
+    frame = call(pair_kernel, shape(W * X, 8, 2, 16, 128), [], parts)
     mine = lax.all_to_all(frame, ("w", "x"), 0, 0)
     other = lax.ppermute(mine, "c", swap)
     same_core, other_core = call(

time: 146 us -> 142 us (0.973)
  the two profiles are of different devices: /device:TPU:80 before, /device:TPU:48 now
where the time goes in v7:
time: 142 us; the launch traced here: 141 us
  waiting for transfers between devices  47.7 us (34%)
  blocking collectives  42.9 us (30%)
  starting transfers between devices  33.2 us (23%)
  Pallas kernels  13 us (9%)
  local copies, waits for them, and re-layouts  2.47 us (2%)
    all_to_all x1, blocking collectives, body(): parts = lax.all_to_all(parts, ('k', 'l'), 0, 0)  27.7 us
    all_to_all x1, blocking collectives, body(): mine = lax.all_to_all(frame, ('w', 'x'), 0, 0)  15.2 us
    pallas_call x8, Pallas kernels, call(): pl.pallas_call(kernel, out_shape=out_shape, in_specs=[pl.BlockSpec(memory...  13 us
    ppermute x1, waiting for transfers between devices, body(): partner_2 = lax.ppermute(weight_2, ('h', 'w'), mirror)  11.9 us
    ppermute x1, waiting for transfers between devices, body(): other_core = lax.ppermute(other_core, ('w', 'x', 'k', 'l', 'c'), route_1)  10.5 us
    ppermute x1, waiting for transfers between devices, body(): partner_1 = lax.ppermute(weight_1, ('h', 'w'), mirror)  8.06 us
    ppermute x1, starting transfers between devices, body(): other_core = lax.ppermute(other_core, ('w', 'x', 'k', 'l', 'c'), route_1)  6.78 us
    all_to_all x1, starting transfers between devices, body(): second = lax.all_to_all(second, ('w', 'x'), 0, 0)  5.79 us
  transfers between devices with their start and end apart: 11, of which 9 were waited for; matrix products, arithmetic and copies ran while one was open for 1% of the time, Pallas kernels for 0%

profile of v7, /device:TPU:48, one launch (start us, length us, event | category | flops | bytes accessed | tf_op | source)
XLA Modules:
  0.0 141.0 jit_solution(12105311862943017643)
XLA Ops:
  0.0 0.9 copy-done.5
  0.9 1.2 shard_map.109
  2.1 0.0 copy-start.8
  2.1 5.2 %all-to-all-start = ((f32[8,256,128]{2,1,0:T(8,128)}), f32[8,256,128]{2,1,0:T(8,128)S(1)}, u32[]{:S(2)}, u32[]{:S(2)}) async-start(f32[8,256,128]{2,1,0:T(8,128)} %shard_map.109), calls=%async_computation | async-start | bytes 2097152 | tf_op jit(solution)/shard_map/all_to_all | solution.py:359
  7.3 0.0 copy-done.1
  7.3 3.1 %collective-permute-start = (f32[432,256]{1,0:T(8,128)S(1)}, f32[432,256]{1,0:T(8,128)S(1)}, u32[]{:S(2)}, u32[]{:S(2)}) collective-permute-start(f32[432,256]{1,0:T(8,128)S(1)} %bitcast.22), channel_id=1, source_target_pairs={{0,384},{128,256},{256,128},{384,0},{1,385},{129,257},{257,129},{3... | collective-permute-start | bytes 1327112 | tf_op jit(solution)/shard_map/ppermute | solution.py:352
  10.4 1.3 dynamic_slice.3
  12.4 0.0 copy-done.9
  12.4 0.1 compare_bitcast_fusion.1
  12.5 0.1 broadcast_in_dim.4
  12.5 0.1 reshape_reshape.3
  12.6 0.1 stack.61.place_ref
  12.7 0.0 copy-done.6
  12.7 0.0 copy-done.7
  12.7 0.0 copy-done.8
  12.7 8.1 %collective-permute-done.partner_ref = f32[432,256]{1,0:T(8,128)S(1)} collective-permute-done((f32[432,256]{1,0:T(8,128)S(1)}, f32[432,256]{1,0:T(8,128)S(1)}, u32[]{:S(2)}, u32[]{:S(2)}) %collective-permute-start) | collective-permute-done | bytes 442400 | tf_op jit(solution)/shard_map/ppermute | solution.py:352
  20.8 2.2 %all-to-all-done = f32[8,256,128]{2,1,0:T(8,128)S(1)} async-done(((f32[8,256,128]{2,1,0:T(8,128)}), f32[8,256,128]{2,1,0:T(8,128)S(1)}, u32[]{:S(2)}, u32[]{:S(2)}) %all-to-all-start) | async-done | bytes 1048608 | tf_op jit(solution)/shard_map/all_to_all | solution.py:359
  23.0 2.4 %shard_map.110 = (f32[8,2,16,128]{3,2,1,0:T(8,128)S(1)}, f32[8,2,16,128]{3,2,1,0:T(8,128)S(1)}, f32[2,2,16,128]{3,2,1,0:T(8,128)S(1)}, f32[2,2,16,128]{3,2,1,0:T(8,128)S(1)}, f32[8,2,16,128]{3,2,1,0:T(8,128)S(1)}) custom-call(s32[7]{0:T(128)S(1)} %stack.61.place_ref, f32[8,4,4,16,128]{4,3,2,1,0:T(8,128)S(1)} %bitcast.21, f32[432,256]{1,0:T(8,128)S(1)} %bitcast.23, ...), custom_call_target="tpu_custom_call" | custom-call | tf_op jit(solution)/shard_map/pallas_call | solution.py:25
  25.4 0.0 collective-permute-start.1
  25.4 1.3 collective-permute-start.2
  26.7 1.3 collective-permute-start.3
  28.0 3.2 %collective-permute-done.2.last_ref = f32[2,2,16,128]{3,2,1,0:T(8,128)S(1)} collective-permute-done((f32[2,2,16,128]{3,2,1,0:T(8,128)S(1)}, f32[2,2,16,128]{3,2,1,0:T(8,128)S(1)}, u32[]{:S(2)}, u32[]{:S(2)}) %collective-permute-start.2) | collective-permute-done | bytes 32800 | tf_op jit(solution)/shard_map/ppermute | solution.py:384
  31.3 1.9 %collective-permute-done.3.last_arrived_ref = f32[2,2,16,128]{3,2,1,0:T(8,128)S(1)} collective-permute-done((f32[2,2,16,128]{3,2,1,0:T(8,128)S(1)}, f32[2,2,16,128]{3,2,1,0:T(8,128)S(1)}, u32[]{:S(2)}, u32[]{:S(2)}) %collective-permute-start.3) | collective-permute-done | bytes 32800 | tf_op jit(solution)/shard_map/ppermute | solution.py:385
  33.1 0.0 collective-permute-done.1.arrived_ref
  33.1 1.7 %shard_map.111 = f32[8,9,2,16,128]{4,3,2,1,0:T(8,128)} custom-call(s32[7]{0:T(128)S(1)} %stack.61.place_ref, f32[8,2,16,128]{3,2,1,0:T(8,128)S(1)} %get-tuple-element.14.own_ref, f32[8,2,16,128]{3,2,1,0:T(8,128)S(1)} %collective-permute-done.1.arrived_ref, f32[2,2,16,128]{3,2,1,0:T(8,128)S(1)} %collective-permute-done.2.last_ref, ...), custom_call_target="tpu_custom_call" | custom-call | tf_op jit(solution)/shard_map/pallas_call | solution.py:25
  34.8 5.8 %all-to-all-start.1 = ((f32[8,9,2,16,128]{4,3,2,1,0:T(8,128)}), f32[8,9,2,16,128]{4,3,2,1,0:T(8,128)S(1)}, u32[]{:S(2)}, u32[]{:S(2)}) async-start(f32[8,9,2,16,128]{4,3,2,1,0:T(8,128)} %shard_map.111), calls=%async_computation.1 | async-start | bytes 2359296 | tf_op jit(solution)/shard_map/all_to_all | solution.py:399
  40.6 2.6 %collective-permute-start.4 = (f32[432,256]{1,0:T(8,128)S(1)}, f32[432,256]{1,0:T(8,128)S(1)}, u32[]{:S(2)}, u32[]{:S(2)}) collective-permute-start(f32[432,256]{1,0:T(8,128)S(1)} %bitcast.24), channel_id=1, source_target_pairs={{0,384},{128,256},{256,128},{384,0},{1,385},{129,257},{257,129},{3... | collective-permute-start | bytes 1327112 | tf_op jit(solution)/shard_map/ppermute | solution.py:353
  43.2 11.9 %collective-permute-done.4.partner_ref = f32[432,256]{1,0:T(8,128)S(1)} collective-permute-done((f32[432,256]{1,0:T(8,128)S(1)}, f32[432,256]{1,0:T(8,128)S(1)}, u32[]{:S(2)}, u32[]{:S(2)}) %collective-permute-start.4) | collective-permute-done | bytes 442400 | tf_op jit(solution)/shard_map/ppermute | solution.py:353
  55.2 3.6 %all-to-all-done.1.second_ref = f32[8,9,2,16,128]{4,3,2,1,0:T(8,128)S(1)} async-done(((f32[8,9,2,16,128]{4,3,2,1,0:T(8,128)}), f32[8,9,2,16,128]{4,3,2,1,0:T(8,128)S(1)}, u32[]{:S(2)}, u32[]{:S(2)}) %all-to-all-start.1) | async-done | bytes 1179680 | tf_op jit(solution)/shard_map/all_to_all | solution.py:399
  58.8 3.2 %shard_map.112 = (f32[8,2,16,128]{3,2,1,0:T(8,128)S(1)}, f32[8,2,16,128]{3,2,1,0:T(8,128)S(1)}) custom-call(s32[7]{0:T(128)S(1)} %stack.61.place_ref, f32[8,9,2,16,128]{4,3,2,1,0:T(8,128)S(1)} %all-to-all-done.1.second_ref, f32[432,256]{1,0:T(8,128)S(1)} %bitcast.25, f32[432,256]{1,0:T(8,128)S(1)} %collective-permute-done.4.partner_ref, ...), custom_call_target="tpu_custom_call" | custom-call | tf_op jit(solution)/shard_map/pallas_call | solution.py:25
  62.0 0.0 collective-permute-start.5
  62.0 4.4 %collective-permute-done.5.arrived_ref = f32[8,2,16,128]{3,2,1,0:T(8,128)S(1)} collective-permute-done((f32[8,2,16,128]{3,2,1,0:T(8,128)S(1)}, f32[8,2,16,128]{3,2,1,0:T(8,128)S(1)}, u32[]{:S(2)}, u32[]{:S(2)}) %collective-permute-start.5) | collective-permute-done | bytes 131104 | tf_op jit(solution)/shard_map/ppermute | solution.py:413
  66.4 0.1 shard_map.113
  66.5 27.7 %all_to_all.20.parts_ref = f32[16,16,128]{2,1,0:T(8,128)S(1)} all-to-all(f32[16,16,128]{2,1,0:T(8,128)S(1)} %shard_map.113), channel_id=1, replica_groups=mesh['h'=2,'w'=2,'x'=4,'k'=8,'l'=2,'c'=2] {'k','l'}, dimensions={0} | all-to-all | bytes 262144 | tf_op jit(solution)/shard_map/all_to_all | solution.py:415
  94.2 0.1 shard_map.114
  94.3 0.0 copy-start
  94.4 0.0 copy-start.3
  94.4 0.0 copy-start.4
  94.4 15.2 %all_to_all.21.mine_ref = f32[8,8,2,16,128]{4,3,2,1,0:T(8,128)S(1)} all-to-all(f32[8,8,2,16,128]{4,3,2,1,0:T(8,128)S(1)} %shard_map.114), channel_id=1, replica_groups=mesh['h'=2,'w'=2,'x'=4,'k'=8,'l'=2,'c'=2] {'w','x'}, dimensions={0} | all-to-all | bytes 2097152 | tf_op jit(solution)/shard_map/all_to_all | solution.py:417
  109.6 1.9 %collective-permute-start.6 = (f32[8,8,2,16,128]{4,3,2,1,0:T(8,128)S(1)}, f32[8,8,2,16,128]{4,3,2,1,0:T(8,128)S(1)}, u32[]{:S(2)}, u32[]{:S(2)}) collective-permute-start(f32[8,8,2,16,128]{4,3,2,1,0:T(8,128)S(1)} %all_to_all.21.mine_ref), channel_id=1, source_target_pairs={{0,1},{1,0},{2,3},{3,2},{4,5},{5,4},{6,7},{7,6},{8,9},{9,8},{10,11... | collective-permute-start | bytes 3145736 | tf_op jit(solution)/shard_map/ppermute | solution.py:418
  111.5 0.7 shard_map.115.folded_ref
  112.2 1.9 %collective-permute-done.6.other_ref = f32[8,8,2,16,128]{4,3,2,1,0:T(8,128)S(1)} collective-permute-done((f32[8,8,2,16,128]{4,3,2,1,0:T(8,128)S(1)}, f32[8,8,2,16,128]{4,3,2,1,0:T(8,128)S(1)}, u32[]{:S(2)}, u32[]{:S(2)}) %collective-permute-start.6) | collective-permute-done | bytes 1048608 | tf_op jit(solution)/shard_map/ppermute | solution.py:418
  114.1 3.6 %shard_map.116 = (f32[64,256]{1,0:T(8,128)S(1)}, f32[64,256]{1,0:T(8,128)S(1)}) custom-call(s32[7]{0:T(128)S(1)} %stack.61.place_ref, f32[8,8,2,16,128]{4,3,2,1,0:T(8,128)S(1)} %all_to_all.21.mine_ref, f32[8,8,2,16,128]{4,3,2,1,0:T(8,128)S(1)} %collective-permute-done.6.other_ref, f32[3,256]{1,0:T(4,128)S(1)} %pad_maximum_fusion.1.gain_ref, ...), custom_call_target="tpu_custom_call" | custom-call | tf_op jit(solution)/shard_map/pallas_call | solution.py:25
  117.7 5.3 %collective-permute-start.7 = (f32[64,256]{1,0:T(8,128)S(1)}, f32[64,256]{1,0:T(8,128)S(1)}, u32[]{:S(2)}, u32[]{:S(2)}) collective-permute-start(f32[64,256]{1,0:T(8,128)S(1)} %get-tuple-element.21), channel_id=1, source_target_pairs={{0,16},{1,14},{2,52},{3,46},{4,92},{5,74},{6,120},{7,114},{8,154},... | collective-permute-start | bytes 196616 | tf_op jit(solution)/shard_map/ppermute | solution.py:434
  123.0 6.8 %collective-permute-start.8 = (f32[64,256]{1,0:T(8,128)S(1)}, f32[64,256]{1,0:T(8,128)S(1)}, u32[]{:S(2)}, u32[]{:S(2)}) collective-permute-start(f32[64,256]{1,0:T(8,128)S(1)} %get-tuple-element.22), channel_id=1, source_target_pairs={{0,17},{1,15},{2,53},{3,47},{4,93},{5,75},{6,121},{7,115},{8,155},... | collective-permute-start | bytes 196616 | tf_op jit(solution)/shard_map/ppermute | solution.py:435
  129.8 0.0 collective-permute-done.7
  129.8 10.5 %collective-permute-done.8 = f32[64,256]{1,0:T(8,128)S(1)} collective-permute-done((f32[64,256]{1,0:T(8,128)S(1)}, f32[64,256]{1,0:T(8,128)S(1)}, u32[]{:S(2)}, u32[]{:S(2)}) %collective-permute-start.8) | collective-permute-done | bytes 65568 | tf_op jit(solution)/shard_map/ppermute | solution.py:435
  140.3 0.7 pad_maximum_fusion
  (14 shorter events, 0.1 us)
Async XLA Ops:
  0.0 0.9 copy-start.5
  2.1 5.2 %copy-start.1 = (f32[3,3,3,16,256]{4,3,2,1,0:T(8,128)S(1)}, f32[3,3,3,16,256]{4,3,2,1,0:T(8,128)}, u32[]{:S(2)}) copy-start(f32[3,3,3,16,256]{4,3,2,1,0:T(8,128)} %param.14) | copy-start | bytes 1327108
  2.1 10.3 %copy-start.9 = (s32[32]{0:T(128)S(1)}, s32[32]{0:T(128)}, u32[]{:S(2)}) copy-start(s32[32]{0:T(128)} %param.12) | copy-start | bytes 388
  2.1 10.6 %copy-start.6 = (f32[256]{0:T(256)S(1)}, f32[256]{0:T(256)}, u32[]{:S(2)}) copy-start(f32[256]{0:T(256)} %param.17) | copy-start | bytes 3076
  2.1 10.6 %copy-start.7 = (f32[256]{0:T(256)S(1)}, f32[256]{0:T(256)}, u32[]{:S(2)}) copy-start(f32[256]{0:T(256)} %param.15) | copy-start | bytes 3076
  2.1 10.6 %copy-start.8 = (f32[256]{0:T(256)S(1)}, f32[256]{0:T(256)}, u32[]{:S(2)}) copy-start(f32[256]{0:T(256)} %param.13) | copy-start | bytes 3076
  2.1 20.9 %all-to-all-start = ((f32[8,256,128]{2,1,0:T(8,128)}), f32[8,256,128]{2,1,0:T(8,128)S(1)}, u32[]{:S(2)}, u32[]{:S(2)}) async-start(f32[8,256,128]{2,1,0:T(8,128)} %shard_map.109), calls=%async_computation | async-start | bytes 2097152 | tf_op jit(solution)/shard_map/all_to_all | solution.py:359
  7.3 13.5 %collective-permute-start = (f32[432,256]{1,0:T(8,128)S(1)}, f32[432,256]{1,0:T(8,128)S(1)}, u32[]{:S(2)}, u32[]{:S(2)}) collective-permute-start(f32[432,256]{1,0:T(8,128)S(1)} %bitcast.22), channel_id=1, source_target_pairs={{0,384},{128,256},{256,128},{384,0},{1,385},{129,257},{257,129},{3... | collective-permute-start | bytes 1327112 | tf_op jit(solution)/shard_map/ppermute | solution.py:352
  25.4 7.7 %collective-permute-start.1 = (f32[8,2,16,128]{3,2,1,0:T(8,128)S(1)}, f32[8,2,16,128]{3,2,1,0:T(8,128)S(1)}, u32[]{:S(2)}, u32[]{:S(2)}) collective-permute-start(f32[8,2,16,128]{3,2,1,0:T(8,128)S(1)} %get-tuple-element.15), channel_id=1, source_target_pairs={{0,1},{1,2},{2,3},{3,4},{4,5},{5,6},{6,7},{7,8},{8,9},{9,10},{10,1... | collective-permute-start | bytes 393224 | tf_op jit(solution)/shard_map/ppermute | solution.py:387
  25.4 5.8 %collective-permute-start.2 = (f32[2,2,16,128]{3,2,1,0:T(8,128)S(1)}, f32[2,2,16,128]{3,2,1,0:T(8,128)S(1)}, u32[]{:S(2)}, u32[]{:S(2)}) collective-permute-start(f32[2,2,16,128]{3,2,1,0:T(8,128)S(1)} %get-tuple-element.16), channel_id=1, source_target_pairs={{0,384},{128,256},{1,385},{129,257},{2,386},{130,258},{3,387},{131... | collective-permute-start | bytes 98312 | tf_op jit(solution)/shard_map/ppermute | solution.py:384
  26.7 6.4 %collective-permute-start.3 = (f32[2,2,16,128]{3,2,1,0:T(8,128)S(1)}, f32[2,2,16,128]{3,2,1,0:T(8,128)S(1)}, u32[]{:S(2)}, u32[]{:S(2)}) collective-permute-start(f32[2,2,16,128]{3,2,1,0:T(8,128)S(1)} %get-tuple-element.17), channel_id=1, source_target_pairs={{0,385},{1,386},{2,387},{3,388},{4,389},{5,390},{6,391},{7,392},{8... | collective-permute-start | bytes 98312 | tf_op jit(solution)/shard_map/ppermute | solution.py:385
  34.8 5.8 %copy-start.2 = (f32[3,3,3,16,256]{4,3,2,1,0:T(8,128)S(1)}, f32[3,3,3,16,256]{4,3,2,1,0:T(8,128)}, u32[]{:S(2)}) copy-start(f32[3,3,3,16,256]{4,3,2,1,0:T(8,128)} %param.16) | copy-start | bytes 1327108
  34.8 23.9 %all-to-all-start.1 = ((f32[8,9,2,16,128]{4,3,2,1,0:T(8,128)}), f32[8,9,2,16,128]{4,3,2,1,0:T(8,128)S(1)}, u32[]{:S(2)}, u32[]{:S(2)}) async-start(f32[8,9,2,16,128]{4,3,2,1,0:T(8,128)} %shard_map.111), calls=%async_computation.1 | async-start | bytes 2359296 | tf_op jit(solution)/shard_map/all_to_all | solution.py:399
  40.6 14.5 %collective-permute-start.4 = (f32[432,256]{1,0:T(8,128)S(1)}, f32[432,256]{1,0:T(8,128)S(1)}, u32[]{:S(2)}, u32[]{:S(2)}) collective-permute-start(f32[432,256]{1,0:T(8,128)S(1)} %bitcast.24), channel_id=1, source_target_pairs={{0,384},{128,256},{256,128},{384,0},{1,385},{129,257},{257,129},{3... | collective-permute-start | bytes 1327112 | tf_op jit(solution)/shard_map/ppermute | solution.py:353
  62.0 4.4 %collective-permute-start.5 = (f32[8,2,16,128]{3,2,1,0:T(8,128)S(1)}, f32[8,2,16,128]{3,2,1,0:T(8,128)S(1)}, u32[]{:S(2)}, u32[]{:S(2)}) collective-permute-start(f32[8,2,16,128]{3,2,1,0:T(8,128)S(1)} %get-tuple-element.20), channel_id=1, source_target_pairs={{0,1},{1,2},{2,3},{3,4},{4,5},{5,6},{6,7},{7,8},{8,9},{9,10},{10,1... | collective-permute-start | bytes 393224 | tf_op jit(solution)/shard_map/ppermute | solution.py:413
  94.3 17.2 %copy-start = (f32[2,256,256]{2,1,0:T(8,128)S(1)}, f32[2,256,256]{2,1,0:T(8,128)}, u32[]{:S(2)}) copy-start(f32[2,256,256]{2,1,0:T(8,128)} %qk_ref.1) | copy-start | bytes 1572868
  94.4 17.2 %copy-start.3 = (f32[256,256]{1,0:T(8,128)S(1)}, f32[256,256]{1,0:T(8,128)}, u32[]{:S(2)}) copy-start(f32[256,256]{1,0:T(8,128)} %value_ref.1) | copy-start | bytes 786436
  94.4 17.2 %copy-start.4 = (f32[256,256]{1,0:T(8,128)S(1)}, f32[256,256]{1,0:T(8,128)}, u32[]{:S(2)}) copy-start(f32[256,256]{1,0:T(8,128)} %proj_ref.1) | copy-start | bytes 786436
  109.6 4.5 %collective-permute-start.6 = (f32[8,8,2,16,128]{4,3,2,1,0:T(8,128)S(1)}, f32[8,8,2,16,128]{4,3,2,1,0:T(8,128)S(1)}, u32[]{:S(2)}, u32[]{:S(2)}) collective-permute-start(f32[8,8,2,16,128]{4,3,2,1,0:T(8,128)S(1)} %all_to_all.21.mine_ref), channel_id=1, source_target_pairs={{0,1},{1,0},{2,3},{3,2},{4,5},{5,4},{6,7},{7,6},{8,9},{9,8},{10,11... | collective-permute-start | bytes 3145736 | tf_op jit(solution)/shard_map/ppermute | solution.py:418
  117.7 12.1 %collective-permute-start.7 = (f32[64,256]{1,0:T(8,128)S(1)}, f32[64,256]{1,0:T(8,128)S(1)}, u32[]{:S(2)}, u32[]{:S(2)}) collective-permute-start(f32[64,256]{1,0:T(8,128)S(1)} %get-tuple-element.21), channel_id=1, source_target_pairs={{0,16},{1,14},{2,52},{3,46},{4,92},{5,74},{6,120},{7,114},{8,154},... | collective-permute-start | bytes 196616 | tf_op jit(solution)/shard_map/ppermute | solution.py:434
  123.0 17.3 %collective-permute-start.8 = (f32[64,256]{1,0:T(8,128)S(1)}, f32[64,256]{1,0:T(8,128)S(1)}, u32[]{:S(2)}, u32[]{:S(2)}) collective-permute-start(f32[64,256]{1,0:T(8,128)S(1)} %get-tuple-element.22), channel_id=1, source_target_pairs={{0,17},{1,15},{2,53},{3,47},{4,93},{5,75},{6,121},{7,115},{8,155},... | collective-permute-start | bytes 196616 | tf_op jit(solution)/shard_map/ppermute | solution.py:435

commit v8 on v7

--- a/solution.py
+++ b/solution.py
@@ -115,7 +115,7 @@
 
 
 def conv1_kernel(
-    place_ref, video_ref, weight_ref, partner_ref, gain_ref, mask_ref,
+    place_ref, video_ref, weight_ref, partner_ref, gain_ref, mask_ref, _,
     own_ref, onward_ref, last_ref, last_onward_ref, kept_ref, high_ref, low_ref, product_ref,
 ):
     gain = column(gain_ref[0:1])
@@ -246,66 +246,78 @@
     )
 
 
-def attend_kernel(
-    place_ref, mine_ref, other_ref, gain_ref, folded_ref, same_ref, cross_ref,
-    high_ref, low_ref,
-):
+def gathered(place_ref, frame_ref, m):
+    blocks = []
+    for slot in range(2):
+        for u in range(W):
+            source = X * jnp.where(place_ref[0] == slot, u, 1 - u)
+            blocks += [frame_ref[source + x, m, slot] for x in range(X)]
+    return jnp.concatenate(blocks, axis=0)
+
+
+def attend(place_ref, frame_ref, gain_ref, queries, high_ref, low_ref):
     gain = column(gain_ref[2:3])
-    half, core = place_ref[0], place_ref[3]
-
-    def gathered(read):
-        blocks = []
-        for slot in range(2):
-            for u in range(W):
-                source = X * jnp.where(half == slot, u, 1 - u)
-                blocks += [read(source + x, slot) for x in range(X)]
-        return jnp.concatenate(blocks, axis=0)
-
-    def of_core(which, m):
-        return gathered(
-            lambda source, slot: jnp.where(
-                core == which, mine_ref[source, m, slot], other_ref[source, m, slot]
-            )
-        )
-
-    even_at = place_ref[5]
-    odd_at = (even_at + 1) & (K * L - 1)
-    even, odd = of_core(1, even_at >> 1), of_core(0, odd_at >> 1)
-    even = jnp.where((even_at & 1) == 0, even, pltpu.roll(even, 64, 1))
-    odd = jnp.where((odd_at & 1) == 1, odd, pltpu.roll(odd, 64, 1))
-    low_half = lax.broadcasted_iota(jnp.int32, even.shape, 1) < 64
-    rows = jnp.where(low_half, even, odd).T
+    for m in range(8):
+        tile = gathered(place_ref, frame_ref, m)
+        normed = tile * lax.rsqrt(jnp.mean(tile * tile, axis=0, keepdims=True) + epsilon) * gain
+        high, low = split(normed)
+        high_ref[:, 128 * m : 128 * m + 128] = high
+        low_ref[:, 128 * m : 128 * m + 128] = low
+    scores = dot3_stacked(*split(queries), high_ref[...], low_ref[...])
+    most = jnp.max(scores, axis=1, keepdims=True)
+    weights = jnp.exp(scores - most)
+    total = jnp.sum(weights, axis=1, keepdims=True)
+    return most, total, dot3_stacked(*split(weights), high_ref[...], low_ref[...], ((1,), (1,)))
+
+
+def attend_mine_kernel(
+    place_ref, frame_ref, gain_ref, folded_ref,
+    rows_ref, queries_ref, most_ref, total_ref, sum_ref, high_ref, low_ref,
+):
+    first_at, second_at = place_ref[4], place_ref[5]
+    first = gathered(place_ref, frame_ref, first_at >> 1)
+    second = gathered(place_ref, frame_ref, second_at >> 1)
+    first = jnp.where((first_at & 1) == 0, first, pltpu.roll(first, 64, 1))
+    second = jnp.where((second_at & 1) == 1, second, pltpu.roll(second, 64, 1))
+    low_half = lax.broadcasted_iota(jnp.int32, first.shape, 1) < 64
+    rows = jnp.where(low_half, first, second).T
     normed = rows * lax.rsqrt(jnp.mean(rows * rows, axis=1, keepdims=True) + epsilon) * gain_ref[2:3]
     queries = dot3_stacked(*split(normed), *split(folded_ref[0]))
-    for p in range(16):
-        ref, m = (mine_ref, p) if p < 8 else (other_ref, p - 8)
-        tile = gathered(lambda source, slot: ref[source, m, slot])
-        normed = tile * lax.rsqrt(jnp.mean(tile * tile, axis=0, keepdims=True) + epsilon) * gain
-        high, low = split(normed)
-        high_ref[:, 128 * p : 128 * p + 128] = high
-        low_ref[:, 128 * p : 128 * p + 128] = low
-    scores = dot3_stacked(*split(queries), high_ref[...], low_ref[...])
-    weights = jnp.exp(scores - jnp.max(scores, axis=1, keepdims=True))
-    total = jnp.sum(weights, axis=1, keepdims=True)
-    attended = dot3_stacked(*split(weights), high_ref[...], low_ref[...], ((1,), (1,))) / total
-    result = rows + dot3_stacked(*split(attended), *split(folded_ref[1]))
-    first_core = place_ref[4] == 0
-    same_ref[...] = jnp.where(first_core, result[:64], result[64:])
-    cross_ref[...] = jnp.where(first_core, result[64:], result[:64])
-
-
-AWAY = ((8, 7), (-7, 6), (-6, 5), (-5, 4), (-4, 3), (-3, 2), (-2, 1), (-1, 0))
+    rows_ref[...] = rows
+    queries_ref[...] = queries
+    most, total, sum_ref[...] = attend(place_ref, frame_ref, gain_ref, queries, high_ref, low_ref)
+    most_ref[...] = jnp.broadcast_to(most, (128, 128))
+    total_ref[...] = jnp.broadcast_to(total, (128, 128))
+
+
+def attend_other_kernel(
+    place_ref, frame_ref, gain_ref, folded_ref, rows_ref, queries_ref, most_ref, total_ref, sum_ref,
+    first_ref, second_ref, high_ref, low_ref,
+):
+    most, total, weighted = attend(
+        place_ref, frame_ref, gain_ref, queries_ref[...], high_ref, low_ref
+    )
+    most_before, total_before = most_ref[:, 0:1], total_ref[:, 0:1]
+    top = jnp.maximum(most, most_before)
+    now, before = jnp.exp(most - top), jnp.exp(most_before - top)
+    attended = (weighted * now + sum_ref[...] * before) / (total * now + total_before * before)
+    result = rows_ref[...] + dot3_stacked(*split(attended), *split(folded_ref[1]))
+    first_ref[...] = result[:64]
+    second_ref[...] = result[64:]
+
+
+AWAY = ((8, 7), (-6, -7), (6, 5), (-4, -5), (4, 3), (-2, -3), (2, 1), (0, -1))
 
 
 def offsets():
-    table = np.zeros((W * X, W * X, CORES), np.int32)
+    table = np.zeros((W * X, W * X, 2, 2), np.int32)
     for home in range(W * X):
         def hops(chip):
             across = abs(chip % X - home % X)
             return abs(chip // X - home // X) + min(across, X - across)
 
         for rank, chip in enumerate(sorted(range(W * X), key=hops)):
-            table[chip, home] = AWAY[rank]
+            table[chip, home] = AWAY[rank], AWAY[rank][::-1]
     return table % (K * L)
 
 
@@ -315,10 +327,10 @@
         for z in range(K * L):
             for c in range(CORES):
                 source = (i * K * L + z) * CORES + c
-                home, f = z % TILES, z // TILES
-                chip = (z + int(table[i, home, c])) % (K * L)
-                for route, core in zip(routes, (f, 1 - f)):
-                    route.append((source, (home * K * L + chip) * CORES + core))
+                home = z % TILES
+                for band, route in enumerate(routes):
+                    chip = (z + int(table[i, home, z // TILES, band])) % (K * L)
+                    route.append((source, (home * K * L + chip) * CORES + 1 - c))
     return routes
 
 
@@ -338,8 +350,8 @@
     h, w, x, k, l, c = (lax.axis_index(n) for n in ("h", "w", "x", "k", "l", "c"))
     z, i = 2 * k + l, X * w + x
     table = offsets()
-    rows_at = (z + jnp.asarray(table)[i, z % TILES, c]) % (K * L)
-    place = jnp.stack([h, w, x, c, z // TILES, rows_at, CORES * z + c]).astype(jnp.int32)
+    bands_at = (z + jnp.asarray(table)[i, z % TILES, z // TILES] + 1 - c) % (K * L)
+    place = jnp.stack([h, w, x, c, bands_at[0], bands_at[1], CORES * z + c]).astype(jnp.int32)
 
     earlier = jnp.concatenate([jnp.full((2,), -1, jnp.int32), clip_ids])
     same = jnp.stack([earlier[1:-1] == clip_ids, earlier[:-2] == clip_ids]).astype(f32)
@@ -374,6 +386,7 @@
         partner_1,
         gains,
         masks,
+        folded,
         smem=1,
     )
     onto_next = [
@@ -416,25 +429,34 @@
     frame = call(pair_kernel, shape(W * X, 8, 2, 16, 128), [], parts)
     mine = lax.all_to_all(frame, ("w", "x"), 0, 0)
     other = lax.ppermute(mine, "c", swap)
-    same_core, other_core = call(
-        attend_kernel,
-        [shape(64, 256), shape(64, 256)],
-        [
-            pltpu.VMEM((256, 2048), bf16),
-            pltpu.VMEM((256, 2048), bf16),
-        ],
+    halves = [pltpu.VMEM((256, 1024), bf16)] * 2
+    partial = call(
+        attend_mine_kernel,
+        [shape(128, 256), shape(128, 256), shape(128, 128), shape(128, 128), shape(128, 256)],
+        halves,
         place,
         mine,
+        gains,
+        folded,
+        smem=1,
+    )
+    near, far = call(
+        attend_other_kernel,
+        [shape(64, 256), shape(64, 256)],
+        halves,
+        place,
         other,
         gains,
         folded,
+        *partial,
         smem=1,
     )
-    route_0, route_1 = delivery(table)
-    same_core = lax.ppermute(same_core, ("w", "x", "k", "l", "c"), route_0)
-    other_core = lax.ppermute(other_core, ("w", "x", "k", "l", "c"), route_1)
-    first_frame = jnp.where(c == 0, same_core, other_core)
-    second_frame = jnp.where(c == 0, other_core, same_core)
+    route_near, route_far = delivery(table)
+    near = lax.ppermute(near, ("w", "x", "k", "l", "c"), route_near)
+    far = lax.ppermute(far, ("w", "x", "k", "l", "c"), route_far)
+    from_first = (z + i) % 2 == 0
+    first_frame = jnp.where(from_first, near, far)
+    second_frame = jnp.where(from_first, far, near)
     return jnp.stack([first_frame, second_frame]).reshape(video.shape)
 
 

time: 142 us -> 140 us (0.986)
  the two profiles are of different devices: /device:TPU:48 before, /device:TPU:80 now
where the time goes in v8:
time: 140 us; the launch traced here: 139 us
  waiting for transfers between devices  48.7 us (35%)
  blocking collectives  41.7 us (30%)
  starting transfers between devices  31.7 us (23%)
  Pallas kernels  14 us (10%)
  other arithmetic  1.48 us (1%)
    all_to_all x1, blocking collectives, body(): parts = lax.all_to_all(parts, ('k', 'l'), 0, 0)  26.7 us
    all_to_all x1, blocking collectives, body(): mine = lax.all_to_all(frame, ('w', 'x'), 0, 0)  15 us
    pallas_call x9, Pallas kernels, call(): pl.pallas_call(kernel, out_shape=out_shape, in_specs=[pl.BlockSpec(memory...  14 us
    ppermute x1, waiting for transfers between devices, body(): far = lax.ppermute(far, ('w', 'x', 'k', 'l', 'c'), route_far)  12.7 us
    ppermute x1, waiting for transfers between devices, body(): partner_2 = lax.ppermute(weight_2, ('h', 'w'), mirror)  11.9 us
    ppermute x1, waiting for transfers between devices, body(): partner_1 = lax.ppermute(weight_1, ('h', 'w'), mirror)  8.53 us
    ppermute x1, starting transfers between devices, body(): far = lax.ppermute(far, ('w', 'x', 'k', 'l', 'c'), route_far)  6.45 us
    all_to_all x1, starting transfers between devices, body(): second = lax.all_to_all(second, ('w', 'x'), 0, 0)  5.96 us
  transfers between devices with their start and end apart: 11, of which 9 were waited for; matrix products, arithmetic and copies ran while one was open for 1% of the time, Pallas kernels for 2%

profile of v8, /device:TPU:80, one launch (start us, length us, event | category | flops | bytes accessed | tf_op | source)
XLA Modules:
  0.0 139.0 jit_solution(15050957105648705374)
XLA Ops:
  0.0 0.9 copy-done.5
  0.9 1.2 shard_map.109
  2.1 0.0 copy-start.4
  2.1 5.2 %all-to-all-start = ((f32[8,256,128]{2,1,0:T(8,128)}), f32[8,256,128]{2,1,0:T(8,128)S(1)}, u32[]{:S(2)}, u32[]{:S(2)}) async-start(f32[8,256,128]{2,1,0:T(8,128)} %shard_map.109), calls=%async_computation | async-start | bytes 2097152 | tf_op jit(solution)/shard_map/all_to_all | solution.py:371
  7.3 0.0 copy-start.7
  7.3 0.0 copy-start.8
  7.3 0.0 copy-done.2
  7.3 3.2 %collective-permute-start = (f32[432,256]{1,0:T(8,128)S(1)}, f32[432,256]{1,0:T(8,128)S(1)}, u32[]{:S(2)}, u32[]{:S(2)}) collective-permute-start(f32[432,256]{1,0:T(8,128)S(1)} %bitcast.23), channel_id=1, source_target_pairs={{0,384},{128,256},{256,128},{384,0},{1,385},{129,257},{257,129},{3... | collective-permute-start | bytes 1327112 | tf_op jit(solution)/shard_map/ppermute | solution.py:364
  10.5 0.0 copy-done.9
  10.5 0.1 compare_bitcast_fusion.1
  10.6 0.1 broadcast_in_dim.4
  10.7 0.1 reshape_reshape.3
  10.8 0.0 copy-done.3
  10.8 0.0 copy-done.4
  10.8 0.7 shard_map.110._.folded_ref
  11.5 0.7 and_select_fusion
  12.2 0.1 stack.53.place_ref
  12.3 0.0 copy-done.7
  12.3 8.5 %collective-permute-done.partner_ref = f32[432,256]{1,0:T(8,128)S(1)} collective-permute-done((f32[432,256]{1,0:T(8,128)S(1)}, f32[432,256]{1,0:T(8,128)S(1)}, u32[]{:S(2)}, u32[]{:S(2)}) %collective-permute-start) | collective-permute-done | bytes 442400 | tf_op jit(solution)/shard_map/ppermute | solution.py:364
  20.8 2.1 %all-to-all-done = f32[8,256,128]{2,1,0:T(8,128)S(1)} async-done(((f32[8,256,128]{2,1,0:T(8,128)}), f32[8,256,128]{2,1,0:T(8,128)S(1)}, u32[]{:S(2)}, u32[]{:S(2)}) %all-to-all-start) | async-done | bytes 1048608 | tf_op jit(solution)/shard_map/all_to_all | solution.py:371
  23.0 2.4 %shard_map.111 = (f32[8,2,16,128]{3,2,1,0:T(8,128)S(1)}, f32[8,2,16,128]{3,2,1,0:T(8,128)S(1)}, f32[2,2,16,128]{3,2,1,0:T(8,128)S(1)}, f32[2,2,16,128]{3,2,1,0:T(8,128)S(1)}, f32[8,2,16,128]{3,2,1,0:T(8,128)S(1)}) custom-call(s32[7]{0:T(128)S(1)} %stack.53.place_ref, f32[8,4,4,16,128]{4,3,2,1,0:T(8,128)S(1)} %bitcast.20, f32[432,256]{1,0:T(8,128)S(1)} %bitcast.24, ...), custom_call_target="tpu_custom_call" | custom-call | tf_op jit(solution)/shard_map/pallas_call | solution.py:25
  25.4 0.0 collective-permute-start.1
  25.4 1.3 collective-permute-start.2
  26.7 1.3 collective-permute-start.3
  28.0 3.2 %collective-permute-done.2.last_ref = f32[2,2,16,128]{3,2,1,0:T(8,128)S(1)} collective-permute-done((f32[2,2,16,128]{3,2,1,0:T(8,128)S(1)}, f32[2,2,16,128]{3,2,1,0:T(8,128)S(1)}, u32[]{:S(2)}, u32[]{:S(2)}) %collective-permute-start.2) | collective-permute-done | bytes 32800 | tf_op jit(solution)/shard_map/ppermute | solution.py:397
  31.3 1.9 %collective-permute-done.3.last_arrived_ref = f32[2,2,16,128]{3,2,1,0:T(8,128)S(1)} collective-permute-done((f32[2,2,16,128]{3,2,1,0:T(8,128)S(1)}, f32[2,2,16,128]{3,2,1,0:T(8,128)S(1)}, u32[]{:S(2)}, u32[]{:S(2)}) %collective-permute-start.3) | collective-permute-done | bytes 32800 | tf_op jit(solution)/shard_map/ppermute | solution.py:398
  33.1 0.0 collective-permute-done.1.arrived_ref
  33.1 1.7 %shard_map.112 = f32[8,9,2,16,128]{4,3,2,1,0:T(8,128)} custom-call(s32[7]{0:T(128)S(1)} %stack.53.place_ref, f32[8,2,16,128]{3,2,1,0:T(8,128)S(1)} %get-tuple-element.19.own_ref, f32[8,2,16,128]{3,2,1,0:T(8,128)S(1)} %collective-permute-done.1.arrived_ref, f32[2,2,16,128]{3,2,1,0:T(8,128)S(1)} %collective-permute-done.2.last_ref, ...), custom_call_target="tpu_custom_call" | custom-call | tf_op jit(solution)/shard_map/pallas_call | solution.py:25
  34.8 6.0 %all-to-all-start.1 = ((f32[8,9,2,16,128]{4,3,2,1,0:T(8,128)}), f32[8,9,2,16,128]{4,3,2,1,0:T(8,128)S(1)}, u32[]{:S(2)}, u32[]{:S(2)}) async-start(f32[8,9,2,16,128]{4,3,2,1,0:T(8,128)} %shard_map.112), calls=%async_computation.1 | async-start | bytes 2359296 | tf_op jit(solution)/shard_map/all_to_all | solution.py:412
  40.8 2.6 %collective-permute-start.4 = (f32[432,256]{1,0:T(8,128)S(1)}, f32[432,256]{1,0:T(8,128)S(1)}, u32[]{:S(2)}, u32[]{:S(2)}) collective-permute-start(f32[432,256]{1,0:T(8,128)S(1)} %bitcast.21), channel_id=1, source_target_pairs={{0,384},{128,256},{256,128},{384,0},{1,385},{129,257},{257,129},{3... | collective-permute-start | bytes 1327112 | tf_op jit(solution)/shard_map/ppermute | solution.py:365
  43.4 11.9 %collective-permute-done.4.partner_ref = f32[432,256]{1,0:T(8,128)S(1)} collective-permute-done((f32[432,256]{1,0:T(8,128)S(1)}, f32[432,256]{1,0:T(8,128)S(1)}, u32[]{:S(2)}, u32[]{:S(2)}) %collective-permute-start.4) | collective-permute-done | bytes 442400 | tf_op jit(solution)/shard_map/ppermute | solution.py:365
  55.3 3.6 %all-to-all-done.1.second_ref = f32[8,9,2,16,128]{4,3,2,1,0:T(8,128)S(1)} async-done(((f32[8,9,2,16,128]{4,3,2,1,0:T(8,128)}), f32[8,9,2,16,128]{4,3,2,1,0:T(8,128)S(1)}, u32[]{:S(2)}, u32[]{:S(2)}) %all-to-all-start.1) | async-done | bytes 1179680 | tf_op jit(solution)/shard_map/all_to_all | solution.py:412
  58.9 3.2 %shard_map.113 = (f32[8,2,16,128]{3,2,1,0:T(8,128)S(1)}, f32[8,2,16,128]{3,2,1,0:T(8,128)S(1)}) custom-call(s32[7]{0:T(128)S(1)} %stack.53.place_ref, f32[8,9,2,16,128]{4,3,2,1,0:T(8,128)S(1)} %all-to-all-done.1.second_ref, f32[432,256]{1,0:T(8,128)S(1)} %bitcast.22, f32[432,256]{1,0:T(8,128)S(1)} %collective-permute-done.4.partner_ref, ...), custom_call_target="tpu_custom_call" | custom-call | tf_op jit(solution)/shard_map/pallas_call | solution.py:25
  62.1 0.0 collective-permute-start.5
  62.2 4.4 %collective-permute-done.5.arrived_ref = f32[8,2,16,128]{3,2,1,0:T(8,128)S(1)} collective-permute-done((f32[8,2,16,128]{3,2,1,0:T(8,128)S(1)}, f32[8,2,16,128]{3,2,1,0:T(8,128)S(1)}, u32[]{:S(2)}, u32[]{:S(2)}) %collective-permute-start.5) | collective-permute-done | bytes 131104 | tf_op jit(solution)/shard_map/ppermute | solution.py:426
  66.5 0.1 shard_map.114
  66.6 26.7 %all_to_all.20.parts_ref = f32[16,16,128]{2,1,0:T(8,128)S(1)} all-to-all(f32[16,16,128]{2,1,0:T(8,128)S(1)} %shard_map.114), channel_id=1, replica_groups=mesh['h'=2,'w'=2,'x'=4,'k'=8,'l'=2,'c'=2] {'k','l'}, dimensions={0} | all-to-all | bytes 262144 | tf_op jit(solution)/shard_map/all_to_all | solution.py:428
  93.3 0.1 shard_map.115
  93.5 15.0 %all_to_all.21.frame_ref = f32[8,8,2,16,128]{4,3,2,1,0:T(8,128)S(1)} all-to-all(f32[8,8,2,16,128]{4,3,2,1,0:T(8,128)S(1)} %shard_map.115), channel_id=1, replica_groups=mesh['h'=2,'w'=2,'x'=4,'k'=8,'l'=2,'c'=2] {'w','x'}, dimensions={0} | all-to-all | bytes 2097152 | tf_op jit(solution)/shard_map/all_to_all | solution.py:430
  108.5 1.9 %collective-permute-start.6 = (f32[8,8,2,16,128]{4,3,2,1,0:T(8,128)S(1)}, f32[8,8,2,16,128]{4,3,2,1,0:T(8,128)S(1)}, u32[]{:S(2)}, u32[]{:S(2)}) collective-permute-start(f32[8,8,2,16,128]{4,3,2,1,0:T(8,128)S(1)} %all_to_all.21.frame_ref), channel_id=1, source_target_pairs={{0,1},{1,0},{2,3},{3,2},{4,5},{5,4},{6,7},{7,6},{8,9},{9,8},{10,11... | collective-permute-start | bytes 3145736 | tf_op jit(solution)/shard_map/ppermute | solution.py:431
  110.4 2.3 %shard_map.116 = (f32[128,256]{1,0:T(8,128)S(1)}, f32[128,256]{1,0:T(8,128)S(1)}, f32[128,128]{1,0:T(8,128)S(1)}, f32[128,128]{1,0:T(8,128)S(1)}, f32[128,256]{1,0:T(8,128)S(1)}) custom-call(s32[7]{0:T(128)S(1)} %stack.53.place_ref, f32[8,8,2,16,128]{4,3,2,1,0:T(8,128)S(1)} %all_to_all.21.frame_ref, f32[3,256]{1,0:T(4,128)S(1)} %pad_maximum_fusion.1.gain_ref, ...), custom_call_target="tpu_custom_call" | custom-call | tf_op jit(solution)/shard_map/pallas_call | solution.py:25
  112.7 0.3 collective-permute-done.6.frame_ref
  113.0 2.2 %shard_map.117 = (f32[64,256]{1,0:T(8,128)S(1)}, f32[64,256]{1,0:T(8,128)S(1)}) custom-call(s32[7]{0:T(128)S(1)} %stack.53.place_ref, f32[8,8,2,16,128]{4,3,2,1,0:T(8,128)S(1)} %collective-permute-done.6.frame_ref, f32[3,256]{1,0:T(4,128)S(1)} %pad_maximum_fusion.1.gain_ref, f32[2,256,256]{2,1,0:T(8,128)S(1)} %shard_map.110._.folded_ref, ...), custom_call_target="tpu_custom_call" | custom-call | tf_op jit(solution)/shard_map/pallas_call | solution.py:25
  115.3 3.8 %collective-permute-start.7 = (f32[64,256]{1,0:T(8,128)S(1)}, f32[64,256]{1,0:T(8,128)S(1)}, u32[]{:S(2)}, u32[]{:S(2)}) collective-permute-start(f32[64,256]{1,0:T(8,128)S(1)} %get-tuple-element.31), channel_id=1, source_target_pairs={{0,17},{1,16},{2,55},{3,54},{4,77},{5,76},{6,123},{7,122},{8,157},... | collective-permute-start | bytes 196616 | tf_op jit(solution)/shard_map/ppermute | solution.py:455
  119.1 6.5 %collective-permute-start.8 = (f32[64,256]{1,0:T(8,128)S(1)}, f32[64,256]{1,0:T(8,128)S(1)}, u32[]{:S(2)}, u32[]{:S(2)}) collective-permute-start(f32[64,256]{1,0:T(8,128)S(1)} %get-tuple-element.32), channel_id=1, source_target_pairs={{0,15},{1,14},{2,53},{3,52},{4,75},{5,74},{6,121},{7,120},{8,155},... | collective-permute-start | bytes 196616 | tf_op jit(solution)/shard_map/ppermute | solution.py:456
  125.6 0.0 collective-permute-done.7
  125.6 12.7 %collective-permute-done.8 = f32[64,256]{1,0:T(8,128)S(1)} collective-permute-done((f32[64,256]{1,0:T(8,128)S(1)}, f32[64,256]{1,0:T(8,128)S(1)}, u32[]{:S(2)}, u32[]{:S(2)}) %collective-permute-start.8) | collective-permute-done | bytes 65568 | tf_op jit(solution)/shard_map/ppermute | solution.py:456
  138.3 0.7 pad_maximum_fusion
  (15 shorter events, 0.1 us)
Async XLA Ops:
  0.0 0.9 copy-start.5
  2.1 5.2 %copy-start.2 = (f32[3,3,3,16,256]{4,3,2,1,0:T(8,128)S(1)}, f32[3,3,3,16,256]{4,3,2,1,0:T(8,128)}, u32[]{:S(2)}) copy-start(f32[3,3,3,16,256]{4,3,2,1,0:T(8,128)} %param.14) | copy-start | bytes 1327108
  2.1 8.4 %copy-start.9 = (s32[32]{0:T(128)S(1)}, s32[32]{0:T(128)}, u32[]{:S(2)}) copy-start(s32[32]{0:T(128)} %param.12) | copy-start | bytes 388
  2.1 8.7 %copy-start = (f32[2,256,256]{2,1,0:T(8,128)S(1)}, f32[2,256,256]{2,1,0:T(8,128)}, u32[]{:S(2)}) copy-start(f32[2,256,256]{2,1,0:T(8,128)} %qk_ref.1) | copy-start | bytes 1572868
  2.1 8.7 %copy-start.3 = (f32[256,256]{1,0:T(8,128)S(1)}, f32[256,256]{1,0:T(8,128)}, u32[]{:S(2)}) copy-start(f32[256,256]{1,0:T(8,128)} %value_ref.1) | copy-start | bytes 786436
  2.1 8.7 %copy-start.4 = (f32[256,256]{1,0:T(8,128)S(1)}, f32[256,256]{1,0:T(8,128)}, u32[]{:S(2)}) copy-start(f32[256,256]{1,0:T(8,128)} %proj_ref.1) | copy-start | bytes 786436
  2.1 20.9 %all-to-all-start = ((f32[8,256,128]{2,1,0:T(8,128)}), f32[8,256,128]{2,1,0:T(8,128)S(1)}, u32[]{:S(2)}, u32[]{:S(2)}) async-start(f32[8,256,128]{2,1,0:T(8,128)} %shard_map.109), calls=%async_computation | async-start | bytes 2097152 | tf_op jit(solution)/shard_map/all_to_all | solution.py:371
  7.3 5.0 %copy-start.6 = (f32[256]{0:T(256)S(1)}, f32[256]{0:T(256)}, u32[]{:S(2)}) copy-start(f32[256]{0:T(256)} %param.17) | copy-start | bytes 3076
  7.3 5.0 %copy-start.7 = (f32[256]{0:T(256)S(1)}, f32[256]{0:T(256)}, u32[]{:S(2)}) copy-start(f32[256]{0:T(256)} %param.15) | copy-start | bytes 3076
  7.3 5.0 %copy-start.8 = (f32[256]{0:T(256)S(1)}, f32[256]{0:T(256)}, u32[]{:S(2)}) copy-start(f32[256]{0:T(256)} %param.13) | copy-start | bytes 3076
  7.3 13.5 %collective-permute-start = (f32[432,256]{1,0:T(8,128)S(1)}, f32[432,256]{1,0:T(8,128)S(1)}, u32[]{:S(2)}, u32[]{:S(2)}) collective-permute-start(f32[432,256]{1,0:T(8,128)S(1)} %bitcast.23), channel_id=1, source_target_pairs={{0,384},{128,256},{256,128},{384,0},{1,385},{129,257},{257,129},{3... | collective-permute-start | bytes 1327112 | tf_op jit(solution)/shard_map/ppermute | solution.py:364
  25.4 7.7 %collective-permute-start.1 = (f32[8,2,16,128]{3,2,1,0:T(8,128)S(1)}, f32[8,2,16,128]{3,2,1,0:T(8,128)S(1)}, u32[]{:S(2)}, u32[]{:S(2)}) collective-permute-start(f32[8,2,16,128]{3,2,1,0:T(8,128)S(1)} %get-tuple-element.20), channel_id=1, source_target_pairs={{0,1},{1,2},{2,3},{3,4},{4,5},{5,6},{6,7},{7,8},{8,9},{9,10},{10,1... | collective-permute-start | bytes 393224 | tf_op jit(solution)/shard_map/ppermute | solution.py:400
  25.4 5.8 %collective-permute-start.2 = (f32[2,2,16,128]{3,2,1,0:T(8,128)S(1)}, f32[2,2,16,128]{3,2,1,0:T(8,128)S(1)}, u32[]{:S(2)}, u32[]{:S(2)}) collective-permute-start(f32[2,2,16,128]{3,2,1,0:T(8,128)S(1)} %get-tuple-element.21), channel_id=1, source_target_pairs={{0,384},{128,256},{1,385},{129,257},{2,386},{130,258},{3,387},{131... | collective-permute-start | bytes 98312 | tf_op jit(solution)/shard_map/ppermute | solution.py:397
  26.7 6.4 %collective-permute-start.3 = (f32[2,2,16,128]{3,2,1,0:T(8,128)S(1)}, f32[2,2,16,128]{3,2,1,0:T(8,128)S(1)}, u32[]{:S(2)}, u32[]{:S(2)}) collective-permute-start(f32[2,2,16,128]{3,2,1,0:T(8,128)S(1)} %get-tuple-element.22), channel_id=1, source_target_pairs={{0,385},{1,386},{2,387},{3,388},{4,389},{5,390},{6,391},{7,392},{8... | collective-permute-start | bytes 98312 | tf_op jit(solution)/shard_map/ppermute | solution.py:398
  34.8 6.0 %copy-start.1 = (f32[3,3,3,16,256]{4,3,2,1,0:T(8,128)S(1)}, f32[3,3,3,16,256]{4,3,2,1,0:T(8,128)}, u32[]{:S(2)}) copy-start(f32[3,3,3,16,256]{4,3,2,1,0:T(8,128)} %param.16) | copy-start | bytes 1327108
  34.8 24.1 %all-to-all-start.1 = ((f32[8,9,2,16,128]{4,3,2,1,0:T(8,128)}), f32[8,9,2,16,128]{4,3,2,1,0:T(8,128)S(1)}, u32[]{:S(2)}, u32[]{:S(2)}) async-start(f32[8,9,2,16,128]{4,3,2,1,0:T(8,128)} %shard_map.112), calls=%async_computation.1 | async-start | bytes 2359296 | tf_op jit(solution)/shard_map/all_to_all | solution.py:412
  40.8 14.5 %collective-permute-start.4 = (f32[432,256]{1,0:T(8,128)S(1)}, f32[432,256]{1,0:T(8,128)S(1)}, u32[]{:S(2)}, u32[]{:S(2)}) collective-permute-start(f32[432,256]{1,0:T(8,128)S(1)} %bitcast.21), channel_id=1, source_target_pairs={{0,384},{128,256},{256,128},{384,0},{1,385},{129,257},{257,129},{3... | collective-permute-start | bytes 1327112 | tf_op jit(solution)/shard_map/ppermute | solution.py:365
  62.1 4.4 %collective-permute-start.5 = (f32[8,2,16,128]{3,2,1,0:T(8,128)S(1)}, f32[8,2,16,128]{3,2,1,0:T(8,128)S(1)}, u32[]{:S(2)}, u32[]{:S(2)}) collective-permute-start(f32[8,2,16,128]{3,2,1,0:T(8,128)S(1)} %get-tuple-element.25), channel_id=1, source_target_pairs={{0,1},{1,2},{2,3},{3,4},{4,5},{5,6},{6,7},{7,8},{8,9},{9,10},{10,1... | collective-permute-start | bytes 393224 | tf_op jit(solution)/shard_map/ppermute | solution.py:426
  108.5 4.5 %collective-permute-start.6 = (f32[8,8,2,16,128]{4,3,2,1,0:T(8,128)S(1)}, f32[8,8,2,16,128]{4,3,2,1,0:T(8,128)S(1)}, u32[]{:S(2)}, u32[]{:S(2)}) collective-permute-start(f32[8,8,2,16,128]{4,3,2,1,0:T(8,128)S(1)} %all_to_all.21.frame_ref), channel_id=1, source_target_pairs={{0,1},{1,0},{2,3},{3,2},{4,5},{5,4},{6,7},{7,6},{8,9},{9,8},{10,11... | collective-permute-start | bytes 3145736 | tf_op jit(solution)/shard_map/ppermute | solution.py:431
  115.3 10.3 %collective-permute-start.7 = (f32[64,256]{1,0:T(8,128)S(1)}, f32[64,256]{1,0:T(8,128)S(1)}, u32[]{:S(2)}, u32[]{:S(2)}) collective-permute-start(f32[64,256]{1,0:T(8,128)S(1)} %get-tuple-element.31), channel_id=1, source_target_pairs={{0,17},{1,16},{2,55},{3,54},{4,77},{5,76},{6,123},{7,122},{8,157},... | collective-permute-start | bytes 196616 | tf_op jit(solution)/shard_map/ppermute | solution.py:455
  119.1 19.2 %collective-permute-start.8 = (f32[64,256]{1,0:T(8,128)S(1)}, f32[64,256]{1,0:T(8,128)S(1)}, u32[]{:S(2)}, u32[]{:S(2)}) collective-permute-start(f32[64,256]{1,0:T(8,128)S(1)} %get-tuple-element.32), channel_id=1, source_target_pairs={{0,15},{1,14},{2,53},{3,52},{4,75},{5,74},{6,121},{7,120},{8,155},... | collective-permute-start | bytes 196616 | tf_op jit(solution)/shard_map/ppermute | solution.py:456

commit v9 on v8

--- a/solution.py
+++ b/solution.py
@@ -60,6 +60,23 @@
     rows = a_high.shape[0]
     both = one(jnp.concatenate([a_high, a_low], axis=0), b_high)
     return both[:rows] + (both[rows:] + one(a_high, b_low))
+
+
+def split3(value):
+    high = value.astype(bf16)
+    rest = value - high.astype(f32)
+    middle = rest.astype(bf16)
+    return high, middle, (rest - middle.astype(f32)).astype(bf16)
+
+
+def dot6(a, b):
+    def one(parts, right):
+        return jnp.dot(jnp.concatenate(parts, axis=0), right, preferred_element_type=f32)
+
+    rows = a[0].shape[0]
+    by_high, by_middle, by_low = one(a, b[0]), one(a[:2], b[1]), one(a[:1], b[2])
+    small = by_high[2 * rows :] + (by_middle[rows:] + by_low)
+    return by_high[:rows] + (by_high[rows : 2 * rows] + by_middle[:rows] + small)
 
 
 def norm_silu(value, gain):
@@ -255,24 +272,23 @@
     return jnp.concatenate(blocks, axis=0)
 
 
-def attend(place_ref, frame_ref, gain_ref, queries, high_ref, low_ref):
+def attend(place_ref, frame_ref, gain_ref, queries, high_ref, middle_ref, low_ref):
     gain = column(gain_ref[2:3])
     for m in range(8):
         tile = gathered(place_ref, frame_ref, m)
         normed = tile * lax.rsqrt(jnp.mean(tile * tile, axis=0, keepdims=True) + epsilon) * gain
-        high, low = split(normed)
-        high_ref[:, 128 * m : 128 * m + 128] = high
-        low_ref[:, 128 * m : 128 * m + 128] = low
-    scores = dot3_stacked(*split(queries), high_ref[...], low_ref[...])
+        for ref, piece in zip((high_ref, middle_ref, low_ref), split3(normed)):
+            ref[:, 128 * m : 128 * m + 128] = piece
+    scores = dot6(split3(queries), (high_ref[...], middle_ref[...], low_ref[...]))
     most = jnp.max(scores, axis=1, keepdims=True)
     weights = jnp.exp(scores - most)
     total = jnp.sum(weights, axis=1, keepdims=True)
-    return most, total, dot3_stacked(*split(weights), high_ref[...], low_ref[...], ((1,), (1,)))
+    return most, total, dot3_stacked(*split(weights), high_ref[...], middle_ref[...], ((1,), (1,)))
 
 
 def attend_mine_kernel(
     place_ref, frame_ref, gain_ref, folded_ref,
-    rows_ref, queries_ref, most_ref, total_ref, sum_ref, high_ref, low_ref,
+    rows_ref, queries_ref, most_ref, total_ref, sum_ref, high_ref, middle_ref, low_ref,
 ):
     first_at, second_at = place_ref[4], place_ref[5]
     first = gathered(place_ref, frame_ref, first_at >> 1)
@@ -282,20 +298,22 @@
     low_half = lax.broadcasted_iota(jnp.int32, first.shape, 1) < 64
     rows = jnp.where(low_half, first, second).T
     normed = rows * lax.rsqrt(jnp.mean(rows * rows, axis=1, keepdims=True) + epsilon) * gain_ref[2:3]
-    queries = dot3_stacked(*split(normed), *split(folded_ref[0]))
+    queries = dot6(split3(normed), split3(folded_ref[0]))
     rows_ref[...] = rows
     queries_ref[...] = queries
-    most, total, sum_ref[...] = attend(place_ref, frame_ref, gain_ref, queries, high_ref, low_ref)
+    most, total, sum_ref[...] = attend(
+        place_ref, frame_ref, gain_ref, queries, high_ref, middle_ref, low_ref
+    )
     most_ref[...] = jnp.broadcast_to(most, (128, 128))
     total_ref[...] = jnp.broadcast_to(total, (128, 128))
 
 
 def attend_other_kernel(
     place_ref, frame_ref, gain_ref, folded_ref, rows_ref, queries_ref, most_ref, total_ref, sum_ref,
-    first_ref, second_ref, high_ref, low_ref,
+    first_ref, second_ref, high_ref, middle_ref, low_ref,
 ):
     most, total, weighted = attend(
-        place_ref, frame_ref, gain_ref, queries_ref[...], high_ref, low_ref
+        place_ref, frame_ref, gain_ref, queries_ref[...], high_ref, middle_ref, low_ref
     )
     most_before, total_before = most_ref[:, 0:1], total_ref[:, 0:1]
     top = jnp.maximum(most, most_before)
@@ -429,7 +447,7 @@
     frame = call(pair_kernel, shape(W * X, 8, 2, 16, 128), [], parts)
     mine = lax.all_to_all(frame, ("w", "x"), 0, 0)
     other = lax.ppermute(mine, "c", swap)
-    halves = [pltpu.VMEM((256, 1024), bf16)] * 2
+    halves = [pltpu.VMEM((256, 1024), bf16)] * 3
     partial = call(
         attend_mine_kernel,
         [shape(128, 256), shape(128, 256), shape(128, 128), shape(128, 128), shape(128, 256)],

time: 140 us -> 140 us (level)
  transfers between devices with their start and end apart: 11 -> 11, of which waited for: 9 -> 8; matrix products, arithmetic and copies ran while one was open for 1% -> 1% of each run, Pallas kernels for 2% -> 2%
where the time goes in v9:
time: 140 us
  waiting for transfers between devices  48.3 us (34%)
  blocking collectives  41.7 us (30%)
  starting transfers between devices  31.7 us (23%)
  Pallas kernels  14.9 us (11%)
  other arithmetic  1.48 us (1%)
    all_to_all x1, blocking collectives, body(): parts = lax.all_to_all(parts, ('k', 'l'), 0, 0)  26.7 us
    all_to_all x1, blocking collectives, body(): mine = lax.all_to_all(frame, ('w', 'x'), 0, 0)  15 us
    pallas_call x9, Pallas kernels, call(): pl.pallas_call(kernel, out_shape=out_shape, in_specs=[pl.BlockSpec(memory...  14.9 us
    ppermute x1, waiting for transfers between devices, body(): far = lax.ppermute(far, ('w', 'x', 'k', 'l', 'c'), route_far)  12.6 us
    ppermute x1, waiting for transfers between devices, body(): partner_2 = lax.ppermute(weight_2, ('h', 'w'), mirror)  11.9 us
    ppermute x1, waiting for transfers between devices, body(): partner_1 = lax.ppermute(weight_1, ('h', 'w'), mirror)  8.53 us
    ppermute x1, starting transfers between devices, body(): far = lax.ppermute(far, ('w', 'x', 'k', 'l', 'c'), route_far)  6.15 us
    all_to_all x1, starting transfers between devices, body(): second = lax.all_to_all(second, ('w', 'x'), 0, 0)  5.96 us
  transfers between devices with their start and end apart: 11, of which 8 were waited for; matrix products, arithmetic and copies ran while one was open for 1% of the time, Pallas kernels for 2%

profile of v9, /device:TPU:80, one launch (start us, length us, event | category | flops | bytes accessed | tf_op | source)
XLA Modules:
  0.0 139.5 jit_solution(6342968168160298361)
XLA Ops:
  0.0 0.9 copy-done.5
  0.9 1.2 shard_map.109
  2.1 0.0 copy-start.4
  2.1 5.2 %all-to-all-start = ((f32[8,256,128]{2,1,0:T(8,128)}), f32[8,256,128]{2,1,0:T(8,128)S(1)}, u32[]{:S(2)}, u32[]{:S(2)}) async-start(f32[8,256,128]{2,1,0:T(8,128)} %shard_map.109), calls=%async_computation | async-start | bytes 2097152 | tf_op jit(solution)/shard_map/all_to_all | solution.py:389
  7.3 0.0 copy-start.7
  7.3 0.0 copy-start.8
  7.3 0.0 copy-done.2
  7.3 3.2 %collective-permute-start = (f32[432,256]{1,0:T(8,128)S(1)}, f32[432,256]{1,0:T(8,128)S(1)}, u32[]{:S(2)}, u32[]{:S(2)}) collective-permute-start(f32[432,256]{1,0:T(8,128)S(1)} %bitcast.23), channel_id=1, source_target_pairs={{0,384},{128,256},{256,128},{384,0},{1,385},{129,257},{257,129},{3... | collective-permute-start | bytes 1327112 | tf_op jit(solution)/shard_map/ppermute | solution.py:382
  10.5 0.0 copy-done.9
  10.5 0.1 compare_bitcast_fusion.1
  10.6 0.1 broadcast_in_dim.4
  10.7 0.1 reshape_reshape.3
  10.8 0.0 copy-done
  10.8 0.7 shard_map.110._.folded_ref
  11.5 0.7 and_select_fusion
  12.2 0.1 stack.53.place_ref
  12.3 0.0 copy-done.6
  12.3 0.0 copy-done.8
  12.3 8.5 %collective-permute-done.partner_ref = f32[432,256]{1,0:T(8,128)S(1)} collective-permute-done((f32[432,256]{1,0:T(8,128)S(1)}, f32[432,256]{1,0:T(8,128)S(1)}, u32[]{:S(2)}, u32[]{:S(2)}) %collective-permute-start) | collective-permute-done | bytes 442400 | tf_op jit(solution)/shard_map/ppermute | solution.py:382
  20.8 2.1 %all-to-all-done = f32[8,256,128]{2,1,0:T(8,128)S(1)} async-done(((f32[8,256,128]{2,1,0:T(8,128)}), f32[8,256,128]{2,1,0:T(8,128)S(1)}, u32[]{:S(2)}, u32[]{:S(2)}) %all-to-all-start) | async-done | bytes 1048608 | tf_op jit(solution)/shard_map/all_to_all | solution.py:389
  23.0 2.4 %shard_map.111 = (f32[8,2,16,128]{3,2,1,0:T(8,128)S(1)}, f32[8,2,16,128]{3,2,1,0:T(8,128)S(1)}, f32[2,2,16,128]{3,2,1,0:T(8,128)S(1)}, f32[2,2,16,128]{3,2,1,0:T(8,128)S(1)}, f32[8,2,16,128]{3,2,1,0:T(8,128)S(1)}) custom-call(s32[7]{0:T(128)S(1)} %stack.53.place_ref, f32[8,4,4,16,128]{4,3,2,1,0:T(8,128)S(1)} %bitcast.20, f32[432,256]{1,0:T(8,128)S(1)} %bitcast.24, ...), custom_call_target="tpu_custom_call" | custom-call | tf_op jit(solution)/shard_map/pallas_call | solution.py:25
  25.4 0.0 collective-permute-start.1
  25.4 1.3 collective-permute-start.2
  26.7 1.3 collective-permute-start.3
  28.0 3.2 %collective-permute-done.2.last_ref = f32[2,2,16,128]{3,2,1,0:T(8,128)S(1)} collective-permute-done((f32[2,2,16,128]{3,2,1,0:T(8,128)S(1)}, f32[2,2,16,128]{3,2,1,0:T(8,128)S(1)}, u32[]{:S(2)}, u32[]{:S(2)}) %collective-permute-start.2) | collective-permute-done | bytes 32800 | tf_op jit(solution)/shard_map/ppermute | solution.py:415
  31.3 1.9 %collective-permute-done.3.last_arrived_ref = f32[2,2,16,128]{3,2,1,0:T(8,128)S(1)} collective-permute-done((f32[2,2,16,128]{3,2,1,0:T(8,128)S(1)}, f32[2,2,16,128]{3,2,1,0:T(8,128)S(1)}, u32[]{:S(2)}, u32[]{:S(2)}) %collective-permute-start.3) | collective-permute-done | bytes 32800 | tf_op jit(solution)/shard_map/ppermute | solution.py:416
  33.1 0.0 collective-permute-done.1.arrived_ref
  33.1 1.7 %shard_map.112 = f32[8,9,2,16,128]{4,3,2,1,0:T(8,128)} custom-call(s32[7]{0:T(128)S(1)} %stack.53.place_ref, f32[8,2,16,128]{3,2,1,0:T(8,128)S(1)} %get-tuple-element.19.own_ref, f32[8,2,16,128]{3,2,1,0:T(8,128)S(1)} %collective-permute-done.1.arrived_ref, f32[2,2,16,128]{3,2,1,0:T(8,128)S(1)} %collective-permute-done.2.last_ref, ...), custom_call_target="tpu_custom_call" | custom-call | tf_op jit(solution)/shard_map/pallas_call | solution.py:25
  34.8 6.0 %all-to-all-start.1 = ((f32[8,9,2,16,128]{4,3,2,1,0:T(8,128)}), f32[8,9,2,16,128]{4,3,2,1,0:T(8,128)S(1)}, u32[]{:S(2)}, u32[]{:S(2)}) async-start(f32[8,9,2,16,128]{4,3,2,1,0:T(8,128)} %shard_map.112), calls=%async_computation.1 | async-start | bytes 2359296 | tf_op jit(solution)/shard_map/all_to_all | solution.py:430
  40.8 2.6 %collective-permute-start.4 = (f32[432,256]{1,0:T(8,128)S(1)}, f32[432,256]{1,0:T(8,128)S(1)}, u32[]{:S(2)}, u32[]{:S(2)}) collective-permute-start(f32[432,256]{1,0:T(8,128)S(1)} %bitcast.21), channel_id=1, source_target_pairs={{0,384},{128,256},{256,128},{384,0},{1,385},{129,257},{257,129},{3... | collective-permute-start | bytes 1327112 | tf_op jit(solution)/shard_map/ppermute | solution.py:383
  43.4 11.9 %collective-permute-done.4.partner_ref = f32[432,256]{1,0:T(8,128)S(1)} collective-permute-done((f32[432,256]{1,0:T(8,128)S(1)}, f32[432,256]{1,0:T(8,128)S(1)}, u32[]{:S(2)}, u32[]{:S(2)}) %collective-permute-start.4) | collective-permute-done | bytes 442400 | tf_op jit(solution)/shard_map/ppermute | solution.py:383
  55.3 3.6 %all-to-all-done.1.second_ref = f32[8,9,2,16,128]{4,3,2,1,0:T(8,128)S(1)} async-done(((f32[8,9,2,16,128]{4,3,2,1,0:T(8,128)}), f32[8,9,2,16,128]{4,3,2,1,0:T(8,128)S(1)}, u32[]{:S(2)}, u32[]{:S(2)}) %all-to-all-start.1) | async-done | bytes 1179680 | tf_op jit(solution)/shard_map/all_to_all | solution.py:430
  58.9 3.2 %shard_map.113 = (f32[8,2,16,128]{3,2,1,0:T(8,128)S(1)}, f32[8,2,16,128]{3,2,1,0:T(8,128)S(1)}) custom-call(s32[7]{0:T(128)S(1)} %stack.53.place_ref, f32[8,9,2,16,128]{4,3,2,1,0:T(8,128)S(1)} %all-to-all-done.1.second_ref, f32[432,256]{1,0:T(8,128)S(1)} %bitcast.22, f32[432,256]{1,0:T(8,128)S(1)} %collective-permute-done.4.partner_ref, ...), custom_call_target="tpu_custom_call" | custom-call | tf_op jit(solution)/shard_map/pallas_call | solution.py:25
  62.1 0.0 collective-permute-start.5
  62.2 4.4 %collective-permute-done.5.arrived_ref = f32[8,2,16,128]{3,2,1,0:T(8,128)S(1)} collective-permute-done((f32[8,2,16,128]{3,2,1,0:T(8,128)S(1)}, f32[8,2,16,128]{3,2,1,0:T(8,128)S(1)}, u32[]{:S(2)}, u32[]{:S(2)}) %collective-permute-start.5) | collective-permute-done | bytes 131104 | tf_op jit(solution)/shard_map/ppermute | solution.py:444
  66.5 0.1 shard_map.114
  66.6 26.7 %all_to_all.20.parts_ref = f32[16,16,128]{2,1,0:T(8,128)S(1)} all-to-all(f32[16,16,128]{2,1,0:T(8,128)S(1)} %shard_map.114), channel_id=1, replica_groups=mesh['h'=2,'w'=2,'x'=4,'k'=8,'l'=2,'c'=2] {'k','l'}, dimensions={0} | all-to-all | bytes 262144 | tf_op jit(solution)/shard_map/all_to_all | solution.py:446
  93.3 0.1 shard_map.115
  93.5 15.0 %all_to_all.21.frame_ref = f32[8,8,2,16,128]{4,3,2,1,0:T(8,128)S(1)} all-to-all(f32[8,8,2,16,128]{4,3,2,1,0:T(8,128)S(1)} %shard_map.115), channel_id=1, replica_groups=mesh['h'=2,'w'=2,'x'=4,'k'=8,'l'=2,'c'=2] {'w','x'}, dimensions={0} | all-to-all | bytes 2097152 | tf_op jit(solution)/shard_map/all_to_all | solution.py:448
  108.5 1.9 %collective-permute-start.6 = (f32[8,8,2,16,128]{4,3,2,1,0:T(8,128)S(1)}, f32[8,8,2,16,128]{4,3,2,1,0:T(8,128)S(1)}, u32[]{:S(2)}, u32[]{:S(2)}) collective-permute-start(f32[8,8,2,16,128]{4,3,2,1,0:T(8,128)S(1)} %all_to_all.21.frame_ref), channel_id=1, source_target_pairs={{0,1},{1,0},{2,3},{3,2},{4,5},{5,4},{6,7},{7,6},{8,9},{9,8},{10,11... | collective-permute-start | bytes 3145736 | tf_op jit(solution)/shard_map/ppermute | solution.py:449
  110.4 2.8 %shard_map.116 = (f32[128,256]{1,0:T(8,128)S(1)}, f32[128,256]{1,0:T(8,128)S(1)}, f32[128,128]{1,0:T(8,128)S(1)}, f32[128,128]{1,0:T(8,128)S(1)}, f32[128,256]{1,0:T(8,128)S(1)}) custom-call(s32[7]{0:T(128)S(1)} %stack.53.place_ref, f32[8,8,2,16,128]{4,3,2,1,0:T(8,128)S(1)} %all_to_all.21.frame_ref, f32[3,256]{1,0:T(4,128)S(1)} %pad_maximum_fusion.1.gain_ref, ...), custom_call_target="tpu_custom_call" | custom-call | tf_op jit(solution)/shard_map/pallas_call | solution.py:25
  113.2 0.0 collective-permute-done.6.frame_ref
  113.2 2.7 %shard_map.117 = (f32[64,256]{1,0:T(8,128)S(1)}, f32[64,256]{1,0:T(8,128)S(1)}) custom-call(s32[7]{0:T(128)S(1)} %stack.53.place_ref, f32[8,8,2,16,128]{4,3,2,1,0:T(8,128)S(1)} %collective-permute-done.6.frame_ref, f32[3,256]{1,0:T(4,128)S(1)} %pad_maximum_fusion.1.gain_ref, f32[2,256,256]{2,1,0:T(8,128)S(1)} %shard_map.110._.folded_ref, ...), custom_call_target="tpu_custom_call" | custom-call | tf_op jit(solution)/shard_map/pallas_call | solution.py:25
  115.9 4.1 %collective-permute-start.7 = (f32[64,256]{1,0:T(8,128)S(1)}, f32[64,256]{1,0:T(8,128)S(1)}, u32[]{:S(2)}, u32[]{:S(2)}) collective-permute-start(f32[64,256]{1,0:T(8,128)S(1)} %get-tuple-element.31), channel_id=1, source_target_pairs={{0,17},{1,16},{2,55},{3,54},{4,77},{5,76},{6,123},{7,122},{8,157},... | collective-permute-start | bytes 196616 | tf_op jit(solution)/shard_map/ppermute | solution.py:473
  120.0 6.2 %collective-permute-start.8 = (f32[64,256]{1,0:T(8,128)S(1)}, f32[64,256]{1,0:T(8,128)S(1)}, u32[]{:S(2)}, u32[]{:S(2)}) collective-permute-start(f32[64,256]{1,0:T(8,128)S(1)} %get-tuple-element.32), channel_id=1, source_target_pairs={{0,15},{1,14},{2,53},{3,52},{4,75},{5,74},{6,121},{7,120},{8,155},... | collective-permute-start | bytes 196616 | tf_op jit(solution)/shard_map/ppermute | solution.py:474
  126.2 0.0 collective-permute-done.7
  126.2 12.6 %collective-permute-done.8 = f32[64,256]{1,0:T(8,128)S(1)} collective-permute-done((f32[64,256]{1,0:T(8,128)S(1)}, f32[64,256]{1,0:T(8,128)S(1)}, u32[]{:S(2)}, u32[]{:S(2)}) %collective-permute-start.8) | collective-permute-done | bytes 65568 | tf_op jit(solution)/shard_map/ppermute | solution.py:474
  138.9 0.7 pad_maximum_fusion
  (15 shorter events, 0.1 us)
Async XLA Ops:
  0.0 0.9 copy-start.5
  2.1 5.2 %copy-start.2 = (f32[3,3,3,16,256]{4,3,2,1,0:T(8,128)S(1)}, f32[3,3,3,16,256]{4,3,2,1,0:T(8,128)}, u32[]{:S(2)}) copy-start(f32[3,3,3,16,256]{4,3,2,1,0:T(8,128)} %param.14) | copy-start | bytes 1327108
  2.1 8.4 %copy-start.9 = (s32[32]{0:T(128)S(1)}, s32[32]{0:T(128)}, u32[]{:S(2)}) copy-start(s32[32]{0:T(128)} %param.12) | copy-start | bytes 388
  2.1 8.7 %copy-start = (f32[2,256,256]{2,1,0:T(8,128)S(1)}, f32[2,256,256]{2,1,0:T(8,128)}, u32[]{:S(2)}) copy-start(f32[2,256,256]{2,1,0:T(8,128)} %qk_ref.1) | copy-start | bytes 1572868
  2.1 8.7 %copy-start.3 = (f32[256,256]{1,0:T(8,128)S(1)}, f32[256,256]{1,0:T(8,128)}, u32[]{:S(2)}) copy-start(f32[256,256]{1,0:T(8,128)} %value_ref.1) | copy-start | bytes 786436
  2.1 8.7 %copy-start.4 = (f32[256,256]{1,0:T(8,128)S(1)}, f32[256,256]{1,0:T(8,128)}, u32[]{:S(2)}) copy-start(f32[256,256]{1,0:T(8,128)} %proj_ref.1) | copy-start | bytes 786436
  2.1 20.9 %all-to-all-start = ((f32[8,256,128]{2,1,0:T(8,128)}), f32[8,256,128]{2,1,0:T(8,128)S(1)}, u32[]{:S(2)}, u32[]{:S(2)}) async-start(f32[8,256,128]{2,1,0:T(8,128)} %shard_map.109), calls=%async_computation | async-start | bytes 2097152 | tf_op jit(solution)/shard_map/all_to_all | solution.py:389
  7.3 5.0 %copy-start.6 = (f32[256]{0:T(256)S(1)}, f32[256]{0:T(256)}, u32[]{:S(2)}) copy-start(f32[256]{0:T(256)} %param.17) | copy-start | bytes 3076
  7.3 5.0 %copy-start.7 = (f32[256]{0:T(256)S(1)}, f32[256]{0:T(256)}, u32[]{:S(2)}) copy-start(f32[256]{0:T(256)} %param.15) | copy-start | bytes 3076
  7.3 5.0 %copy-start.8 = (f32[256]{0:T(256)S(1)}, f32[256]{0:T(256)}, u32[]{:S(2)}) copy-start(f32[256]{0:T(256)} %param.13) | copy-start | bytes 3076
  7.3 13.5 %collective-permute-start = (f32[432,256]{1,0:T(8,128)S(1)}, f32[432,256]{1,0:T(8,128)S(1)}, u32[]{:S(2)}, u32[]{:S(2)}) collective-permute-start(f32[432,256]{1,0:T(8,128)S(1)} %bitcast.23), channel_id=1, source_target_pairs={{0,384},{128,256},{256,128},{384,0},{1,385},{129,257},{257,129},{3... | collective-permute-start | bytes 1327112 | tf_op jit(solution)/shard_map/ppermute | solution.py:382
  25.4 7.7 %collective-permute-start.1 = (f32[8,2,16,128]{3,2,1,0:T(8,128)S(1)}, f32[8,2,16,128]{3,2,1,0:T(8,128)S(1)}, u32[]{:S(2)}, u32[]{:S(2)}) collective-permute-start(f32[8,2,16,128]{3,2,1,0:T(8,128)S(1)} %get-tuple-element.20), channel_id=1, source_target_pairs={{0,1},{1,2},{2,3},{3,4},{4,5},{5,6},{6,7},{7,8},{8,9},{9,10},{10,1... | collective-permute-start | bytes 393224 | tf_op jit(solution)/shard_map/ppermute | solution.py:418
  25.4 5.8 %collective-permute-start.2 = (f32[2,2,16,128]{3,2,1,0:T(8,128)S(1)}, f32[2,2,16,128]{3,2,1,0:T(8,128)S(1)}, u32[]{:S(2)}, u32[]{:S(2)}) collective-permute-start(f32[2,2,16,128]{3,2,1,0:T(8,128)S(1)} %get-tuple-element.21), channel_id=1, source_target_pairs={{0,384},{128,256},{1,385},{129,257},{2,386},{130,258},{3,387},{131... | collective-permute-start | bytes 98312 | tf_op jit(solution)/shard_map/ppermute | solution.py:415
  26.7 6.4 %collective-permute-start.3 = (f32[2,2,16,128]{3,2,1,0:T(8,128)S(1)}, f32[2,2,16,128]{3,2,1,0:T(8,128)S(1)}, u32[]{:S(2)}, u32[]{:S(2)}) collective-permute-start(f32[2,2,16,128]{3,2,1,0:T(8,128)S(1)} %get-tuple-element.22), channel_id=1, source_target_pairs={{0,385},{1,386},{2,387},{3,388},{4,389},{5,390},{6,391},{7,392},{8... | collective-permute-start | bytes 98312 | tf_op jit(solution)/shard_map/ppermute | solution.py:416
  34.8 6.0 %copy-start.1 = (f32[3,3,3,16,256]{4,3,2,1,0:T(8,128)S(1)}, f32[3,3,3,16,256]{4,3,2,1,0:T(8,128)}, u32[]{:S(2)}) copy-start(f32[3,3,3,16,256]{4,3,2,1,0:T(8,128)} %param.16) | copy-start | bytes 1327108
  34.8 24.1 %all-to-all-start.1 = ((f32[8,9,2,16,128]{4,3,2,1,0:T(8,128)}), f32[8,9,2,16,128]{4,3,2,1,0:T(8,128)S(1)}, u32[]{:S(2)}, u32[]{:S(2)}) async-start(f32[8,9,2,16,128]{4,3,2,1,0:T(8,128)} %shard_map.112), calls=%async_computation.1 | async-start | bytes 2359296 | tf_op jit(solution)/shard_map/all_to_all | solution.py:430
  40.8 14.5 %collective-permute-start.4 = (f32[432,256]{1,0:T(8,128)S(1)}, f32[432,256]{1,0:T(8,128)S(1)}, u32[]{:S(2)}, u32[]{:S(2)}) collective-permute-start(f32[432,256]{1,0:T(8,128)S(1)} %bitcast.21), channel_id=1, source_target_pairs={{0,384},{128,256},{256,128},{384,0},{1,385},{129,257},{257,129},{3... | collective-permute-start | bytes 1327112 | tf_op jit(solution)/shard_map/ppermute | solution.py:383
  62.1 4.4 %collective-permute-start.5 = (f32[8,2,16,128]{3,2,1,0:T(8,128)S(1)}, f32[8,2,16,128]{3,2,1,0:T(8,128)S(1)}, u32[]{:S(2)}, u32[]{:S(2)}) collective-permute-start(f32[8,2,16,128]{3,2,1,0:T(8,128)S(1)} %get-tuple-element.25), channel_id=1, source_target_pairs={{0,1},{1,2},{2,3},{3,4},{4,5},{5,6},{6,7},{7,8},{8,9},{9,10},{10,1... | collective-permute-start | bytes 393224 | tf_op jit(solution)/shard_map/ppermute | solution.py:444
  108.5 4.7 %collective-permute-start.6 = (f32[8,8,2,16,128]{4,3,2,1,0:T(8,128)S(1)}, f32[8,8,2,16,128]{4,3,2,1,0:T(8,128)S(1)}, u32[]{:S(2)}, u32[]{:S(2)}) collective-permute-start(f32[8,8,2,16,128]{4,3,2,1,0:T(8,128)S(1)} %all_to_all.21.frame_ref), channel_id=1, source_target_pairs={{0,1},{1,0},{2,3},{3,2},{4,5},{5,4},{6,7},{7,6},{8,9},{9,8},{10,11... | collective-permute-start | bytes 3145736 | tf_op jit(solution)/shard_map/ppermute | solution.py:449
  115.9 10.3 %collective-permute-start.7 = (f32[64,256]{1,0:T(8,128)S(1)}, f32[64,256]{1,0:T(8,128)S(1)}, u32[]{:S(2)}, u32[]{:S(2)}) collective-permute-start(f32[64,256]{1,0:T(8,128)S(1)} %get-tuple-element.31), channel_id=1, source_target_pairs={{0,17},{1,16},{2,55},{3,54},{4,77},{5,76},{6,123},{7,122},{8,157},... | collective-permute-start | bytes 196616 | tf_op jit(solution)/shard_map/ppermute | solution.py:473
  120.0 18.8 %collective-permute-start.8 = (f32[64,256]{1,0:T(8,128)S(1)}, f32[64,256]{1,0:T(8,128)S(1)}, u32[]{:S(2)}, u32[]{:S(2)}) collective-permute-start(f32[64,256]{1,0:T(8,128)S(1)} %get-tuple-element.32), channel_id=1, source_target_pairs={{0,15},{1,14},{2,53},{3,52},{4,75},{5,74},{6,121},{7,120},{8,155},... | collective-permute-start | bytes 196616 | tf_op jit(solution)/shard_map/ppermute | solution.py:474

commit v10 on v9

--- a/solution.py
+++ b/solution.py
@@ -207,26 +207,34 @@
     adjacent = jnp.full((16, 128), place_ref[6], jnp.int32) != 0
     gain = column(gain_ref[1:2])
     half = place_ref[0]
-    for q in range(TILES + 1):
-        blocks = []
-        for slot in range(2):
-            for u in range(W):
-                source = jnp.where(half == slot, u, 1 - u)
-                blocks += [second_ref[X * source + x, q, slot] for x in range(X)]
-        high, low = split(norm_silu(jnp.concatenate(blocks, axis=0), gain))
-        high_ref[:, 128 * q : 128 * q + 128] = high
-        low_ref[:, 128 * q : 128 * q + 128] = low
     for g, ref in enumerate((weight_ref, partner_ref)):
-        slot = half if g == 0 else 1 - half
-        w_high, w_low = split(ref[...])
-        product_ref[...] = dot3(w_high, w_low, high_ref[...], low_ref[...])
-        before = taps(product_ref[:, :128], adjacent)
-        for q in range(TILES):
-            now = taps(product_ref[:, 128 * (q + 1) : 128 * (q + 2)], adjacent)
-            at = TILES * half + q
-            done = in_time(now, before, mask_ref[0, pl.ds(at, 1)], mask_ref[1, pl.ds(at, 1)])
-            stay_ref[q, slot] = done[:16]
-            go_ref[q, slot] = done[16:] + kept_ref[q, slot]
+        high_ref[g], low_ref[g] = split(ref[...])
+    before = None
+    for pair in range(0, TILES + 1, 2):
+        tiles = range(pair, min(pair + 2, TILES + 1))
+        pieces = []
+        for q in tiles:
+            blocks = []
+            for slot in range(2):
+                for u in range(W):
+                    source = jnp.where(half == slot, u, 1 - u)
+                    blocks += [second_ref[X * source + x, q, slot] for x in range(X)]
+            pieces.append(split(norm_silu(jnp.concatenate(blocks, axis=0), gain)))
+        high, low = (jnp.concatenate([p[i] for p in pieces], axis=1) for i in range(2))
+        for g in range(2):
+            product_ref[g, :, : 128 * len(tiles)] = dot3(high_ref[g], low_ref[g], high, low)
+        for side, q in enumerate(tiles):
+            now = [
+                taps(product_ref[g, :, 128 * side : 128 * side + 128], adjacent) for g in range(2)
+            ]
+            if q > 0:
+                at = TILES * half + q - 1
+                masks = mask_ref[0, pl.ds(at, 1)], mask_ref[1, pl.ds(at, 1)]
+                for g in range(2):
+                    slot = half if g == 0 else 1 - half
+                    done = in_time(now[g], before[g], *masks)
+                    stay_ref[q - 1, slot] = done[:16]
+                    go_ref[q - 1, slot] = done[16:] + kept_ref[q - 1, slot]
             before = now
 
 
@@ -431,7 +439,7 @@
     stay, go = call(
         conv2_kernel,
         [shape(TILES, 2, 16, 128)] * 2,
-        [pltpu.VMEM((256, 1152), bf16)] * 2 + [pltpu.VMEM((432, 1152), f32)],
+        weights_scratch + [pltpu.VMEM((2, 432, 256), f32)],
         place,
         second,
         weight_2,

time: 140 us -> 140 us (level)
  no operation moved by 1% of the time
where the time goes in v10:
time: 140 us; the launch traced here: 139 us
  waiting for transfers between devices  48.3 us (34%)
  blocking collectives  41.7 us (30%)
  starting transfers between devices  31.7 us (23%)
  Pallas kernels  14.4 us (10%)
  other arithmetic  1.48 us (1%)
    all_to_all x1, blocking collectives, body(): parts = lax.all_to_all(parts, ('k', 'l'), 0, 0)  26.7 us
    all_to_all x1, blocking collectives, body(): mine = lax.all_to_all(frame, ('w', 'x'), 0, 0)  15.1 us
    pallas_call x9, Pallas kernels, call(): pl.pallas_call(kernel, out_shape=out_shape, in_specs=[pl.BlockSpec(memory...  14.4 us
    ppermute x1, waiting for transfers between devices, body(): far = lax.ppermute(far, ('w', 'x', 'k', 'l', 'c'), route_far)  12.6 us
    ppermute x1, waiting for transfers between devices, body(): partner_2 = lax.ppermute(weight_2, ('h', 'w'), mirror)  11.9 us
    ppermute x1, waiting for transfers between devices, body(): partner_1 = lax.ppermute(weight_1, ('h', 'w'), mirror)  8.53 us
    ppermute x1, starting transfers between devices, body(): far = lax.ppermute(far, ('w', 'x', 'k', 'l', 'c'), route_far)  6.15 us
    all_to_all x1, starting transfers between devices, body(): second = lax.all_to_all(second, ('w', 'x'), 0, 0)  5.96 us
  transfers between devices with their start and end apart: 11, of which 8 were waited for; matrix products, arithmetic and copies ran while one was open for 1% of the time, Pallas kernels for 2%

profile of v10, /device:TPU:80, one launch (start us, length us, event | category | flops | bytes accessed | tf_op | source)
XLA Modules:
  0.0 139.1 jit_solution(17194431059095822267)
XLA Ops:
  0.0 0.9 copy-done.5
  0.9 1.2 shard_map.109
  2.1 0.0 copy-start.4
  2.1 5.2 %all-to-all-start = ((f32[8,256,128]{2,1,0:T(8,128)}), f32[8,256,128]{2,1,0:T(8,128)S(1)}, u32[]{:S(2)}, u32[]{:S(2)}) async-start(f32[8,256,128]{2,1,0:T(8,128)} %shard_map.109), calls=%async_computation | async-start | bytes 2097152 | tf_op jit(solution)/shard_map/all_to_all | solution.py:397
  7.3 0.0 copy-start.7
  7.3 0.0 copy-start.8
  7.3 0.0 copy-done.2
  7.3 3.2 %collective-permute-start = (f32[432,256]{1,0:T(8,128)S(1)}, f32[432,256]{1,0:T(8,128)S(1)}, u32[]{:S(2)}, u32[]{:S(2)}) collective-permute-start(f32[432,256]{1,0:T(8,128)S(1)} %bitcast.23), channel_id=1, source_target_pairs={{0,384},{128,256},{256,128},{384,0},{1,385},{129,257},{257,129},{3... | collective-permute-start | bytes 1327112 | tf_op jit(solution)/shard_map/ppermute | solution.py:390
  10.5 0.0 copy-done.9
  10.5 0.1 compare_bitcast_fusion.1
  10.6 0.1 broadcast_in_dim.4
  10.7 0.1 reshape_reshape.3
  10.8 0.0 copy-done
  10.8 0.0 copy-done.3
  10.8 0.7 shard_map.110._.folded_ref
  11.5 0.7 and_select_fusion
  12.2 0.1 stack.53.place_ref
  12.3 8.5 %collective-permute-done.partner_ref = f32[432,256]{1,0:T(8,128)S(1)} collective-permute-done((f32[432,256]{1,0:T(8,128)S(1)}, f32[432,256]{1,0:T(8,128)S(1)}, u32[]{:S(2)}, u32[]{:S(2)}) %collective-permute-start) | collective-permute-done | bytes 442400 | tf_op jit(solution)/shard_map/ppermute | solution.py:390
  20.8 2.1 %all-to-all-done = f32[8,256,128]{2,1,0:T(8,128)S(1)} async-done(((f32[8,256,128]{2,1,0:T(8,128)}), f32[8,256,128]{2,1,0:T(8,128)S(1)}, u32[]{:S(2)}, u32[]{:S(2)}) %all-to-all-start) | async-done | bytes 1048608 | tf_op jit(solution)/shard_map/all_to_all | solution.py:397
  23.0 2.4 %shard_map.111 = (f32[8,2,16,128]{3,2,1,0:T(8,128)S(1)}, f32[8,2,16,128]{3,2,1,0:T(8,128)S(1)}, f32[2,2,16,128]{3,2,1,0:T(8,128)S(1)}, f32[2,2,16,128]{3,2,1,0:T(8,128)S(1)}, f32[8,2,16,128]{3,2,1,0:T(8,128)S(1)}) custom-call(s32[7]{0:T(128)S(1)} %stack.53.place_ref, f32[8,4,4,16,128]{4,3,2,1,0:T(8,128)S(1)} %bitcast.20, f32[432,256]{1,0:T(8,128)S(1)} %bitcast.24, ...), custom_call_target="tpu_custom_call" | custom-call | tf_op jit(solution)/shard_map/pallas_call | solution.py:25
  25.4 0.0 collective-permute-start.1
  25.4 1.3 collective-permute-start.2
  26.7 1.3 collective-permute-start.3
  28.0 3.2 %collective-permute-done.2.last_ref = f32[2,2,16,128]{3,2,1,0:T(8,128)S(1)} collective-permute-done((f32[2,2,16,128]{3,2,1,0:T(8,128)S(1)}, f32[2,2,16,128]{3,2,1,0:T(8,128)S(1)}, u32[]{:S(2)}, u32[]{:S(2)}) %collective-permute-start.2) | collective-permute-done | bytes 32800 | tf_op jit(solution)/shard_map/ppermute | solution.py:423
  31.3 1.9 %collective-permute-done.3.last_arrived_ref = f32[2,2,16,128]{3,2,1,0:T(8,128)S(1)} collective-permute-done((f32[2,2,16,128]{3,2,1,0:T(8,128)S(1)}, f32[2,2,16,128]{3,2,1,0:T(8,128)S(1)}, u32[]{:S(2)}, u32[]{:S(2)}) %collective-permute-start.3) | collective-permute-done | bytes 32800 | tf_op jit(solution)/shard_map/ppermute | solution.py:424
  33.1 0.0 collective-permute-done.1.arrived_ref
  33.1 1.7 %shard_map.112 = f32[8,9,2,16,128]{4,3,2,1,0:T(8,128)} custom-call(s32[7]{0:T(128)S(1)} %stack.53.place_ref, f32[8,2,16,128]{3,2,1,0:T(8,128)S(1)} %get-tuple-element.19.own_ref, f32[8,2,16,128]{3,2,1,0:T(8,128)S(1)} %collective-permute-done.1.arrived_ref, f32[2,2,16,128]{3,2,1,0:T(8,128)S(1)} %collective-permute-done.2.last_ref, ...), custom_call_target="tpu_custom_call" | custom-call | tf_op jit(solution)/shard_map/pallas_call | solution.py:25
  34.8 6.0 %all-to-all-start.1 = ((f32[8,9,2,16,128]{4,3,2,1,0:T(8,128)}), f32[8,9,2,16,128]{4,3,2,1,0:T(8,128)S(1)}, u32[]{:S(2)}, u32[]{:S(2)}) async-start(f32[8,9,2,16,128]{4,3,2,1,0:T(8,128)} %shard_map.112), calls=%async_computation.1 | async-start | bytes 2359296 | tf_op jit(solution)/shard_map/all_to_all | solution.py:438
  40.8 0.0 copy-done.1
  40.8 2.6 %collective-permute-start.4 = (f32[432,256]{1,0:T(8,128)S(1)}, f32[432,256]{1,0:T(8,128)S(1)}, u32[]{:S(2)}, u32[]{:S(2)}) collective-permute-start(f32[432,256]{1,0:T(8,128)S(1)} %bitcast.21), channel_id=1, source_target_pairs={{0,384},{128,256},{256,128},{384,0},{1,385},{129,257},{257,129},{3... | collective-permute-start | bytes 1327112 | tf_op jit(solution)/shard_map/ppermute | solution.py:391
  43.4 11.9 %collective-permute-done.4.partner_ref = f32[432,256]{1,0:T(8,128)S(1)} collective-permute-done((f32[432,256]{1,0:T(8,128)S(1)}, f32[432,256]{1,0:T(8,128)S(1)}, u32[]{:S(2)}, u32[]{:S(2)}) %collective-permute-start.4) | collective-permute-done | bytes 442400 | tf_op jit(solution)/shard_map/ppermute | solution.py:391
  55.3 3.6 %all-to-all-done.1.second_ref = f32[8,9,2,16,128]{4,3,2,1,0:T(8,128)S(1)} async-done(((f32[8,9,2,16,128]{4,3,2,1,0:T(8,128)}), f32[8,9,2,16,128]{4,3,2,1,0:T(8,128)S(1)}, u32[]{:S(2)}, u32[]{:S(2)}) %all-to-all-start.1) | async-done | bytes 1179680 | tf_op jit(solution)/shard_map/all_to_all | solution.py:438
  58.9 2.7 %shard_map.113 = (f32[8,2,16,128]{3,2,1,0:T(8,128)S(1)}, f32[8,2,16,128]{3,2,1,0:T(8,128)S(1)}) custom-call(s32[7]{0:T(128)S(1)} %stack.53.place_ref, f32[8,9,2,16,128]{4,3,2,1,0:T(8,128)S(1)} %all-to-all-done.1.second_ref, f32[432,256]{1,0:T(8,128)S(1)} %bitcast.22, f32[432,256]{1,0:T(8,128)S(1)} %collective-permute-done.4.partner_ref, ...), custom_call_target="tpu_custom_call" | custom-call | tf_op jit(solution)/shard_map/pallas_call | solution.py:25
  61.7 0.0 collective-permute-start.5
  61.7 4.4 %collective-permute-done.5.arrived_ref = f32[8,2,16,128]{3,2,1,0:T(8,128)S(1)} collective-permute-done((f32[8,2,16,128]{3,2,1,0:T(8,128)S(1)}, f32[8,2,16,128]{3,2,1,0:T(8,128)S(1)}, u32[]{:S(2)}, u32[]{:S(2)}) %collective-permute-start.5) | collective-permute-done | bytes 131104 | tf_op jit(solution)/shard_map/ppermute | solution.py:452
  66.1 0.1 shard_map.114
  66.2 26.7 %all_to_all.20.parts_ref = f32[16,16,128]{2,1,0:T(8,128)S(1)} all-to-all(f32[16,16,128]{2,1,0:T(8,128)S(1)} %shard_map.114), channel_id=1, replica_groups=mesh['h'=2,'w'=2,'x'=4,'k'=8,'l'=2,'c'=2] {'k','l'}, dimensions={0} | all-to-all | bytes 262144 | tf_op jit(solution)/shard_map/all_to_all | solution.py:454
  92.8 0.1 shard_map.115
  93.0 15.1 %all_to_all.21.frame_ref = f32[8,8,2,16,128]{4,3,2,1,0:T(8,128)S(1)} all-to-all(f32[8,8,2,16,128]{4,3,2,1,0:T(8,128)S(1)} %shard_map.115), channel_id=1, replica_groups=mesh['h'=2,'w'=2,'x'=4,'k'=8,'l'=2,'c'=2] {'w','x'}, dimensions={0} | all-to-all | bytes 2097152 | tf_op jit(solution)/shard_map/all_to_all | solution.py:456
  108.0 1.9 %collective-permute-start.6 = (f32[8,8,2,16,128]{4,3,2,1,0:T(8,128)S(1)}, f32[8,8,2,16,128]{4,3,2,1,0:T(8,128)S(1)}, u32[]{:S(2)}, u32[]{:S(2)}) collective-permute-start(f32[8,8,2,16,128]{4,3,2,1,0:T(8,128)S(1)} %all_to_all.21.frame_ref), channel_id=1, source_target_pairs={{0,1},{1,0},{2,3},{3,2},{4,5},{5,4},{6,7},{7,6},{8,9},{9,8},{10,11... | collective-permute-start | bytes 3145736 | tf_op jit(solution)/shard_map/ppermute | solution.py:457
  109.9 2.8 %shard_map.116 = (f32[128,256]{1,0:T(8,128)S(1)}, f32[128,256]{1,0:T(8,128)S(1)}, f32[128,128]{1,0:T(8,128)S(1)}, f32[128,128]{1,0:T(8,128)S(1)}, f32[128,256]{1,0:T(8,128)S(1)}) custom-call(s32[7]{0:T(128)S(1)} %stack.53.place_ref, f32[8,8,2,16,128]{4,3,2,1,0:T(8,128)S(1)} %all_to_all.21.frame_ref, f32[3,256]{1,0:T(4,128)S(1)} %pad_maximum_fusion.1.gain_ref, ...), custom_call_target="tpu_custom_call" | custom-call | tf_op jit(solution)/shard_map/pallas_call | solution.py:25
  112.8 0.0 collective-permute-done.6.frame_ref
  112.8 2.7 %shard_map.117 = (f32[64,256]{1,0:T(8,128)S(1)}, f32[64,256]{1,0:T(8,128)S(1)}) custom-call(s32[7]{0:T(128)S(1)} %stack.53.place_ref, f32[8,8,2,16,128]{4,3,2,1,0:T(8,128)S(1)} %collective-permute-done.6.frame_ref, f32[3,256]{1,0:T(4,128)S(1)} %pad_maximum_fusion.1.gain_ref, f32[2,256,256]{2,1,0:T(8,128)S(1)} %shard_map.110._.folded_ref, ...), custom_call_target="tpu_custom_call" | custom-call | tf_op jit(solution)/shard_map/pallas_call | solution.py:25
  115.4 4.1 %collective-permute-start.7 = (f32[64,256]{1,0:T(8,128)S(1)}, f32[64,256]{1,0:T(8,128)S(1)}, u32[]{:S(2)}, u32[]{:S(2)}) collective-permute-start(f32[64,256]{1,0:T(8,128)S(1)} %get-tuple-element.31), channel_id=1, source_target_pairs={{0,17},{1,16},{2,55},{3,54},{4,77},{5,76},{6,123},{7,122},{8,157},... | collective-permute-start | bytes 196616 | tf_op jit(solution)/shard_map/ppermute | solution.py:481
  119.6 6.2 %collective-permute-start.8 = (f32[64,256]{1,0:T(8,128)S(1)}, f32[64,256]{1,0:T(8,128)S(1)}, u32[]{:S(2)}, u32[]{:S(2)}) collective-permute-start(f32[64,256]{1,0:T(8,128)S(1)} %get-tuple-element.32), channel_id=1, source_target_pairs={{0,15},{1,14},{2,53},{3,52},{4,75},{5,74},{6,121},{7,120},{8,155},... | collective-permute-start | bytes 196616 | tf_op jit(solution)/shard_map/ppermute | solution.py:482
  125.7 0.0 collective-permute-done.7
  125.7 12.6 %collective-permute-done.8 = f32[64,256]{1,0:T(8,128)S(1)} collective-permute-done((f32[64,256]{1,0:T(8,128)S(1)}, f32[64,256]{1,0:T(8,128)S(1)}, u32[]{:S(2)}, u32[]{:S(2)}) %collective-permute-start.8) | collective-permute-done | bytes 65568 | tf_op jit(solution)/shard_map/ppermute | solution.py:482
  138.4 0.7 pad_maximum_fusion
  (15 shorter events, 0.1 us)
Async XLA Ops:
  0.0 0.9 copy-start.5
  2.1 5.2 %copy-start.2 = (f32[3,3,3,16,256]{4,3,2,1,0:T(8,128)S(1)}, f32[3,3,3,16,256]{4,3,2,1,0:T(8,128)}, u32[]{:S(2)}) copy-start(f32[3,3,3,16,256]{4,3,2,1,0:T(8,128)} %param.14) | copy-start | bytes 1327108
  2.1 8.4 %copy-start.9 = (s32[32]{0:T(128)S(1)}, s32[32]{0:T(128)}, u32[]{:S(2)}) copy-start(s32[32]{0:T(128)} %param.12) | copy-start | bytes 388
  2.1 8.7 %copy-start = (f32[2,256,256]{2,1,0:T(8,128)S(1)}, f32[2,256,256]{2,1,0:T(8,128)}, u32[]{:S(2)}) copy-start(f32[2,256,256]{2,1,0:T(8,128)} %qk_ref.1) | copy-start | bytes 1572868
  2.1 8.7 %copy-start.3 = (f32[256,256]{1,0:T(8,128)S(1)}, f32[256,256]{1,0:T(8,128)}, u32[]{:S(2)}) copy-start(f32[256,256]{1,0:T(8,128)} %value_ref.1) | copy-start | bytes 786436
  2.1 8.7 %copy-start.4 = (f32[256,256]{1,0:T(8,128)S(1)}, f32[256,256]{1,0:T(8,128)}, u32[]{:S(2)}) copy-start(f32[256,256]{1,0:T(8,128)} %proj_ref.1) | copy-start | bytes 786436
  2.1 20.9 %all-to-all-start = ((f32[8,256,128]{2,1,0:T(8,128)}), f32[8,256,128]{2,1,0:T(8,128)S(1)}, u32[]{:S(2)}, u32[]{:S(2)}) async-start(f32[8,256,128]{2,1,0:T(8,128)} %shard_map.109), calls=%async_computation | async-start | bytes 2097152 | tf_op jit(solution)/shard_map/all_to_all | solution.py:397
  7.3 5.0 %copy-start.6 = (f32[256]{0:T(256)S(1)}, f32[256]{0:T(256)}, u32[]{:S(2)}) copy-start(f32[256]{0:T(256)} %param.17) | copy-start | bytes 3076
  7.3 5.0 %copy-start.7 = (f32[256]{0:T(256)S(1)}, f32[256]{0:T(256)}, u32[]{:S(2)}) copy-start(f32[256]{0:T(256)} %param.15) | copy-start | bytes 3076
  7.3 5.0 %copy-start.8 = (f32[256]{0:T(256)S(1)}, f32[256]{0:T(256)}, u32[]{:S(2)}) copy-start(f32[256]{0:T(256)} %param.13) | copy-start | bytes 3076
  7.3 13.5 %collective-permute-start = (f32[432,256]{1,0:T(8,128)S(1)}, f32[432,256]{1,0:T(8,128)S(1)}, u32[]{:S(2)}, u32[]{:S(2)}) collective-permute-start(f32[432,256]{1,0:T(8,128)S(1)} %bitcast.23), channel_id=1, source_target_pairs={{0,384},{128,256},{256,128},{384,0},{1,385},{129,257},{257,129},{3... | collective-permute-start | bytes 1327112 | tf_op jit(solution)/shard_map/ppermute | solution.py:390
  25.4 7.7 %collective-permute-start.1 = (f32[8,2,16,128]{3,2,1,0:T(8,128)S(1)}, f32[8,2,16,128]{3,2,1,0:T(8,128)S(1)}, u32[]{:S(2)}, u32[]{:S(2)}) collective-permute-start(f32[8,2,16,128]{3,2,1,0:T(8,128)S(1)} %get-tuple-element.20), channel_id=1, source_target_pairs={{0,1},{1,2},{2,3},{3,4},{4,5},{5,6},{6,7},{7,8},{8,9},{9,10},{10,1... | collective-permute-start | bytes 393224 | tf_op jit(solution)/shard_map/ppermute | solution.py:426
  25.4 5.8 %collective-permute-start.2 = (f32[2,2,16,128]{3,2,1,0:T(8,128)S(1)}, f32[2,2,16,128]{3,2,1,0:T(8,128)S(1)}, u32[]{:S(2)}, u32[]{:S(2)}) collective-permute-start(f32[2,2,16,128]{3,2,1,0:T(8,128)S(1)} %get-tuple-element.21), channel_id=1, source_target_pairs={{0,384},{128,256},{1,385},{129,257},{2,386},{130,258},{3,387},{131... | collective-permute-start | bytes 98312 | tf_op jit(solution)/shard_map/ppermute | solution.py:423
  26.7 6.4 %collective-permute-start.3 = (f32[2,2,16,128]{3,2,1,0:T(8,128)S(1)}, f32[2,2,16,128]{3,2,1,0:T(8,128)S(1)}, u32[]{:S(2)}, u32[]{:S(2)}) collective-permute-start(f32[2,2,16,128]{3,2,1,0:T(8,128)S(1)} %get-tuple-element.22), channel_id=1, source_target_pairs={{0,385},{1,386},{2,387},{3,388},{4,389},{5,390},{6,391},{7,392},{8... | collective-permute-start | bytes 98312 | tf_op jit(solution)/shard_map/ppermute | solution.py:424
  34.8 6.0 %copy-start.1 = (f32[3,3,3,16,256]{4,3,2,1,0:T(8,128)S(1)}, f32[3,3,3,16,256]{4,3,2,1,0:T(8,128)}, u32[]{:S(2)}) copy-start(f32[3,3,3,16,256]{4,3,2,1,0:T(8,128)} %param.16) | copy-start | bytes 1327108
  34.8 24.1 %all-to-all-start.1 = ((f32[8,9,2,16,128]{4,3,2,1,0:T(8,128)}), f32[8,9,2,16,128]{4,3,2,1,0:T(8,128)S(1)}, u32[]{:S(2)}, u32[]{:S(2)}) async-start(f32[8,9,2,16,128]{4,3,2,1,0:T(8,128)} %shard_map.112), calls=%async_computation.1 | async-start | bytes 2359296 | tf_op jit(solution)/shard_map/all_to_all | solution.py:438
  40.8 14.5 %collective-permute-start.4 = (f32[432,256]{1,0:T(8,128)S(1)}, f32[432,256]{1,0:T(8,128)S(1)}, u32[]{:S(2)}, u32[]{:S(2)}) collective-permute-start(f32[432,256]{1,0:T(8,128)S(1)} %bitcast.21), channel_id=1, source_target_pairs={{0,384},{128,256},{256,128},{384,0},{1,385},{129,257},{257,129},{3... | collective-permute-start | bytes 1327112 | tf_op jit(solution)/shard_map/ppermute | solution.py:391
  61.7 4.4 %collective-permute-start.5 = (f32[8,2,16,128]{3,2,1,0:T(8,128)S(1)}, f32[8,2,16,128]{3,2,1,0:T(8,128)S(1)}, u32[]{:S(2)}, u32[]{:S(2)}) collective-permute-start(f32[8,2,16,128]{3,2,1,0:T(8,128)S(1)} %get-tuple-element.25), channel_id=1, source_target_pairs={{0,1},{1,2},{2,3},{3,4},{4,5},{5,6},{6,7},{7,8},{8,9},{9,10},{10,1... | collective-permute-start | bytes 393224 | tf_op jit(solution)/shard_map/ppermute | solution.py:452
  108.0 4.7 %collective-permute-start.6 = (f32[8,8,2,16,128]{4,3,2,1,0:T(8,128)S(1)}, f32[8,8,2,16,128]{4,3,2,1,0:T(8,128)S(1)}, u32[]{:S(2)}, u32[]{:S(2)}) collective-permute-start(f32[8,8,2,16,128]{4,3,2,1,0:T(8,128)S(1)} %all_to_all.21.frame_ref), channel_id=1, source_target_pairs={{0,1},{1,0},{2,3},{3,2},{4,5},{5,4},{6,7},{7,6},{8,9},{9,8},{10,11... | collective-permute-start | bytes 3145736 | tf_op jit(solution)/shard_map/ppermute | solution.py:457
  115.4 10.3 %collective-permute-start.7 = (f32[64,256]{1,0:T(8,128)S(1)}, f32[64,256]{1,0:T(8,128)S(1)}, u32[]{:S(2)}, u32[]{:S(2)}) collective-permute-start(f32[64,256]{1,0:T(8,128)S(1)} %get-tuple-element.31), channel_id=1, source_target_pairs={{0,17},{1,16},{2,55},{3,54},{4,77},{5,76},{6,123},{7,122},{8,157},... | collective-permute-start | bytes 196616 | tf_op jit(solution)/shard_map/ppermute | solution.py:481
  119.6 18.8 %collective-permute-start.8 = (f32[64,256]{1,0:T(8,128)S(1)}, f32[64,256]{1,0:T(8,128)S(1)}, u32[]{:S(2)}, u32[]{:S(2)}) collective-permute-start(f32[64,256]{1,0:T(8,128)S(1)} %get-tuple-element.32), channel_id=1, source_target_pairs={{0,15},{1,14},{2,53},{3,52},{4,75},{5,74},{6,121},{7,120},{8,155},... | collective-permute-start | bytes 196616 | tf_op jit(solution)/shard_map/ppermute | solution.py:482
